TPU v7x, 32 devices: a whole 2x2x4 slice. The times are simulated.
32 devices in a mesh: stn: 8 (over y, x, core), chan: 4 (over z).
Axes of the slice: x: 2, y: 2, z: 4, core: 2. Of those that a mesh axis runs over, the one named last changes fastest.
Arguments:
- volts: bfloat16 [4, 2, 512, 18048], P('chan', None, 'stn'), may hold values from -6 to 6
- taps: float32 [16, 384], replicated, may hold values from -1.5 to 1.5
- survive: int32 [4, 8], replicated, may hold values from 0 to 383, as said below
- owner: int32 [4, 8], replicated, may hold values from 0 to 3, as said below
Outputs:
- visibilities: bfloat16 [4, 24, 2, 512, 512], P('chan', None, None, 'stn')
Inputs may be any that keep to these rules, and one draw needn't show every extreme that they name: `survive`: each band lists 8 distinct fine channels. Within one band at most 6 channels share an owner, and in some band exactly 6 do; each owner holds at most 24 channels in all, and one owner holds exactly 24.
All inputs are finite; a program needn't handle non-finite values.
Results may differ from a plain program's by a relative error of at most 0.0076.
Values may be sent and summed in bfloat16 or wider, within the bound.
No kernel may reach another device: no remote copies, remote signals or barrier semaphores. Data moves between devices by JAX's collectives and lax.ppermute only.
A program may use at most 128 MiB of HBM per device.

v0:
```python
import math

import jax
import jax.numpy as jnp
from jax import lax
from jax.sharding import PartitionSpec as P

RCAP = 24


def shifted(x, axis, by):
    peers = lax.axis_size(axis)
    return lax.ppermute(x, axis, [(i, (i + by) % peers) for i in range(peers)])


def fine_tables(chosen, fine_len):
    branch_ids = jnp.arange(fine_len, dtype=jnp.int32)
    phase_index = chosen[:, None] * branch_ids[None, :] % fine_len
    angles = phase_index.astype(jnp.float32) * (2.0 * math.pi / fine_len)
    factor = 1.0 / math.sqrt(fine_len)
    cosine = (jnp.cos(angles) * factor).astype(jnp.bfloat16)
    sine_table = (jnp.sin(angles) * factor).astype(jnp.bfloat16)
    return (cosine, sine_table)


def polyphase(signal, taps, spectra_count):
    accum = jnp.zeros((2, signal.shape[1], spectra_count, signal.shape[3]), jnp.float32)
    for tap_index in range(taps.shape[0]):
        accum = accum + taps[tap_index] * signal[
            :, :, tap_index : tap_index + spectra_count, :
        ].astype(jnp.float32)
    return accum.astype(jnp.bfloat16)


def split_parts(products, inputs, spectra_count):
    real_part = products[..., :inputs, :inputs] + products[..., inputs:, inputs:]
    imag_part = products[..., inputs:, :inputs] - products[..., :inputs, inputs:]
    return (jnp.stack([real_part, imag_part], axis=-3) / spectra_count).astype(jnp.bfloat16)


def per_device(volts, taps, survive, owner):
    band_index = lax.axis_index("chan")
    chan_count = lax.axis_size("chan")
    stn_count = lax.axis_size("stn")
    stn_index = lax.axis_index("stn")
    inputs = volts.shape[2]
    samples = volts.shape[3]
    taps_count, fine_len = taps.shape
    keep_count = survive.shape[1]
    spectra_count = samples // fine_len - taps_count + 1
    slot_cap = max(2, (RCAP + chan_count - 1) // chan_count)
    chosen = lax.dynamic_index_in_dim(survive, band_index, 0, keepdims=False)
    signal = volts[0].reshape(2, inputs, samples // fine_len, fine_len)
    filtered = polyphase(signal, taps, spectra_count)
    signal_rows = filtered.transpose(1, 2, 0, 3).reshape(inputs * spectra_count, 2 * fine_len)
    cosine, sine_table = fine_tables(chosen, fine_len)
    dft_table = jnp.concatenate(
        [
            jnp.concatenate([cosine.T, -sine_table.T], 1),
            jnp.concatenate([sine_table.T, cosine.T], 1),
        ],
        0,
    )
    spectra = jnp.dot(signal_rows, dft_table, preferred_element_type=jnp.float32).astype(
        jnp.bfloat16
    )
    spectra = spectra.reshape(inputs, spectra_count, 2, keep_count).transpose(3, 1, 2, 0)
    spectra = spectra.reshape(keep_count, spectra_count * 2 * inputs)
    owner_ids = jnp.arange(chan_count, dtype=jnp.int32)
    owner_hits = (owner[:, :, None] == owner_ids).astype(jnp.int32)
    pair_rank = jnp.sum((jnp.cumsum(owner_hits, 1) - owner_hits) * owner_hits, 2)
    flat_hits = owner_hits.reshape(-1, chan_count)
    owner_slot = jnp.sum((jnp.cumsum(flat_hits, 0) - flat_hits) * flat_hits, 1)
    my_target = lax.dynamic_index_in_dim(
        owner * slot_cap + pair_rank, band_index, 0, keepdims=False
    )
    send_slots = jnp.arange(chan_count * slot_cap, dtype=jnp.int32)
    send_pick = (send_slots[:, None] == my_target[None, :]).astype(jnp.bfloat16)
    outgoing = jnp.dot(send_pick, spectra, preferred_element_type=jnp.float32).astype(jnp.bfloat16)
    outgoing = outgoing.reshape(chan_count, slot_cap, spectra_count, 2 * inputs)
    arrived = lax.all_to_all(outgoing, "chan", split_axis=0, concat_axis=0, tiled=True)
    source_ids = jnp.arange(owner.shape[0], dtype=jnp.int32)
    slot_column = (source_ids[:, None] * slot_cap + pair_rank).reshape(-1)
    is_mine = (owner == band_index).reshape(-1)
    slot_rows = (
        (jnp.arange(RCAP, dtype=jnp.int32)[:, None] == owner_slot[None, :]) & is_mine[None, :]
    ).astype(jnp.bfloat16)
    slot_cols = (slot_column[:, None] == send_slots[None, :]).astype(jnp.bfloat16)
    compact_map = jnp.dot(slot_rows, slot_cols, preferred_element_type=jnp.float32).astype(
        jnp.bfloat16
    )
    local_block = jnp.dot(
        compact_map, arrived.reshape(chan_count * slot_cap, -1), preferred_element_type=jnp.float32
    ).astype(jnp.bfloat16)
    local_block = local_block.reshape(RCAP, spectra_count, 2 * inputs)

    def place(totals, remote_block, anchor):
        products = jnp.einsum(
            "stp,stq->spq", local_block, remote_block, preferred_element_type=jnp.float32
        )
        return lax.dynamic_update_slice_in_dim(
            totals, split_parts(products, inputs, spectra_count)[None], anchor, 0
        )

    empty_out = jnp.zeros((stn_count, RCAP, 2, inputs, inputs), jnp.bfloat16)
    totals = place(empty_out, local_block, stn_index)

    def one_step(turn_index, carry):
        remote_block, partial_out = carry
        remote_block = shifted(remote_block, "stn", 1)
        partial_out = place(partial_out, remote_block, (stn_index - turn_index) % stn_count)
        return (remote_block, partial_out)

    remote_block, totals = lax.fori_loop(1, stn_count, one_step, (local_block, totals))
    visibilities = totals.transpose(1, 2, 3, 0, 4).reshape(RCAP, 2, inputs, stn_count * inputs)
    return visibilities[None]


def solution(mesh):
    return jax.shard_map(
        per_device,
        mesh=mesh,
        in_specs=(P("chan", None, "stn", None), P(), P(), P()),
        out_specs=P("chan", None, None, "stn", None),
        check_vma=False,
    )
```

profile of v0, /device:TPU:0, one launch (start us, length us, event | category | flops | bytes accessed | tf_op | source)
XLA Modules:
  0.0 155.2 jit_solution(2757584176102330934)
XLA Ops:
  0.0 0.7 fusion.31
  0.7 0.7 reduce_window_sum.23
  1.4 0.7 select_reduce_fusion.1
  2.1 0.8 broadcast_add_fusion
  2.9 0.7 fusion.38
  3.5 0.1 fusion.37
  3.7 0.1 multiply_convert_fusion
  3.8 1.1 slice_reduce_fusion.15
  5.0 7.9 %reshape_squeeze.3 = bf16[2,64,47,384]{3,2,1,0:T(8,128)(2,1)} reshape(bf16[1,2,64,18048]{3,2,1,0:T(8,128)(2,1)} %param.6) | data formatting | bytes 9240576 | tf_op jit(solution)/shard_map/reshape;squeeze | solution.py:53
  12.8 32.3 %fusion.4 = bf16[64,32,2,384]{3,1,0,2:T(8,128)(2,1)S(1)} fusion(bf16[2,64,47,384]{3,2,1,0:T(8,128)(2,1)} %reshape_squeeze.3, f32[384]{0:T(512)S(1)} %get-tuple-element.153, f32[384]{0:T(512)S(1)} %get-tuple-element.154, f32[384]{0:T(512)S(1)} %get-tuple-element.140, f32[384]{0:T(512)S(1)} %get-tuple-element.141, f32[384]{0:T(512)S(1)} %get-tuple-element.142, ...), kind=kLoop, calls=%fused_computation.10 | loop fusion | flops 75497472 | bytes 53501952 | tf_op jit(solution)/shard_map/transpose | solution.py:55
  45.1 3.2 %copy.12 = bf16[64,32,2,384]{3,2,1,0:T(2,128)(2,1)S(1)} copy(bf16[64,32,2,384]{3,1,0,2:T(8,128)(2,1)S(1)} %fusion.4) | data formatting | bytes 6291456 | tf_op jit(solution)/shard_map/transpose | solution.py:55
  48.4 0.7 copy.15
  49.0 0.9 convolution_convert_fusion.2
  50.0 0.2 reshape.138
  50.2 0.1 copy.13
  50.3 0.2 reshape.139
  50.5 0.2 fusion.6
  50.7 0.7 copy.16
  51.4 6.3 %all-to-all-start = ((bf16[4,6,32,128]{3,2,1,0:T(8,128)(2,1)}), bf16[4,6,32,128]{3,2,1,0:T(8,128)(2,1)S(1)}, u32[]{:S(2)}, u32[]{:S(2)}) async-start(bf16[4,6,32,128]{3,2,1,0:T(8,128)(2,1)} %bitcast.16), calls=%async_computation | async-start | bytes 393216 | tf_op jit(solution)/shard_map/all_to_all | solution.py:81
  57.7 0.1 eq.80
  57.8 0.1 and.30
  57.9 0.1 add.135
  58.0 0.1 fusion.20
  58.1 0.2 select_reduce_fusion
  58.3 6.9 %all-to-all-done = bf16[4,6,32,128]{3,2,1,0:T(8,128)(2,1)S(1)} async-done(((bf16[4,6,32,128]{3,2,1,0:T(8,128)(2,1)}), bf16[4,6,32,128]{3,2,1,0:T(8,128)(2,1)S(1)}, u32[]{:S(2)}, u32[]{:S(2)}) %all-to-all-start) | async-done | bytes 196640 | tf_op jit(solution)/shard_map/all_to_all | solution.py:81
  65.2 0.4 fusion.7
  65.7 0.4 fusion.42
  66.1 0.5 fusion.10
  66.6 1.6 %broadcast_in_dim.4 = bf16[8,24,2,64,64]{4,3,1,2,0:T(8,128)(2,1)S(1)} broadcast(bf16[]{:T(256)} %constant.104.clone.1), dimensions={} | broadcast | bytes 3145730 | tf_op jit(solution)/shard_map/broadcast_in_dim | solution.py:105
  68.2 0.3 fusion.8
  68.5 2.7 %copy-done = bf16[8,24,2,64,64]{4,3,1,2,0:T(8,128)(2,1)} copy-done((bf16[8,24,2,64,64]{4,3,1,2,0:T(8,128)(2,1)}, bf16[8,24,2,64,64]{4,3,1,2,0:T(8,128)(2,1)S(1)}, u32[]{:S(2)}) %copy-start) | copy-done | bytes 3145752
  71.2 56.8 %while.17 = (s32[]{:T(128)}, bf16[24,32,128]{2,1,0:T(8,128)(2,1)S(1)}, bf16[8,24,2,64,64]{4,3,1,2,0:T(8,128)(2,1)}, bf16[24,32,128]{2,1,0:T(8,128)(2,1)S(1)}, s3...) while((s32[]{:T(128)}, bf16[24,32,128]{2,1,0:T(8,128)(2,1)S(1)}, ...), condition=%wide.region_5.6_spmd, body=%wide.region_4.5_spmd.sunk | while | flops 25952272 | bytes 7078180 | solution.py:114
  71.2 6.0 %collective-permute-done = bf16[24,32,128]{2,1,0:T(8,128)(2,1)S(1)} collective-permute-done((bf16[24,32,128]{2,1,0:T(8,128)(2,1)S(1)}, bf16[24,32,128]{2,1,0:T(8,128)(2,1)S(1)}, u32[]{:S(2)}, u32[]{:S(2)}) %collective-permute-start) | collective-permute-done | bytes 196640 | tf_op jit(solution)/shard_map/while/body/eval_jaxpr/ppermute | solution.py:13
  77.2 0.4 fusion.56
  77.6 0.5 fusion.57
  78.1 1.2 fusion.58
  79.3 0.1 collective-permute-start
  79.4 6.0 %collective-permute-done = bf16[24,32,128]{2,1,0:T(8,128)(2,1)S(1)} collective-permute-done((bf16[24,32,128]{2,1,0:T(8,128)(2,1)S(1)}, bf16[24,32,128]{2,1,0:T(8,128)(2,1)S(1)}, u32[]{:S(2)}, u32[]{:S(2)}) %collective-permute-start) | collective-permute-done | bytes 196640 | tf_op jit(solution)/shard_map/while/body/eval_jaxpr/ppermute | solution.py:13
  85.3 0.4 fusion.56
  85.7 0.5 fusion.57
  86.2 1.1 fusion.58
  87.5 6.0 %collective-permute-done = bf16[24,32,128]{2,1,0:T(8,128)(2,1)S(1)} collective-permute-done((bf16[24,32,128]{2,1,0:T(8,128)(2,1)S(1)}, bf16[24,32,128]{2,1,0:T(8,128)(2,1)S(1)}, u32[]{:S(2)}, u32[]{:S(2)}) %collective-permute-start) | collective-permute-done | bytes 196640 | tf_op jit(solution)/shard_map/while/body/eval_jaxpr/ppermute | solution.py:13
  93.4 0.4 fusion.56
  93.8 0.5 fusion.57
  94.3 1.1 fusion.58
  95.5 0.1 collective-permute-start
  95.6 6.0 %collective-permute-done = bf16[24,32,128]{2,1,0:T(8,128)(2,1)S(1)} collective-permute-done((bf16[24,32,128]{2,1,0:T(8,128)(2,1)S(1)}, bf16[24,32,128]{2,1,0:T(8,128)(2,1)S(1)}, u32[]{:S(2)}, u32[]{:S(2)}) %collective-permute-start) | collective-permute-done | bytes 196640 | tf_op jit(solution)/shard_map/while/body/eval_jaxpr/ppermute | solution.py:13
  101.5 0.4 fusion.56
  101.9 0.5 fusion.57
  102.4 1.1 fusion.58
  103.7 6.0 %collective-permute-done = bf16[24,32,128]{2,1,0:T(8,128)(2,1)S(1)} collective-permute-done((bf16[24,32,128]{2,1,0:T(8,128)(2,1)S(1)}, bf16[24,32,128]{2,1,0:T(8,128)(2,1)S(1)}, u32[]{:S(2)}, u32[]{:S(2)}) %collective-permute-start) | collective-permute-done | bytes 196640 | tf_op jit(solution)/shard_map/while/body/eval_jaxpr/ppermute | solution.py:13
  109.6 0.4 fusion.56
  110.0 0.5 fusion.57
  110.5 1.1 fusion.58
  111.8 6.0 %collective-permute-done = bf16[24,32,128]{2,1,0:T(8,128)(2,1)S(1)} collective-permute-done((bf16[24,32,128]{2,1,0:T(8,128)(2,1)S(1)}, bf16[24,32,128]{2,1,0:T(8,128)(2,1)S(1)}, u32[]{:S(2)}, u32[]{:S(2)}) %collective-permute-start) | collective-permute-done | bytes 196640 | tf_op jit(solution)/shard_map/while/body/eval_jaxpr/ppermute | solution.py:13
  117.7 0.4 fusion.56
  118.2 0.5 fusion.57
  118.6 1.1 fusion.58
  119.9 6.0 %collective-permute-done = bf16[24,32,128]{2,1,0:T(8,128)(2,1)S(1)} collective-permute-done((bf16[24,32,128]{2,1,0:T(8,128)(2,1)S(1)}, bf16[24,32,128]{2,1,0:T(8,128)(2,1)S(1)}, u32[]{:S(2)}, u32[]{:S(2)}) %collective-permute-start) | collective-permute-done | bytes 196640 | tf_op jit(solution)/shard_map/while/body/eval_jaxpr/ppermute | solution.py:13
  125.9 0.4 fusion.56
  126.3 0.5 fusion.57
  126.8 1.2 fusion.58
  127.9 17.9 %copy.14 = bf16[24,2,64,8,64]{4,3,2,1,0:T(8,128)(2,1)} copy(bf16[24,2,64,8,64]{4,2,0,1,3:T(8,128)(2,1)} %bitcast.49) | data formatting | bytes 6291456 | tf_op jit(solution)/shard_map/transpose | solution.py:115
  145.8 9.3 %broadcast_in_dim_reshape.2 = bf16[1,24,2,64,512]{4,3,2,1,0:T(8,128)(2,1)} reshape(bf16[24,2,64,8,64]{4,3,2,1,0:T(8,128)(2,1)} %copy.14) | data formatting | bytes 6291456 | tf_op jit(solution)/shard_map/broadcast_in_dim;reshape | solution.py:116
  (20 shorter events, 0.4 us)
Async XLA Ops:
  48.4 9.4 %copy-start.1 = (s32[4,8]{1,0:T(4,128)S(1)}, s32[4,8]{1,0:T(4,128)}, u32[]{:S(2)}) copy-start(s32[4,8]{1,0:T(4,128)} %param.9) | copy-start | bytes 388
  51.4 13.8 %all-to-all-start = ((bf16[4,6,32,128]{3,2,1,0:T(8,128)(2,1)}), bf16[4,6,32,128]{3,2,1,0:T(8,128)(2,1)S(1)}, u32[]{:S(2)}, u32[]{:S(2)}) async-start(bf16[4,6,32,128]{3,2,1,0:T(8,128)(2,1)} %bitcast.16), calls=%async_computation | async-start | bytes 393216 | tf_op jit(solution)/shard_map/all_to_all | solution.py:81
  68.5 2.7 %copy-start = (bf16[8,24,2,64,64]{4,3,1,2,0:T(8,128)(2,1)}, bf16[8,24,2,64,64]{4,3,1,2,0:T(8,128)(2,1)S(1)}, u32[]{:S(2)}) copy-start(bf16[8,24,2,64,64]{4,3,1,2,0:T(8,128)(2,1)S(1)} %fusion.8) | copy-start | bytes 9437188
  71.2 6.0 %collective-permute-start = (bf16[24,32,128]{2,1,0:T(8,128)(2,1)S(1)}, bf16[24,32,128]{2,1,0:T(8,128)(2,1)S(1)}, u32[]{:S(2)}, u32[]{:S(2)}) collective-permute-start(bf16[24,32,128]{2,1,0:T(8,128)(2,1)S(1)} %get-tuple-element.220), channel_id=1, source_target_pairs={{0,4},{4,8},{8,12},{12,16},{16,20},{20,24},{24,28},{28,0},{1,5},{5... | collective-permute-start | bytes 589832 | tf_op jit(solution)/shard_map/while/body/eval_jaxpr/ppermute | solution.py:13
  79.3 6.0 %collective-permute-start = (bf16[24,32,128]{2,1,0:T(8,128)(2,1)S(1)}, bf16[24,32,128]{2,1,0:T(8,128)(2,1)S(1)}, u32[]{:S(2)}, u32[]{:S(2)}) collective-permute-start(bf16[24,32,128]{2,1,0:T(8,128)(2,1)S(1)} %get-tuple-element.220), channel_id=1, source_target_pairs={{0,4},{4,8},{8,12},{12,16},{16,20},{20,24},{24,28},{28,0},{1,5},{5... | collective-permute-start | bytes 589832 | tf_op jit(solution)/shard_map/while/body/eval_jaxpr/ppermute | solution.py:13
  87.4 6.0 %collective-permute-start = (bf16[24,32,128]{2,1,0:T(8,128)(2,1)S(1)}, bf16[24,32,128]{2,1,0:T(8,128)(2,1)S(1)}, u32[]{:S(2)}, u32[]{:S(2)}) collective-permute-start(bf16[24,32,128]{2,1,0:T(8,128)(2,1)S(1)} %get-tuple-element.220), channel_id=1, source_target_pairs={{0,4},{4,8},{8,12},{12,16},{16,20},{20,24},{24,28},{28,0},{1,5},{5... | collective-permute-start | bytes 589832 | tf_op jit(solution)/shard_map/while/body/eval_jaxpr/ppermute | solution.py:13
  95.5 6.0 %collective-permute-start = (bf16[24,32,128]{2,1,0:T(8,128)(2,1)S(1)}, bf16[24,32,128]{2,1,0:T(8,128)(2,1)S(1)}, u32[]{:S(2)}, u32[]{:S(2)}) collective-permute-start(bf16[24,32,128]{2,1,0:T(8,128)(2,1)S(1)} %get-tuple-element.220), channel_id=1, source_target_pairs={{0,4},{4,8},{8,12},{12,16},{16,20},{20,24},{24,28},{28,0},{1,5},{5... | collective-permute-start | bytes 589832 | tf_op jit(solution)/shard_map/while/body/eval_jaxpr/ppermute | solution.py:13
  103.6 6.0 %collective-permute-start = (bf16[24,32,128]{2,1,0:T(8,128)(2,1)S(1)}, bf16[24,32,128]{2,1,0:T(8,128)(2,1)S(1)}, u32[]{:S(2)}, u32[]{:S(2)}) collective-permute-start(bf16[24,32,128]{2,1,0:T(8,128)(2,1)S(1)} %get-tuple-element.220), channel_id=1, source_target_pairs={{0,4},{4,8},{8,12},{12,16},{16,20},{20,24},{24,28},{28,0},{1,5},{5... | collective-permute-start | bytes 589832 | tf_op jit(solution)/shard_map/while/body/eval_jaxpr/ppermute | solution.py:13
  111.7 6.0 %collective-permute-start = (bf16[24,32,128]{2,1,0:T(8,128)(2,1)S(1)}, bf16[24,32,128]{2,1,0:T(8,128)(2,1)S(1)}, u32[]{:S(2)}, u32[]{:S(2)}) collective-permute-start(bf16[24,32,128]{2,1,0:T(8,128)(2,1)S(1)} %get-tuple-element.220), channel_id=1, source_target_pairs={{0,4},{4,8},{8,12},{12,16},{16,20},{20,24},{24,28},{28,0},{1,5},{5... | collective-permute-start | bytes 589832 | tf_op jit(solution)/shard_map/while/body/eval_jaxpr/ppermute | solution.py:13
  119.8 6.0 %collective-permute-start = (bf16[24,32,128]{2,1,0:T(8,128)(2,1)S(1)}, bf16[24,32,128]{2,1,0:T(8,128)(2,1)S(1)}, u32[]{:S(2)}, u32[]{:S(2)}) collective-permute-start(bf16[24,32,128]{2,1,0:T(8,128)(2,1)S(1)} %get-tuple-element.220), channel_id=1, source_target_pairs={{0,4},{4,8},{8,12},{12,16},{16,20},{20,24},{24,28},{28,0},{1,5},{5... | collective-permute-start | bytes 589832 | tf_op jit(solution)/shard_map/while/body/eval_jaxpr/ppermute | solution.py:13
where the time goes:
time: 156 us; the launch traced here: 155 us
  waiting for transfers between devices  48.7 us (31%)
  other arithmetic  47.9 us (31%)
  local copies, waits for them, and re-layouts  46.7 us (30%)
  starting transfers between devices  6.67 us (4%)
  matrix products  4.8 us (3%)
    ppermute x7, waiting for transfers between devices, shifted(): return lax.ppermute(x, axis, [(i, (i + by) % peers) for i in range(peers)])  41.7 us
    transpose x1, other arithmetic, per_device(): filtered.transpose(1, 2, 0, 3).reshape(inputs * spectra_count, 2 * fine_len)  32.3 us
    transpose x1, local copies, waits for them, and re-layouts, per_device(): totals.transpose(1, 2, 3, 0, 4).reshape(RCAP, 2, inputs, stn_count * inputs)  17.9 us
    another operation x1, local copies, waits for them, and re-layouts, per_device(): return visibilities[None]  9.32 us
    dynamic_update_slice x8, other arithmetic, place(): lax.dynamic_update_slice_in_dim(totals, split_parts(products, inputs, spe...  8.33 us
    another operation x1, local copies, waits for them, and re-layouts, per_device(): signal = volts[0].reshape(2, inputs, samples // fine_len, fine_len)  7.86 us
    all_to_all x1, waiting for transfers between devices, per_device(): lax.all_to_all(outgoing, 'chan', split_axis=0, concat_axis=0, tiled=True)  6.94 us
    all_to_all x1, starting transfers between devices, per_device(): lax.all_to_all(outgoing, 'chan', split_axis=0, concat_axis=0, tiled=True)  6.32 us
  transfers between devices with their start and end apart: 8, of which 8 were waited for; matrix products, arithmetic and copies ran while one was open for 0% of the time, Pallas kernels for 0%

commit v1 on v0

v1 whole, which is shorter than its diff:
```python
import functools
import math

import jax
import jax.numpy as jnp
from jax import lax
from jax.experimental import pallas as pl
from jax.experimental.pallas import tpu as pltpu
from jax.sharding import PartitionSpec as P

RCAP = 24
LANES = 128
GROUP = 4
VMEM_LIMIT = 48 << 20


def swapped(x, axis, mask):
    peers = lax.axis_size(axis)
    return lax.ppermute(x, axis, [(i, i ^ mask) for i in range(peers)])


def front_kernel(chan_count, slot_cap, survive_ref, owner_ref, taps_ref, volts_ref, *rest):
    outs = rest[:chan_count]
    volts, table, even, odd, spectra, stage, in_sems, out_sems = rest[chan_count:]
    taps_count, fine_len = taps_ref.shape
    inputs, samples = volts_ref.shape[2:]
    keep = survive_ref.shape[1]
    blocks = samples // fine_len
    times = blocks - taps_count + 1
    pack = max(1, LANES // inputs)
    rows = times // pack
    band = lax.axis_index("chan")

    groups = []
    for first in range(0, blocks, GROUP):
        count = min(GROUP, blocks - first)
        lanes = pl.ds(first * fine_len, count * fine_len)
        copy = pltpu.make_async_copy(
            volts_ref.at[0, :, :, lanes], volts.at[:, :, lanes], in_sems.at[first // GROUP]
        )
        copy.start()
        groups.append((first, count, copy))

    row_ids = lax.broadcasted_iota(jnp.int32, (keep, fine_len), 0)
    branch_ids = lax.broadcasted_iota(jnp.int32, (keep, fine_len), 1)
    chosen = jnp.zeros((keep, fine_len), jnp.int32)
    for c in range(keep):
        chosen = jnp.where(row_ids == c, survive_ref[band, c], chosen)
    angles = (chosen * branch_ids % fine_len).astype(jnp.float32) * (2.0 * math.pi / fine_len)
    factor = 1.0 / math.sqrt(fine_len)
    cosine = (jnp.cos(angles) * factor).astype(jnp.bfloat16).astype(jnp.float32)
    sine = (jnp.sin(angles) * factor).astype(jnp.bfloat16).astype(jnp.float32)
    real_row = jnp.concatenate([cosine, sine], 1)
    imag_row = jnp.concatenate([-sine, cosine], 1)
    both = jnp.concatenate([real_row, imag_row], 0)
    for p in range(taps_count):
        tap = taps_ref[p : p + 1, :]
        table[p * 2 * keep : (p + 1) * 2 * keep, :] = (
            both * jnp.concatenate([tap, tap], 1)
        ).astype(jnp.bfloat16)

    stage[...] = jnp.zeros_like(stage)
    even[...] = jnp.zeros_like(even)
    odd[...] = jnp.zeros_like(odd)
    for first, count, copy in groups:
        copy.wait()
        parts = []
        for s in range(first, first + count):
            lanes = slice(s * fine_len, (s + 1) * fine_len)
            parts.append(jnp.concatenate([volts[0, :, lanes], volts[1, :, lanes]], 1))
        if (count * inputs) % LANES:
            parts.append(parts[-1])
        signal = jnp.concatenate(parts, 0)
        products = lax.dot_general(
            table[...], signal, (((1,), (1,)), ((), ())), preferred_element_type=jnp.float32
        )
        for u in range(first // pack, (first + len(parts)) // pack):
            lanes = slice((u - first // pack) * LANES, (u - first // pack + 1) * LANES)
            for p in range(taps_count):
                term = products[p * 2 * keep : (p + 1) * 2 * keep, lanes]
                v = u - p // pack
                if p % pack == 0:
                    if 0 <= v < rows:
                        even[v] += term
                elif 0 <= v <= rows:
                    odd[v] += term

    first_half = lax.broadcasted_iota(jnp.int32, (2 * keep, LANES), 1) < LANES // 2
    for v in range(rows):
        total = even[v]
        if pack == 2:
            late = jnp.where(first_half, odd[v + 1], odd[v])
            total = total + pltpu.roll(late, LANES // 2, 1)
        spectra[v * 2 * keep : (v + 1) * 2 * keep, :] = total

    for c in range(keep):
        owner = owner_ref[band, c]
        rank = jnp.int32(0)
        for earlier in range(c):
            rank += (owner_ref[band, earlier] == owner).astype(jnp.int32)
        piece = owner ^ band
        for part in range(2):
            line = spectra[pl.ds(part * keep + c, rows, stride=2 * keep), :]
            stage[piece, rank, part * rows : (part + 1) * rows, :] = line.astype(jnp.bfloat16)

    copies = []
    for k in range(chan_count):
        copy = pltpu.make_async_copy(stage.at[k], outs[k], out_sems.at[k])
        copy.start()
        copies.append(copy)
    for copy in copies:
        copy.wait()


def back_kernel(stn_count, chan_count, slot_cap, times, owner_ref, near_ref, far_ref, out_ref, *rest):
    result, zeros, sems = rest
    keep = owner_ref.shape[1]
    inputs = out_ref.shape[2]
    slots = chan_count * slot_cap
    band = lax.axis_index("chan")
    stn = lax.axis_index("stn")
    chip = stn // 2
    core = stn % 2
    pack = max(1, LANES // inputs)
    rows = times // pack

    held = []
    for b in range(chan_count):
        count = jnp.int32(0)
        for c in range(keep):
            count += (owner_ref[b, c] == band).astype(jnp.int32)
        held.append(count)
    total = functools.reduce(lambda x, y: x + y, held)

    zeros[...] = jnp.zeros_like(zeros)
    for slot in range(RCAP):

        @pl.when(slot >= total)
        def _():
            pltpu.make_async_copy(zeros, out_ref.at[slot], sems.at[slot]).start()

    def halves(x, y):
        if pack == 1:
            return jnp.concatenate([x, y], 1)
        return jnp.concatenate(
            [
                jnp.concatenate([x[:, :inputs], y[:, :inputs]], 1),
                jnp.concatenate([x[:, inputs:], y[:, inputs:]], 1),
            ],
            0,
        )

    for k in range(chan_count):
        source = band ^ k
        base = jnp.int32(0)
        count = jnp.int32(0)
        for b in range(chan_count):
            base += jnp.where(b < source, held[b], 0)
            count += jnp.where(b == source, held[b], 0)
        for j in range(slot_cap):
            slot = k * slot_cap + j
            mine = near_ref[slot]
            turned = jnp.concatenate([mine[rows:], -mine[:rows]], 0)
            left = halves(mine, turned)
            right = []
            for other in range(stn_count // 2):
                index = (chip ^ other) * slots + slot
                x = near_ref[index]
                y = far_ref[index]
                right.append(halves(jnp.where(core == 0, x, y), jnp.where(core == 0, y, x)))
            products = lax.dot_general(
                left,
                jnp.concatenate(right, 1),
                (((0,), (0,)), ((), ())),
                preferred_element_type=jnp.float32,
            )
            products = (products * (1.0 / times)).astype(jnp.bfloat16)
            result[slot, 0] = products[:inputs]
            result[slot, 1] = products[inputs:]
        for j in range(slot_cap):

            @pl.when(j < count)
            def _():
                pltpu.make_async_copy(
                    result.at[k * slot_cap + j], out_ref.at[base + j], sems.at[base + j]
                ).start()

    for slot in range(RCAP):
        pltpu.make_async_copy(zeros, out_ref.at[slot], sems.at[slot]).wait()


def per_device(volts, taps, survive, owner):
    chan_count = lax.axis_size("chan")
    stn_count = lax.axis_size("stn")
    inputs, samples = volts.shape[2:]
    taps_count, fine_len = taps.shape
    keep = survive.shape[1]
    blocks = samples // fine_len
    times = blocks - taps_count + 1
    slot_cap = max(2, (RCAP + chan_count - 1) // chan_count)
    pack = max(1, LANES // inputs)
    rows = times // pack
    smem = pl.BlockSpec(memory_space=pltpu.SMEM)
    vmem = pl.BlockSpec(memory_space=pltpu.VMEM)
    anywhere = pl.BlockSpec(memory_space=pl.ANY)

    block = (slot_cap, 2 * rows, pack * inputs)
    pieces = pl.pallas_call(
        functools.partial(front_kernel, chan_count, slot_cap),
        out_shape=[jax.ShapeDtypeStruct(block, jnp.bfloat16)] * chan_count,
        in_specs=[smem, smem, vmem, anywhere],
        out_specs=[anywhere] * chan_count,
        scratch_shapes=[
            pltpu.VMEM((2, inputs, samples), jnp.bfloat16),
            pltpu.VMEM((taps_count * 2 * keep, 2 * fine_len), jnp.bfloat16),
            pltpu.VMEM((rows, 2 * keep, LANES), jnp.float32),
            pltpu.VMEM((rows + 1, 2 * keep, LANES), jnp.float32),
            pltpu.VMEM((rows * 2 * keep, LANES), jnp.float32),
            pltpu.VMEM((chan_count,) + block, jnp.bfloat16),
            pltpu.SemaphoreType.DMA((-(-blocks // GROUP),)),
            pltpu.SemaphoreType.DMA((chan_count,)),
        ],
        compiler_params=pltpu.CompilerParams(vmem_limit_bytes=VMEM_LIMIT),
    )(survive, owner, taps, volts)

    held = jnp.concatenate(
        [pieces[0]] + [swapped(pieces[k], "chan", k) for k in range(1, chan_count)], 0
    )
    near = jnp.concatenate([held] + [swapped(held, "stn", m) for m in range(2, stn_count, 2)], 0)
    far = swapped(near, "stn", 1)

    out_shape = (RCAP, 2, inputs, stn_count * inputs)
    visibilities = pl.pallas_call(
        functools.partial(back_kernel, stn_count, chan_count, slot_cap, times),
        out_shape=jax.ShapeDtypeStruct(out_shape, jnp.bfloat16),
        in_specs=[smem, vmem, vmem],
        out_specs=anywhere,
        scratch_shapes=[
            pltpu.VMEM((chan_count * slot_cap,) + out_shape[1:], jnp.bfloat16),
            pltpu.VMEM(out_shape[1:], jnp.bfloat16),
            pltpu.SemaphoreType.DMA((RCAP,)),
        ],
        compiler_params=pltpu.CompilerParams(vmem_limit_bytes=VMEM_LIMIT),
    )(owner, near, far)
    return visibilities[None]


def solution(mesh):
    return jax.shard_map(
        per_device,
        mesh=mesh,
        in_specs=(P("chan", None, "stn", None), P(), P(), P()),
        out_specs=P("chan", None, None, "stn", None),
        check_vma=False,
    )
```

time: 156 us -> 39 us (0.25)
  other arithmetic: 47.9 us -> 0 us
  local copies, waits for them, and re-layouts: 46.7 us -> 4.57 us
  waiting for transfers between devices: 48.7 us -> 15.3 us
  Pallas kernels: 0 us -> 9.48 us
  matrix products: 4.8 us -> 0 us
  starting transfers between devices: 6.67 us -> 9.3 us
    transpose x1 -> x0, other arithmetic: 32.3 us -> none  [per_device(): filtered.transpose(1, 2, 0, 3).reshape(inputs * spectra_count, 2 * fine_len)]
    ppermute x7, waiting for transfers between devices: 41.7 us -> 15.3 us  [swapped(): return lax.ppermute(x, axis, [(i, i ^ mask) for i in range(peers)])]
    transpose x3 -> x0, local copies, waits for them, and re-layouts: 21.3 us -> none  [the longest x1 17.9 us: per_device(): totals.transpose(1, 2, 3, 0, 4).reshape(RCAP, 2, inputs, stn_count * inputs)]
    another operation x2 -> x0, local copies, waits for them, and re-layouts: 17.2 us -> none  [the longest x1 9.32 us: per_device(): return visibilities[None]]
    pallas_call x0 -> x2, Pallas kernels: none -> 9.48 us  [the longest x1 6.22 us: per_device(): pl.pallas_call(functools.partial(front_kernel, chan_count, slot_cap), out...]
    ppermute x7, starting transfers between devices: 0.35 us -> 9.3 us  [swapped(): return lax.ppermute(x, axis, [(i, i ^ mask) for i in range(peers)])]
    dynamic_update_slice x8 -> x0, other arithmetic: 8.33 us -> none  [place(): lax.dynamic_update_slice_in_dim(totals, split_parts(products, inputs, spe...]
    all_to_all x1 -> x0, waiting for transfers between devices: 6.94 us -> none  [per_device(): lax.all_to_all(outgoing, 'chan', split_axis=0, concat_axis=0, tiled=True)]
  transfers between devices with their start and end apart: 8 -> 7, of which waited for: 8 -> 5; matrix products, arithmetic and copies ran while one was open for 0% -> 0% of each run, Pallas kernels for 0% -> 0%
where the time goes in v1:
time: 39 us; the launch traced here: 38.8 us
  waiting for transfers between devices  15.3 us (39%)
  Pallas kernels  9.48 us (24%)
  starting transfers between devices  9.3 us (24%)
  local copies, waits for them, and re-layouts  4.57 us (12%)
    ppermute x7, waiting for transfers between devices, swapped(): return lax.ppermute(x, axis, [(i, i ^ mask) for i in range(peers)])  15.3 us
    ppermute x7, starting transfers between devices, swapped(): return lax.ppermute(x, axis, [(i, i ^ mask) for i in range(peers)])  9.3 us
    pallas_call x1, Pallas kernels, per_device(): pl.pallas_call(functools.partial(front_kernel, chan_count, slot_cap), out...  6.22 us
    unnamed x15, local copies, waits for them, and re-layouts  4.52 us
    pallas_call x1, Pallas kernels, per_device(): pl.pallas_call(functools.partial(back_kernel, stn_count, chan_count, slot...  3.26 us
  transfers between devices with their start and end apart: 7, of which 5 were waited for; matrix products, arithmetic and copies ran while one was open for 0% of the time, Pallas kernels for 0%

profile of v1, /device:TPU:0, one launch (start us, length us, event | category | flops | bytes accessed | tf_op | source)
XLA Modules:
  0.0 38.8 jit_solution(10424626661217443652)
XLA Ops:
  0.0 0.0 copy-start
  0.0 2.3 %copy-done = bf16[1,2,64,18048]{3,2,1,0:T(8,128)(2,1)S(1)} copy-done((bf16[1,2,64,18048]{3,2,1,0:T(8,128)(2,1)S(1)}, bf16[1,2,64,18048]{3,2,1,0:T(8,128)(2,1)}, u32[]{:S(2)}) %copy-start) | copy-done | bytes 4620312
  2.3 0.0 copy-start.1
  2.3 0.7 %copy-done.1 = f32[16,384]{1,0:T(8,128)S(1)} copy-done((f32[16,384]{1,0:T(8,128)S(1)}, f32[16,384]{1,0:T(8,128)}, u32[]{:S(2)}) %copy-start.1) | copy-done | bytes 24600
  3.0 0.0 copy-start.2
  3.0 0.7 %copy-done.2 = s32[4,8]{1,0:T(4,128)S(1)} copy-done((s32[4,8]{1,0:T(4,128)S(1)}, s32[4,8]{1,0:T(4,128)}, u32[]{:S(2)}) %copy-start.2) | copy-done | bytes 152
  3.7 0.0 copy-start.4
  3.7 0.7 %copy-done.4 = s32[4,8]{1,0:T(4,128)S(1)} copy-done((s32[4,8]{1,0:T(4,128)S(1)}, s32[4,8]{1,0:T(4,128)}, u32[]{:S(2)}) %copy-start.4) | copy-done | bytes 152
  4.4 0.0 copy-start.3
  4.4 6.2 %shard_map.46 = (bf16[6,32,128]{2,1,0:T(8,128)(2,1)S(1)}, bf16[6,32,128]{2,1,0:T(8,128)(2,1)S(1)}, bf16[6,32,128]{2,1,0:T(8,128)(2,1)S(1)}, bf16[6,32,128]{2,1,0:T(8,128)(2,1)S(1)}) custom-call(s32[4,8]{1,0:T(4,128)S(1)} %copy-done.4, s32[4,8]{1,0:T(4,128)S(1)} %copy-done.2, f32[16,384]{1,0:T(8,128)S(1)} %copy-done.1, bf16[1,2,64,18048]{3,2,1,0:T(8,128)(2,1)S(1)} %copy-done), custom_call_target="tpu_custom_call" | custom-call | tf_op jit(solution)/shard_map/pallas_call | solution.py:208
  10.6 3.1 %collective-permute-start = (bf16[6,32,128]{2,1,0:T(8,128)(2,1)S(1)}, bf16[6,32,128]{2,1,0:T(8,128)(2,1)S(1)}, u32[]{:S(2)}, u32[]{:S(2)}) collective-permute-start(bf16[6,32,128]{2,1,0:T(8,128)(2,1)S(1)} %get-tuple-element.10), channel_id=1, source_target_pairs={{0,1},{1,0},{2,3},{3,2},{4,5},{5,4},{6,7},{7,6},{8,9},{9,8},{10,11... | collective-permute-start | bytes 147464 | tf_op jit(solution)/shard_map/ppermute | solution.py:19
  13.7 2.6 %collective-permute-start.1 = (bf16[6,32,128]{2,1,0:T(8,128)(2,1)S(1)}, bf16[6,32,128]{2,1,0:T(8,128)(2,1)S(1)}, u32[]{:S(2)}, u32[]{:S(2)}) collective-permute-start(bf16[6,32,128]{2,1,0:T(8,128)(2,1)S(1)} %get-tuple-element.11), channel_id=1, source_target_pairs={{0,2},{1,3},{2,0},{3,1},{4,6},{5,7},{6,4},{7,5},{8,10},{9,11},{10,... | collective-permute-start | bytes 147464 | tf_op jit(solution)/shard_map/ppermute | solution.py:19
  16.3 0.0 collective-permute-start.2
  16.3 0.0 collective-permute-done
  16.4 3.3 %collective-permute-done.1 = bf16[6,32,128]{2,1,0:T(8,128)(2,1)S(1)} collective-permute-done((bf16[6,32,128]{2,1,0:T(8,128)(2,1)S(1)}, bf16[6,32,128]{2,1,0:T(8,128)(2,1)S(1)}, u32[]{:S(2)}, u32[]{:S(2)}) %collective-permute-start.1) | collective-permute-done | bytes 49184 | tf_op jit(solution)/shard_map/ppermute | solution.py:19
  19.7 2.5 %collective-permute-done.2 = bf16[6,32,128]{2,1,0:T(8,128)(2,1)S(1)} collective-permute-done((bf16[6,32,128]{2,1,0:T(8,128)(2,1)S(1)}, bf16[6,32,128]{2,1,0:T(8,128)(2,1)S(1)}, u32[]{:S(2)}, u32[]{:S(2)}) %collective-permute-start.2) | collective-permute-done | bytes 49184 | tf_op jit(solution)/shard_map/ppermute | solution.py:19
  22.2 1.6 %collective-permute-start.3 = (bf16[24,32,128]{2,1,0:T(8,128)(2,1)S(1)}, bf16[24,32,128]{2,1,0:T(8,128)(2,1)S(1)}, u32[]{:S(2)}, u32[]{:S(2)}) collective-permute-start(bf16[24,32,128]{2,1,0:T(8,128)(2,1)S(1)} %get-tuple-element.13), channel_id=1, source_target_pairs={{0,8},{4,12},{8,0},{12,4},{16,24},{20,28},{24,16},{28,20},{1,9},{5... | collective-permute-start | bytes 589832 | tf_op jit(solution)/shard_map/ppermute | solution.py:19
  23.8 1.5 %collective-permute-start.4 = (bf16[24,32,128]{2,1,0:T(8,128)(2,1)S(1)}, bf16[24,32,128]{2,1,0:T(8,128)(2,1)S(1)}, u32[]{:S(2)}, u32[]{:S(2)}) collective-permute-start(bf16[24,32,128]{2,1,0:T(8,128)(2,1)S(1)} %get-tuple-element.13), channel_id=1, source_target_pairs={{0,16},{4,20},{8,24},{12,28},{16,0},{20,4},{24,8},{28,12},{1,17},{... | collective-permute-start | bytes 589832 | tf_op jit(solution)/shard_map/ppermute | solution.py:19
  25.3 0.5 %collective-permute-start.5 = (bf16[24,32,128]{2,1,0:T(8,128)(2,1)S(1)}, bf16[24,32,128]{2,1,0:T(8,128)(2,1)S(1)}, u32[]{:S(2)}, u32[]{:S(2)}) collective-permute-start(bf16[24,32,128]{2,1,0:T(8,128)(2,1)S(1)} %get-tuple-element.13), channel_id=1, source_target_pairs={{0,24},{4,28},{8,16},{12,20},{16,8},{20,12},{24,0},{28,4},{1,25},{... | collective-permute-start | bytes 589832 | tf_op jit(solution)/shard_map/ppermute | solution.py:19
  25.8 3.9 %collective-permute-done.3 = bf16[24,32,128]{2,1,0:T(8,128)(2,1)S(1)} collective-permute-done((bf16[24,32,128]{2,1,0:T(8,128)(2,1)S(1)}, bf16[24,32,128]{2,1,0:T(8,128)(2,1)S(1)}, u32[]{:S(2)}, u32[]{:S(2)}) %collective-permute-start.3) | collective-permute-done | bytes 196640 | tf_op jit(solution)/shard_map/ppermute | solution.py:19
  29.8 3.3 %collective-permute-done.4 = bf16[24,32,128]{2,1,0:T(8,128)(2,1)S(1)} collective-permute-done((bf16[24,32,128]{2,1,0:T(8,128)(2,1)S(1)}, bf16[24,32,128]{2,1,0:T(8,128)(2,1)S(1)}, u32[]{:S(2)}, u32[]{:S(2)}) %collective-permute-start.4) | collective-permute-done | bytes 196640 | tf_op jit(solution)/shard_map/ppermute | solution.py:19
  33.1 0.0 collective-permute-done.5
  33.1 0.1 collective-permute-start.6
  33.2 2.3 %collective-permute-done.6.far_ref = bf16[96,32,128]{2,1,0:T(8,128)(2,1)S(1)} collective-permute-done((bf16[96,32,128]{2,1,0:T(8,128)(2,1)S(1)}, bf16[96,32,128]{2,1,0:T(8,128)(2,1)S(1)}, u32[]{:S(2)}, u32[]{:S(2)}) %collective-permute-start.6) | collective-permute-done | bytes 786464 | tf_op jit(solution)/shard_map/ppermute | solution.py:19
  35.5 0.0 copy-done.3
  35.5 3.3 %shard_map.47 = bf16[24,2,64,512]{3,2,1,0:T(8,128)(2,1)} custom-call(s32[4,8]{1,0:T(4,128)S(1)} %copy-done.3, bf16[96,32,128]{2,1,0:T(8,128)(2,1)S(1)} %constant_dynamic-update-slice_fusion.4.near_ref, bf16[96,32,128]{2,1,0:T(8,128)(2,1)S(1)} %collective-permute-done.6.far_ref), custom_call_target="tpu_custom_call" | custom-call | tf_op jit(solution)/shard_map/pallas_call | solution.py:233
  (7 shorter events, 0.2 us)
Async XLA Ops:
  0.0 2.3 %copy-start = (bf16[1,2,64,18048]{3,2,1,0:T(8,128)(2,1)S(1)}, bf16[1,2,64,18048]{3,2,1,0:T(8,128)(2,1)}, u32[]{:S(2)}) copy-start(bf16[1,2,64,18048]{3,2,1,0:T(8,128)(2,1)} %volts_ref.1) | copy-start | bytes 13860868
  2.3 0.7 %copy-start.1 = (f32[16,384]{1,0:T(8,128)S(1)}, f32[16,384]{1,0:T(8,128)}, u32[]{:S(2)}) copy-start(f32[16,384]{1,0:T(8,128)} %taps_ref.1) | copy-start | bytes 73732
  3.0 0.7 %copy-start.2 = (s32[4,8]{1,0:T(4,128)S(1)}, s32[4,8]{1,0:T(4,128)}, u32[]{:S(2)}) copy-start(s32[4,8]{1,0:T(4,128)} %owner_ref.3) | copy-start | bytes 388
  3.7 0.7 %copy-start.4 = (s32[4,8]{1,0:T(4,128)S(1)}, s32[4,8]{1,0:T(4,128)}, u32[]{:S(2)}) copy-start(s32[4,8]{1,0:T(4,128)} %survive_ref.1) | copy-start | bytes 388
  4.4 31.1 %copy-start.3 = (s32[4,8]{1,0:T(4,128)S(1)}, s32[4,8]{1,0:T(4,128)}, u32[]{:S(2)}) copy-start(s32[4,8]{1,0:T(4,128)} %owner_ref.3) | copy-start | bytes 388
  10.6 5.7 %collective-permute-start = (bf16[6,32,128]{2,1,0:T(8,128)(2,1)S(1)}, bf16[6,32,128]{2,1,0:T(8,128)(2,1)S(1)}, u32[]{:S(2)}, u32[]{:S(2)}) collective-permute-start(bf16[6,32,128]{2,1,0:T(8,128)(2,1)S(1)} %get-tuple-element.10), channel_id=1, source_target_pairs={{0,1},{1,0},{2,3},{3,2},{4,5},{5,4},{6,7},{7,6},{8,9},{9,8},{10,11... | collective-permute-start | bytes 147464 | tf_op jit(solution)/shard_map/ppermute | solution.py:19
  13.7 5.9 %collective-permute-start.1 = (bf16[6,32,128]{2,1,0:T(8,128)(2,1)S(1)}, bf16[6,32,128]{2,1,0:T(8,128)(2,1)S(1)}, u32[]{:S(2)}, u32[]{:S(2)}) collective-permute-start(bf16[6,32,128]{2,1,0:T(8,128)(2,1)S(1)} %get-tuple-element.11), channel_id=1, source_target_pairs={{0,2},{1,3},{2,0},{3,1},{4,6},{5,7},{6,4},{7,5},{8,10},{9,11},{10,... | collective-permute-start | bytes 147464 | tf_op jit(solution)/shard_map/ppermute | solution.py:19
  16.3 5.9 %collective-permute-start.2 = (bf16[6,32,128]{2,1,0:T(8,128)(2,1)S(1)}, bf16[6,32,128]{2,1,0:T(8,128)(2,1)S(1)}, u32[]{:S(2)}, u32[]{:S(2)}) collective-permute-start(bf16[6,32,128]{2,1,0:T(8,128)(2,1)S(1)} %get-tuple-element.12), channel_id=1, source_target_pairs={{0,3},{1,2},{2,1},{3,0},{4,7},{5,6},{6,5},{7,4},{8,11},{9,10},{10,... | collective-permute-start | bytes 147464 | tf_op jit(solution)/shard_map/ppermute | solution.py:19
  22.2 7.5 %collective-permute-start.3 = (bf16[24,32,128]{2,1,0:T(8,128)(2,1)S(1)}, bf16[24,32,128]{2,1,0:T(8,128)(2,1)S(1)}, u32[]{:S(2)}, u32[]{:S(2)}) collective-permute-start(bf16[24,32,128]{2,1,0:T(8,128)(2,1)S(1)} %get-tuple-element.13), channel_id=1, source_target_pairs={{0,8},{4,12},{8,0},{12,4},{16,24},{20,28},{24,16},{28,20},{1,9},{5... | collective-permute-start | bytes 589832 | tf_op jit(solution)/shard_map/ppermute | solution.py:19
  23.8 9.3 %collective-permute-start.4 = (bf16[24,32,128]{2,1,0:T(8,128)(2,1)S(1)}, bf16[24,32,128]{2,1,0:T(8,128)(2,1)S(1)}, u32[]{:S(2)}, u32[]{:S(2)}) collective-permute-start(bf16[24,32,128]{2,1,0:T(8,128)(2,1)S(1)} %get-tuple-element.13), channel_id=1, source_target_pairs={{0,16},{4,20},{8,24},{12,28},{16,0},{20,4},{24,8},{28,12},{1,17},{... | collective-permute-start | bytes 589832 | tf_op jit(solution)/shard_map/ppermute | solution.py:19
  25.3 7.8 %collective-permute-start.5 = (bf16[24,32,128]{2,1,0:T(8,128)(2,1)S(1)}, bf16[24,32,128]{2,1,0:T(8,128)(2,1)S(1)}, u32[]{:S(2)}, u32[]{:S(2)}) collective-permute-start(bf16[24,32,128]{2,1,0:T(8,128)(2,1)S(1)} %get-tuple-element.13), channel_id=1, source_target_pairs={{0,24},{4,28},{8,16},{12,20},{16,8},{20,12},{24,0},{28,4},{1,25},{... | collective-permute-start | bytes 589832 | tf_op jit(solution)/shard_map/ppermute | solution.py:19
  33.1 2.4 %collective-permute-start.6 = (bf16[96,32,128]{2,1,0:T(8,128)(2,1)S(1)}, bf16[96,32,128]{2,1,0:T(8,128)(2,1)S(1)}, u32[]{:S(2)}, u32[]{:S(2)}) collective-permute-start(bf16[96,32,128]{2,1,0:T(8,128)(2,1)S(1)} %constant_dynamic-update-slice_fusion.4.near_ref), channel_id=1, source_target_pairs={{0,4},{4,0},{8,12},{12,8},{16,20},{20,16},{24,28},{28,24},{1,5},{5... | collective-permute-start | bytes 2359304 | tf_op jit(solution)/shard_map/ppermute | solution.py:19

commit v2 on v1

v2 whole, which is shorter than its diff:
```python
import functools
import math

import jax
import jax.numpy as jnp
from jax import lax
from jax.experimental import pallas as pl
from jax.experimental.pallas import tpu as pltpu
from jax.sharding import PartitionSpec as P

RCAP = 24
LANES = 128
GROUPS = (24, 23)
FRONT_VMEM = 62 << 20
BACK_VMEM = 16 << 20


def swapped(x, axis, mask):
    peers = lax.axis_size(axis)
    return lax.ppermute(x, axis, [(i, i ^ mask) for i in range(peers)])


def group_sizes(blocks):
    groups, first = [], 0
    while first < blocks:
        count = min(GROUPS[min(len(groups), len(GROUPS) - 1)], blocks - first)
        groups.append((first, count))
        first += count
    return groups


def front_kernel(chan_count, slot_cap, survive_any, owner_any, taps_any, volts_ref, *rest):
    outs = rest[:chan_count]
    volts, survive_ref, owner_ref, taps_ref, table, products, spectra, stage = rest[
        chan_count:-3
    ]
    in_sems, small_sems, out_sems = rest[-3:]
    taps_count, fine_len = taps_ref.shape
    inputs, samples = volts_ref.shape[2:]
    keep = survive_ref.shape[1]
    blocks = samples // fine_len
    times = blocks - taps_count + 1
    pack = max(1, LANES // inputs)
    rows = times // pack
    band = lax.axis_index("chan")

    small = []
    for n, (source, target) in enumerate(
        ((survive_any, survive_ref), (taps_any, taps_ref), (owner_any, owner_ref))
    ):
        copy = pltpu.make_async_copy(source, target, small_sems.at[n])
        copy.start()
        small.append(copy)
    groups = []
    for first, count in group_sizes(blocks):
        lanes = pl.ds(first * fine_len, count * fine_len)
        copy = pltpu.make_async_copy(
            volts_ref.at[0, :, :, lanes], volts.at[:, :, lanes], in_sems.at[len(groups)]
        )
        copy.start()
        groups.append((first, count, copy))

    small[0].wait()
    row_ids = lax.broadcasted_iota(jnp.int32, (keep, fine_len), 0)
    branch_ids = lax.broadcasted_iota(jnp.int32, (keep, fine_len), 1)
    chosen = jnp.zeros((keep, fine_len), jnp.int32)
    for c in range(keep):
        chosen = jnp.where(row_ids == c, survive_ref[band, c], chosen)
    angles = (chosen * branch_ids % fine_len).astype(jnp.float32) * (2.0 * math.pi / fine_len)
    factor = 1.0 / math.sqrt(fine_len)
    cosine = (jnp.cos(angles) * factor).astype(jnp.bfloat16).astype(jnp.float32)
    sine = (jnp.sin(angles) * factor).astype(jnp.bfloat16).astype(jnp.float32)
    real_row = jnp.concatenate([cosine, sine], 1)
    imag_row = jnp.concatenate([-sine, cosine], 1)
    both = jnp.concatenate([real_row, imag_row], 0)
    small[1].wait()
    for p in range(taps_count):
        tap = taps_ref[p : p + 1, :]
        table[p * 2 * keep : (p + 1) * 2 * keep, :] = (
            both * jnp.concatenate([tap, tap], 1)
        ).astype(jnp.bfloat16)

    stage[...] = jnp.zeros_like(stage)
    first_half = lax.broadcasted_iota(jnp.int32, (2 * keep, LANES), 1) < LANES // 2

    def finish(v):
        sums = [None] * (2 * pack - 1)
        for p in range(taps_count):
            for late in range(1 if p % pack == 0 else 2):
                u = v + p // pack + late
                which = 0 if p % pack == 0 else 1 + late
                term = products[p * 2 * keep : (p + 1) * 2 * keep, u * LANES : (u + 1) * LANES]
                sums[which] = term if sums[which] is None else sums[which] + term
        total = sums[0]
        if pack == 2:
            total = total + pltpu.roll(jnp.where(first_half, sums[2], sums[1]), LANES // 2, 1)
        spectra[v * 2 * keep : (v + 1) * 2 * keep, :] = total

    done = 0
    ready = 0
    for first, count, copy in groups:
        copy.wait()
        parts = []
        for s in range(first, first + count):
            lanes = slice(s * fine_len, (s + 1) * fine_len)
            parts.append(jnp.concatenate([volts[0, :, lanes], volts[1, :, lanes]], 1))
        if (count * inputs) % LANES:
            parts.append(parts[-1])
        end = first + len(parts)
        products[:, first * inputs : end * inputs] = lax.dot_general(
            table[...],
            jnp.concatenate(parts, 0),
            (((1,), (1,)), ((), ())),
            preferred_element_type=jnp.float32,
        )
        while done < ready:
            finish(done)
            done += 1
        ready = min(rows, max(0, end // pack - (taps_count - 1 + pack - 1) // pack))
    while done < rows:
        finish(done)
        done += 1

    small[2].wait()
    for c in range(keep):
        owner = owner_ref[band, c]
        rank = jnp.int32(0)
        for earlier in range(c):
            rank += (owner_ref[band, earlier] == owner).astype(jnp.int32)
        piece = owner ^ band
        for part in range(2):
            line = spectra[pl.ds(part * keep + c, rows, stride=2 * keep), :]
            stage[piece, rank, part * rows : (part + 1) * rows, :] = line.astype(jnp.bfloat16)

    copies = []
    for k in range(chan_count):
        copy = pltpu.make_async_copy(stage.at[k], outs[k], out_sems.at[k])
        copy.start()
        copies.append(copy)
    for copy in copies:
        copy.wait()


def back_kernel(others, stn_count, slot_cap, times, aliased, owner_any, held_ref, *rest):
    near_refs = rest[: len(others)]
    far_refs = rest[len(others) : 2 * len(others)]
    out_ref, result, zeros, owner_ref, owner_sem, out_sem = rest[2 * len(others) + aliased :]
    bands, keep = owner_ref.shape
    inputs = out_ref.shape[2]
    width = 2 * inputs
    band = lax.axis_index("chan")
    stn = lax.axis_index("stn")
    chip = stn // 2
    core = stn % 2
    pack = max(1, LANES // inputs)
    rows = times // pack
    owner_copy = pltpu.make_async_copy(owner_any, owner_ref, owner_sem)
    owner_copy.start()
    zeros[...] = jnp.zeros_like(zeros)

    def halves(x, y):
        if pack == 1:
            return jnp.concatenate([x, y], 1)
        return jnp.concatenate(
            [
                jnp.concatenate([x[:, :inputs], y[:, :inputs]], 1),
                jnp.concatenate([x[:, inputs:], y[:, inputs:]], 1),
            ],
            0,
        )

    def correlate(slot):
        mine = held_ref[slot]
        left = halves(mine, jnp.concatenate([mine[rows:], -mine[:rows]], 0))
        right = []
        for near_ref, far_ref in zip(near_refs, far_refs):
            x = near_ref[slot]
            y = far_ref[slot]
            right.append(halves(jnp.where(core == 0, x, y), jnp.where(core == 0, y, x)))
        products = lax.dot_general(
            left,
            jnp.concatenate(right, 1),
            (((0,), (0,)), ((), ())),
            preferred_element_type=jnp.float32,
        )
        products = (products * (1.0 / times)).astype(jnp.bfloat16)
        for n in range(len(others)):
            lanes = slice(n * width, (n + 1) * width)
            result[slot, n, 0] = products[:inputs, lanes]
            result[slot, n, 1] = products[inputs:, lanes]

    def store(source, n, slot):
        column = pl.multiple_of((chip ^ others[n]) * width, LANES)
        return pltpu.make_async_copy(
            source, out_ref.at[slot, :, :, pl.ds(column, width)], out_sem.at[slot, n]
        )

    for j in range(slot_cap):
        correlate(j)

    owner_copy.wait()
    held = []
    for b in range(bands):
        count = jnp.int32(0)
        for c in range(keep):
            count += (owner_ref[b, c] == band).astype(jnp.int32)
        held.append(count)
    total = functools.reduce(lambda x, y: x + y, held)

    for k in range(bands):
        if k > 0:
            for j in range(slot_cap):
                correlate(k * slot_cap + j)
        source = band ^ k
        base = jnp.int32(0)
        count = jnp.int32(0)
        for b in range(bands):
            base += jnp.where(b < source, held[b], 0)
            count += jnp.where(b == source, held[b], 0)
        for j in range(slot_cap):

            @pl.when(j < count)
            def _():
                for n in range(len(others)):
                    store(result.at[k * slot_cap + j, n], n, base + j).start()

    for slot in range(RCAP):

        @pl.when(slot >= total)
        def _():
            for n in range(len(others)):
                store(zeros, n, slot).start()

    for slot in range(RCAP):
        for n in range(len(others)):
            store(zeros, n, slot).wait()


def per_device(volts, taps, survive, owner):
    chan_count = lax.axis_size("chan")
    stn_count = lax.axis_size("stn")
    inputs, samples = volts.shape[2:]
    taps_count, fine_len = taps.shape
    keep = survive.shape[1]
    blocks = samples // fine_len
    times = blocks - taps_count + 1
    slot_cap = max(2, (RCAP + chan_count - 1) // chan_count)
    pack = max(1, LANES // inputs)
    rows = times // pack
    smem = pl.BlockSpec(memory_space=pltpu.SMEM)
    vmem = pl.BlockSpec(memory_space=pltpu.VMEM)
    anywhere = pl.BlockSpec(memory_space=pl.ANY)

    block = (slot_cap, 2 * rows, pack * inputs)
    pieces = pl.pallas_call(
        functools.partial(front_kernel, chan_count, slot_cap),
        out_shape=[jax.ShapeDtypeStruct(block, jnp.bfloat16)] * chan_count,
        in_specs=[anywhere] * 4,
        out_specs=[anywhere] * chan_count,
        scratch_shapes=[
            pltpu.VMEM((2, inputs, samples), jnp.bfloat16),
            pltpu.SMEM(survive.shape, jnp.int32),
            pltpu.SMEM(owner.shape, jnp.int32),
            pltpu.VMEM(taps.shape, jnp.float32),
            pltpu.VMEM((taps_count * 2 * keep, 2 * fine_len), jnp.bfloat16),
            pltpu.VMEM((taps_count * 2 * keep, -(-blocks // pack) * pack * inputs), jnp.float32),
            pltpu.VMEM((rows * 2 * keep, LANES), jnp.float32),
            pltpu.VMEM((chan_count,) + block, jnp.bfloat16),
            pltpu.SemaphoreType.DMA((len(group_sizes(blocks)),)),
            pltpu.SemaphoreType.DMA((3,)),
            pltpu.SemaphoreType.DMA((chan_count,)),
        ],
        compiler_params=pltpu.CompilerParams(vmem_limit_bytes=FRONT_VMEM),
    )(survive, owner, taps, volts)

    held = jnp.concatenate(
        [pieces[0]] + [swapped(pieces[k], "chan", k) for k in range(1, chan_count)], 0
    )
    chips = list(range(stn_count // 2))
    near = [held] + [swapped(held, "stn", 2 * n) for n in chips[1:]]
    far = [swapped(x, "stn", 1) for x in near[:-1]]

    out_shape = (RCAP, 2, inputs, stn_count * inputs)

    def back(others, previous):
        blocks_in = [near[n] for n in others] + [far[n] for n in others]
        aliased = 0 if previous is None else 1
        slots = held.shape[0]
        return pl.pallas_call(
            functools.partial(back_kernel, others, stn_count, slot_cap, times, aliased),
            out_shape=jax.ShapeDtypeStruct(out_shape, jnp.bfloat16),
            in_specs=[anywhere] + [vmem] * (1 + len(blocks_in)) + [anywhere] * aliased,
            out_specs=anywhere,
            input_output_aliases={2 + len(blocks_in): 0} if aliased else {},
            scratch_shapes=[
                pltpu.VMEM((slots, len(others), 2, inputs, 2 * inputs), jnp.bfloat16),
                pltpu.VMEM((2, inputs, 2 * inputs), jnp.bfloat16),
                pltpu.SMEM(owner.shape, jnp.int32),
                pltpu.SemaphoreType.DMA(()),
                pltpu.SemaphoreType.DMA((RCAP, len(others))),
            ],
            compiler_params=pltpu.CompilerParams(vmem_limit_bytes=BACK_VMEM),
            cost_estimate=pl.CostEstimate(flops=1000, bytes_accessed=1000, transcendentals=0),
        )(owner, held, *blocks_in, *([previous] if aliased else []))

    visibilities = back(chips[:1], None)
    near[-1], visibilities = lax.optimization_barrier((near[-1], visibilities))
    far.append(swapped(near[-1], "stn", 1))
    visibilities = back(chips[1:-1], visibilities)
    visibilities = back(chips[-1:], visibilities)
    return visibilities[None]


def solution(mesh):
    return jax.shard_map(
        per_device,
        mesh=mesh,
        in_specs=(P("chan", None, "stn", None), P(), P(), P()),
        out_specs=P("chan", None, None, "stn", None),
        check_vma=False,
    )
```

time: 39 us -> 32.7 us (0.84)
  waiting for transfers between devices: 15.3 us -> 10.9 us
  local copies, waits for them, and re-layouts: 4.57 us -> 0.84 us
  Pallas kernels: 9.48 us -> 11.5 us
    ppermute x7 -> x10, waiting for transfers between devices: 15.3 us -> 10.9 us  [swapped(): return lax.ppermute(x, axis, [(i, i ^ mask) for i in range(peers)])]
    pallas_call x1 -> x3, Pallas kernels: 3.26 us -> 7.24 us  [back(): pl.pallas_call(functools.partial(back_kernel, others, stn_count, slot_cap...]
    unnamed x15 -> x5, local copies, waits for them, and re-layouts: 4.52 us -> 0.83 us
    pallas_call x1, Pallas kernels: 6.22 us -> 4.21 us  [per_device(): pl.pallas_call(functools.partial(front_kernel, chan_count, slot_cap), out...]
    ppermute x7 -> x10, starting transfers between devices: 9.3 us -> 9.24 us  [swapped(): return lax.ppermute(x, axis, [(i, i ^ mask) for i in range(peers)])]
  transfers between devices with their start and end apart: 7 -> 10, of which waited for: 5 -> 5; matrix products, arithmetic and copies ran while one was open for 0% -> 3% of each run, Pallas kernels for 0% -> 16%
where the time goes in v2:
time: 32.7 us; the launch traced here: 32.5 us
  Pallas kernels  11.5 us (35%)
  waiting for transfers between devices  10.9 us (33%)
  starting transfers between devices  9.24 us (28%)
  local copies, waits for them, and re-layouts  0.84 us (3%)
    ppermute x10, waiting for transfers between devices, swapped(): return lax.ppermute(x, axis, [(i, i ^ mask) for i in range(peers)])  10.9 us
    ppermute x10, starting transfers between devices, swapped(): return lax.ppermute(x, axis, [(i, i ^ mask) for i in range(peers)])  9.24 us
    pallas_call x3, Pallas kernels, back(): pl.pallas_call(functools.partial(back_kernel, others, stn_count, slot_cap...  7.24 us
    pallas_call x1, Pallas kernels, per_device(): pl.pallas_call(functools.partial(front_kernel, chan_count, slot_cap), out...  4.21 us
    unnamed x5, local copies, waits for them, and re-layouts  0.83 us
  transfers between devices with their start and end apart: 10, of which 5 were waited for; matrix products, arithmetic and copies ran while one was open for 3% of the time, Pallas kernels for 16%

profile of v2, /device:TPU:0, one launch (start us, length us, event | category | flops | bytes accessed | tf_op | source)
XLA Modules:
  0.0 32.5 jit_solution(5737437986600677837)
XLA Ops:
  0.0 0.0 copy-start
  0.0 4.2 %shard_map.46 = (bf16[6,32,128]{2,1,0:T(8,128)(2,1)}, bf16[6,32,128]{2,1,0:T(8,128)(2,1)}, bf16[6,32,128]{2,1,0:T(8,128)(2,1)}, bf16[6,32,128]{2,1,0:T(8,128)(2,1)}) custom-call(s32[4,8]{1,0:T(4,128)} %survive_any.1, s32[4,8]{1,0:T(4,128)} %owner_any.7, f32[16,384]{1,0:T(8,128)} %taps_any.1, bf16[1,2,64,18048]{3,2,1,0:T(8,128)(2,1)} %volts_ref.1), custom_call_target="tpu_custom_call" | custom-call | tf_op jit(solution)/shard_map/pallas_call | solution.py:255
  4.2 3.1 %collective-permute-start = (bf16[6,32,128]{2,1,0:T(8,128)(2,1)}, bf16[6,32,128]{2,1,0:T(8,128)(2,1)S(1)}, u32[]{:S(2)}, u32[]{:S(2)}) collective-permute-start(bf16[6,32,128]{2,1,0:T(8,128)(2,1)} %get-tuple-element.12), channel_id=1, source_target_pairs={{0,1},{1,0},{2,3},{3,2},{4,5},{5,4},{6,7},{7,6},{8,9},{9,8},{10,11... | collective-permute-start | bytes 147464 | tf_op jit(solution)/shard_map/ppermute | solution.py:20
  7.3 2.6 %collective-permute-start.1 = (bf16[6,32,128]{2,1,0:T(8,128)(2,1)}, bf16[6,32,128]{2,1,0:T(8,128)(2,1)S(1)}, u32[]{:S(2)}, u32[]{:S(2)}) collective-permute-start(bf16[6,32,128]{2,1,0:T(8,128)(2,1)} %get-tuple-element.13), channel_id=1, source_target_pairs={{0,2},{1,3},{2,0},{3,1},{4,6},{5,7},{6,4},{7,5},{8,10},{9,11},{10,... | collective-permute-start | bytes 147464 | tf_op jit(solution)/shard_map/ppermute | solution.py:20
  9.9 0.0 collective-permute-start.2
  9.9 0.8 %constant_dynamic-update-slice_fusion.3 = bf16[24,32,128]{2,1,0:T(8,128)(2,1)S(1)} fusion(bf16[6,32,128]{2,1,0:T(8,128)(2,1)} %get-tuple-element.11), kind=kLoop, calls=%fused_computation.3 | loop fusion | bytes 98304
  10.7 0.0 collective-permute-done
  10.7 2.7 %collective-permute-done.1 = bf16[6,32,128]{2,1,0:T(8,128)(2,1)S(1)} collective-permute-done((bf16[6,32,128]{2,1,0:T(8,128)(2,1)}, bf16[6,32,128]{2,1,0:T(8,128)(2,1)S(1)}, u32[]{:S(2)}, u32[]{:S(2)}) %collective-permute-start.1) | collective-permute-done | bytes 49184 | tf_op jit(solution)/shard_map/ppermute | solution.py:20
  13.4 2.5 %collective-permute-done.2 = bf16[6,32,128]{2,1,0:T(8,128)(2,1)S(1)} collective-permute-done((bf16[6,32,128]{2,1,0:T(8,128)(2,1)}, bf16[6,32,128]{2,1,0:T(8,128)(2,1)S(1)}, u32[]{:S(2)}, u32[]{:S(2)}) %collective-permute-start.2) | collective-permute-done | bytes 49184 | tf_op jit(solution)/shard_map/ppermute | solution.py:20
  16.0 1.6 %collective-permute-start.7 = (bf16[24,32,128]{2,1,0:T(8,128)(2,1)S(1)}, bf16[24,32,128]{2,1,0:T(8,128)(2,1)S(1)}, u32[]{:S(2)}, u32[]{:S(2)}) collective-permute-start(bf16[24,32,128]{2,1,0:T(8,128)(2,1)S(1)} %constant_dynamic-update-slice_fusion.held_ref.rest_0_), channel_id=1, source_target_pairs={{0,16},{4,20},{8,24},{12,28},{16,0},{20,4},{24,8},{28,12},{1,17},{... | collective-permute-start | bytes 589832 | tf_op jit(solution)/shard_map/ppermute | solution.py:20
  17.6 1.5 %collective-permute-start.6 = (bf16[24,32,128]{2,1,0:T(8,128)(2,1)S(1)}, bf16[24,32,128]{2,1,0:T(8,128)(2,1)S(1)}, u32[]{:S(2)}, u32[]{:S(2)}) collective-permute-start(bf16[24,32,128]{2,1,0:T(8,128)(2,1)S(1)} %constant_dynamic-update-slice_fusion.held_ref.rest_0_), channel_id=1, source_target_pairs={{0,8},{4,12},{8,0},{12,4},{16,24},{20,28},{24,16},{28,20},{1,9},{5... | collective-permute-start | bytes 589832 | tf_op jit(solution)/shard_map/ppermute | solution.py:20
  19.1 0.0 collective-permute-start.4
  19.1 0.5 %collective-permute-start.3 = (bf16[24,32,128]{2,1,0:T(8,128)(2,1)S(1)}, bf16[24,32,128]{2,1,0:T(8,128)(2,1)S(1)}, u32[]{:S(2)}, u32[]{:S(2)}) collective-permute-start(bf16[24,32,128]{2,1,0:T(8,128)(2,1)S(1)} %constant_dynamic-update-slice_fusion.held_ref.rest_0_), channel_id=1, source_target_pairs={{0,24},{4,28},{8,16},{12,20},{16,8},{20,12},{24,0},{28,4},{1,25},{... | collective-permute-start | bytes 589832 | tf_op jit(solution)/shard_map/ppermute | solution.py:20
  19.6 2.2 %collective-permute-done.7.rest_1_ = bf16[24,32,128]{2,1,0:T(8,128)(2,1)S(1)} collective-permute-done((bf16[24,32,128]{2,1,0:T(8,128)(2,1)S(1)}, bf16[24,32,128]{2,1,0:T(8,128)(2,1)S(1)}, u32[]{:S(2)}, u32[]{:S(2)}) %collective-permute-start.7) | collective-permute-done | bytes 196640 | tf_op jit(solution)/shard_map/ppermute | solution.py:20
  21.7 0.0 collective-permute-start.9
  21.7 2.7 %collective-permute-done.6.rest_0_ = bf16[24,32,128]{2,1,0:T(8,128)(2,1)S(1)} collective-permute-done((bf16[24,32,128]{2,1,0:T(8,128)(2,1)S(1)}, bf16[24,32,128]{2,1,0:T(8,128)(2,1)S(1)}, u32[]{:S(2)}, u32[]{:S(2)}) %collective-permute-start.6) | collective-permute-done | bytes 196640 | tf_op jit(solution)/shard_map/ppermute | solution.py:20
  24.4 0.0 collective-permute-start.8
  24.4 0.0 collective-permute-done.4.rest_1_
  24.4 0.0 copy-done
  24.4 2.2 %shard_map.47.rest_4_ = bf16[24,2,64,512]{3,2,1,0:T(8,128)(2,1)} custom-call(s32[4,8]{1,0:T(4,128)S(1)} %copy-done, bf16[24,32,128]{2,1,0:T(8,128)(2,1)S(1)} %constant_dynamic-update-slice_fusion.held_ref.rest_0_, bf16[24,32,128]{2,1,0:T(8,128)(2,1)S(1)} %constant_dynamic-update-slice_fusion.held_ref.rest_0_, ...), custom_call_target="tpu_custom_call" | custom-call | flops 1000 | bytes 1000 | tf_op jit(solution)/shard_map/pallas_call | solution.py:289
  26.6 0.8 %collective-permute-done.3.rest_0_ = bf16[24,32,128]{2,1,0:T(8,128)(2,1)S(1)} collective-permute-done((bf16[24,32,128]{2,1,0:T(8,128)(2,1)S(1)}, bf16[24,32,128]{2,1,0:T(8,128)(2,1)S(1)}, u32[]{:S(2)}, u32[]{:S(2)}) %collective-permute-start.3) | collective-permute-done | bytes 196640 | tf_op jit(solution)/shard_map/ppermute | solution.py:20
  27.4 0.0 collective-permute-start.5
  27.4 0.0 collective-permute-done.9.rest_3_
  27.4 0.0 collective-permute-done.8.rest_2_
  27.4 2.9 %shard_map.48.rest_2_ = bf16[24,2,64,512]{3,2,1,0:T(8,128)(2,1)} custom-call(s32[4,8]{1,0:T(4,128)S(1)} %copy-done, bf16[24,32,128]{2,1,0:T(8,128)(2,1)S(1)} %constant_dynamic-update-slice_fusion.held_ref.rest_0_, bf16[24,32,128]{2,1,0:T(8,128)(2,1)S(1)} %collective-permute-done.6.rest_0_, ...), custom_call_target="tpu_custom_call", output_to_operand_aliasing={{}: (6, {})} | custom-call | flops 1000 | bytes 1000 | tf_op jit(solution)/shard_map/pallas_call | solution.py:289
  30.3 0.0 collective-permute-done.5.rest_1_
  30.3 2.2 %shard_map.49 = bf16[24,2,64,512]{3,2,1,0:T(8,128)(2,1)} custom-call(s32[4,8]{1,0:T(4,128)S(1)} %copy-done, bf16[24,32,128]{2,1,0:T(8,128)(2,1)S(1)} %constant_dynamic-update-slice_fusion.held_ref.rest_0_, bf16[24,32,128]{2,1,0:T(8,128)(2,1)S(1)} %collective-permute-done.3.rest_0_, ...), custom_call_target="tpu_custom_call", output_to_operand_aliasing={{}: (4, {})} | custom-call | flops 1000 | bytes 1000 | tf_op jit(solution)/shard_map/pallas_call | solution.py:289
  (3 shorter events, 0.0 us)
Async XLA Ops:
  0.0 24.4 %copy-start = (s32[4,8]{1,0:T(4,128)S(1)}, s32[4,8]{1,0:T(4,128)}, u32[]{:S(2)}) copy-start(s32[4,8]{1,0:T(4,128)} %owner_any.7) | copy-start | bytes 388
  4.2 6.5 %collective-permute-start = (bf16[6,32,128]{2,1,0:T(8,128)(2,1)}, bf16[6,32,128]{2,1,0:T(8,128)(2,1)S(1)}, u32[]{:S(2)}, u32[]{:S(2)}) collective-permute-start(bf16[6,32,128]{2,1,0:T(8,128)(2,1)} %get-tuple-element.12), channel_id=1, source_target_pairs={{0,1},{1,0},{2,3},{3,2},{4,5},{5,4},{6,7},{7,6},{8,9},{9,8},{10,11... | collective-permute-start | bytes 147464 | tf_op jit(solution)/shard_map/ppermute | solution.py:20
  7.3 6.1 %collective-permute-start.1 = (bf16[6,32,128]{2,1,0:T(8,128)(2,1)}, bf16[6,32,128]{2,1,0:T(8,128)(2,1)S(1)}, u32[]{:S(2)}, u32[]{:S(2)}) collective-permute-start(bf16[6,32,128]{2,1,0:T(8,128)(2,1)} %get-tuple-element.13), channel_id=1, source_target_pairs={{0,2},{1,3},{2,0},{3,1},{4,6},{5,7},{6,4},{7,5},{8,10},{9,11},{10,... | collective-permute-start | bytes 147464 | tf_op jit(solution)/shard_map/ppermute | solution.py:20
  9.9 6.1 %collective-permute-start.2 = (bf16[6,32,128]{2,1,0:T(8,128)(2,1)}, bf16[6,32,128]{2,1,0:T(8,128)(2,1)S(1)}, u32[]{:S(2)}, u32[]{:S(2)}) collective-permute-start(bf16[6,32,128]{2,1,0:T(8,128)(2,1)} %get-tuple-element.14), channel_id=1, source_target_pairs={{0,3},{1,2},{2,1},{3,0},{4,7},{5,6},{6,5},{7,4},{8,11},{9,10},{10,... | collective-permute-start | bytes 147464 | tf_op jit(solution)/shard_map/ppermute | solution.py:20
  16.0 5.7 %collective-permute-start.7 = (bf16[24,32,128]{2,1,0:T(8,128)(2,1)S(1)}, bf16[24,32,128]{2,1,0:T(8,128)(2,1)S(1)}, u32[]{:S(2)}, u32[]{:S(2)}) collective-permute-start(bf16[24,32,128]{2,1,0:T(8,128)(2,1)S(1)} %constant_dynamic-update-slice_fusion.held_ref.rest_0_), channel_id=1, source_target_pairs={{0,16},{4,20},{8,24},{12,28},{16,0},{20,4},{24,8},{28,12},{1,17},{... | collective-permute-start | bytes 589832 | tf_op jit(solution)/shard_map/ppermute | solution.py:20
  17.6 6.8 %collective-permute-start.6 = (bf16[24,32,128]{2,1,0:T(8,128)(2,1)S(1)}, bf16[24,32,128]{2,1,0:T(8,128)(2,1)S(1)}, u32[]{:S(2)}, u32[]{:S(2)}) collective-permute-start(bf16[24,32,128]{2,1,0:T(8,128)(2,1)S(1)} %constant_dynamic-update-slice_fusion.held_ref.rest_0_), channel_id=1, source_target_pairs={{0,8},{4,12},{8,0},{12,4},{16,24},{20,28},{24,16},{28,20},{1,9},{5... | collective-permute-start | bytes 589832 | tf_op jit(solution)/shard_map/ppermute | solution.py:20
  19.1 5.3 %collective-permute-start.4 = (bf16[24,32,128]{2,1,0:T(8,128)(2,1)S(1)}, bf16[24,32,128]{2,1,0:T(8,128)(2,1)S(1)}, u32[]{:S(2)}, u32[]{:S(2)}) collective-permute-start(bf16[24,32,128]{2,1,0:T(8,128)(2,1)S(1)} %constant_dynamic-update-slice_fusion.held_ref.rest_0_), channel_id=1, source_target_pairs={{0,4},{4,0},{8,12},{12,8},{16,20},{20,16},{24,28},{28,24},{1,5},{5... | collective-permute-start | bytes 589832 | tf_op jit(solution)/shard_map/ppermute | solution.py:20
  19.1 8.3 %collective-permute-start.3 = (bf16[24,32,128]{2,1,0:T(8,128)(2,1)S(1)}, bf16[24,32,128]{2,1,0:T(8,128)(2,1)S(1)}, u32[]{:S(2)}, u32[]{:S(2)}) collective-permute-start(bf16[24,32,128]{2,1,0:T(8,128)(2,1)S(1)} %constant_dynamic-update-slice_fusion.held_ref.rest_0_), channel_id=1, source_target_pairs={{0,24},{4,28},{8,16},{12,20},{16,8},{20,12},{24,0},{28,4},{1,25},{... | collective-permute-start | bytes 589832 | tf_op jit(solution)/shard_map/ppermute | solution.py:20
  21.7 5.7 %collective-permute-start.9 = (bf16[24,32,128]{2,1,0:T(8,128)(2,1)S(1)}, bf16[24,32,128]{2,1,0:T(8,128)(2,1)S(1)}, u32[]{:S(2)}, u32[]{:S(2)}) collective-permute-start(bf16[24,32,128]{2,1,0:T(8,128)(2,1)S(1)} %collective-permute-done.7.rest_1_), channel_id=1, source_target_pairs={{0,4},{4,0},{8,12},{12,8},{16,20},{20,16},{24,28},{28,24},{1,5},{5... | collective-permute-start | bytes 589832 | tf_op jit(solution)/shard_map/ppermute | solution.py:20
  24.4 3.0 %collective-permute-start.8 = (bf16[24,32,128]{2,1,0:T(8,128)(2,1)S(1)}, bf16[24,32,128]{2,1,0:T(8,128)(2,1)S(1)}, u32[]{:S(2)}, u32[]{:S(2)}) collective-permute-start(bf16[24,32,128]{2,1,0:T(8,128)(2,1)S(1)} %collective-permute-done.6.rest_0_), channel_id=1, source_target_pairs={{0,4},{4,0},{8,12},{12,8},{16,20},{20,16},{24,28},{28,24},{1,5},{5... | collective-permute-start | bytes 589832 | tf_op jit(solution)/shard_map/ppermute | solution.py:20
  27.4 2.9 %collective-permute-start.5 = (bf16[24,32,128]{2,1,0:T(8,128)(2,1)S(1)}, bf16[24,32,128]{2,1,0:T(8,128)(2,1)S(1)}, u32[]{:S(2)}, u32[]{:S(2)}) collective-permute-start(bf16[24,32,128]{2,1,0:T(8,128)(2,1)S(1)} %collective-permute-done.3.rest_0_), channel_id=1, source_target_pairs={{0,4},{4,0},{8,12},{12,8},{16,20},{20,16},{24,28},{28,24},{1,5},{5... | collective-permute-start | bytes 589832 | tf_op jit(solution)/shard_map/ppermute | solution.py:20

commit v3 on v2

v3 whole, which is shorter than its diff:
```python
import functools
import math

import jax
import jax.numpy as jnp
from jax import lax
from jax.experimental import pallas as pl
from jax.experimental.pallas import tpu as pltpu
from jax.sharding import PartitionSpec as P

RCAP = 24
BATCH = 6
LANES = 128
GROUPS = (24, 23)
FRONT_VMEM = 62 << 20
BACK_VMEM = 16 << 20


def swapped(x, axis, mask):
    peers = lax.axis_size(axis)
    return lax.ppermute(x, axis, [(i, i ^ mask) for i in range(peers)])


def group_sizes(blocks):
    groups, first = [], 0
    while first < blocks:
        count = min(GROUPS[min(len(groups), len(GROUPS) - 1)], blocks - first)
        groups.append((first, count))
        first += count
    return groups


def front_kernel(chan_count, slot_cap, survive_any, owner_any, taps_any, volts_ref, *rest):
    outs = rest[:chan_count]
    volts, survive_ref, owner_ref, taps_ref = rest[chan_count:-7]
    table, products, spectra, stage, in_sems, small_sems, out_sems = rest[-7:]
    taps_count, fine_len = taps_ref.shape
    inputs, samples = volts_ref.shape[2:]
    keep = survive_ref.shape[1]
    blocks = samples // fine_len
    times = blocks - taps_count + 1
    pack = max(1, LANES // inputs)
    lines = times // pack
    band = lax.axis_index("chan")
    core = lax.axis_index("stn") % 2

    small = []
    for n, (source, target) in enumerate(
        ((survive_any, survive_ref), (taps_any, taps_ref), (owner_any, owner_ref))
    ):
        copy = pltpu.make_async_copy(source, target, small_sems.at[n])
        copy.start()
        small.append(copy)
    groups = []
    for first, count in group_sizes(blocks):
        lanes = pl.ds(first * fine_len, count * fine_len)
        copy = pltpu.make_async_copy(
            volts_ref.at[0, :, :, lanes], volts.at[:, :, lanes], in_sems.at[len(groups)]
        )
        copy.start()
        groups.append((first, count, copy))

    small[0].wait()
    row_ids = lax.broadcasted_iota(jnp.int32, (keep, fine_len), 0)
    branch_ids = lax.broadcasted_iota(jnp.int32, (keep, fine_len), 1)
    chosen = jnp.zeros((keep, fine_len), jnp.int32)
    for c in range(keep):
        chosen = jnp.where(row_ids == c, survive_ref[band, c], chosen)
    angles = (chosen * branch_ids % fine_len).astype(jnp.float32) * (2.0 * math.pi / fine_len)
    factor = 1.0 / math.sqrt(fine_len)
    cosine = (jnp.cos(angles) * factor).astype(jnp.bfloat16).astype(jnp.float32)
    sine = (jnp.sin(angles) * factor).astype(jnp.bfloat16).astype(jnp.float32)
    real_row = jnp.concatenate([cosine, sine], 1)
    imag_row = jnp.concatenate([-sine, cosine], 1)
    both = jnp.concatenate([real_row, imag_row], 0)
    small[1].wait()
    for p in range(taps_count):
        tap = taps_ref[p : p + 1, :]
        table[p * 2 * keep : (p + 1) * 2 * keep, :] = (
            both * jnp.concatenate([tap, tap], 1)
        ).astype(jnp.bfloat16)

    stage[...] = jnp.zeros_like(stage)
    first_half = lax.broadcasted_iota(jnp.int32, (2 * keep, LANES), 1) < LANES // 2

    def finish(v):
        sums = [None] * (2 * pack - 1)
        for p in range(taps_count):
            for late in range(1 if p % pack == 0 else 2):
                u = v + p // pack + late
                which = 0 if p % pack == 0 else 1 + late
                term = products[p * 2 * keep : (p + 1) * 2 * keep, u * LANES : (u + 1) * LANES]
                sums[which] = term if sums[which] is None else sums[which] + term
        total = sums[0]
        if pack == 2:
            late = jnp.where(first_half, sums[2], sums[1])
            total = jnp.where(core == 0, total, late) + pltpu.roll(
                jnp.where(core == 0, late, total), LANES // 2, 1
            )
        spectra[v * 2 * keep : (v + 1) * 2 * keep, :] = total

    done = 0
    ready = 0
    for first, count, copy in groups:
        copy.wait()
        parts = []
        for s in range(first, first + count):
            lanes = slice(s * fine_len, (s + 1) * fine_len)
            parts.append(jnp.concatenate([volts[0, :, lanes], volts[1, :, lanes]], 1))
        if (count * inputs) % LANES:
            parts.append(parts[-1])
        end = first + len(parts)
        products[:, first * inputs : end * inputs] = lax.dot_general(
            table[...],
            jnp.concatenate(parts, 0),
            (((1,), (1,)), ((), ())),
            preferred_element_type=jnp.float32,
        )
        while done < ready:
            finish(done)
            done += 1
        ready = min(lines, max(0, end // pack - (taps_count - 1 + pack - 1) // pack))
    while done < lines:
        finish(done)
        done += 1

    small[2].wait()
    for c in range(keep):
        owner = owner_ref[band, c]
        rank = jnp.int32(0)
        for earlier in range(c):
            rank += (owner_ref[band, earlier] == owner).astype(jnp.int32)
        piece = owner ^ band
        for part in range(2):
            line = spectra[pl.ds(part * keep + c, lines, stride=2 * keep), :]
            stage[piece, rank, part * lines : (part + 1) * lines, :] = line.astype(jnp.bfloat16)

    copies = []
    for k in range(chan_count):
        copy = pltpu.make_async_copy(stage.at[k], outs[k], out_sems.at[k])
        copy.start()
        copies.append(copy)
    for copy in copies:
        copy.wait()


def back_kernel(sequences, order, slot_cap, times, owner_any, *rest):
    chips = len(sequences)
    near = rest[:chips]
    far = [rest[chips + sequences.index((m, n))] for n, m in sequences]
    out_ref, result, zeros, owner_ref, owner_sem, sems, zero_sems = rest[2 * chips :]
    bands, keep = owner_ref.shape
    slots = near[0].shape[0]
    inputs = out_ref.shape[2]
    band = lax.axis_index("chan")
    stn = lax.axis_index("stn")
    chip = stn // 2
    core = stn % 2
    pack = max(1, LANES // inputs)
    lines = times // pack
    owner_copy = pltpu.make_async_copy(owner_any, owner_ref, owner_sem)
    owner_copy.start()
    zeros[...] = jnp.zeros_like(zeros)

    lane = lax.broadcasted_iota(jnp.int32, (2 * lines, LANES), 1)
    low = lane < LANES // 2
    first = (lane // (LANES // 2)) == core

    def turn(x):
        return jnp.concatenate([x[:, LANES // 2 :], x[:, : LANES // 2]], 1)

    def correlate(slot):
        mine = near[0][slot]
        turned = jnp.concatenate([mine[lines:], -mine[:lines]], 0)
        if pack == 1:
            left = jnp.concatenate([mine, turned], 1)
        else:
            ahead = jnp.where(low, mine, turn(turned))
            behind = jnp.where(low, turn(mine), turned)
            left = jnp.concatenate(
                [jnp.where(core == 0, ahead, behind), jnp.where(core == 0, behind, ahead)], 0
            )
        right = []
        for near_ref, far_ref in zip(near, far):
            x = near_ref[slot]
            y = far_ref[slot]
            if pack == 1:
                right.append(
                    jnp.concatenate([jnp.where(core == 0, x, y), jnp.where(core == 0, y, x)], 1)
                )
            else:
                right.append(
                    jnp.concatenate([jnp.where(first, x, y), turn(jnp.where(first, y, x))], 0)
                )
        products = lax.dot_general(
            left,
            jnp.concatenate(right, 1),
            (((0,), (0,)), ((), ())),
            preferred_element_type=jnp.float32,
        )
        products = (products * (1.0 / times)).astype(jnp.bfloat16)
        for n, distances in enumerate(sequences):
            other = chip ^ jnp.where(core == 0, distances[0], distances[1])
            here = pl.ds(pl.multiple_of(other * 2 * inputs, LANES), 2 * inputs)
            lanes = slice(n * 2 * inputs, (n + 1) * 2 * inputs)
            result[slot, 0, :, here] = products[:inputs, lanes]
            result[slot, 1, :, here] = products[inputs:, lanes]

    pending = []
    held = None
    for start in range(0, slots, BATCH):
        batch = range(start, min(slots, start + BATCH))
        for slot in batch:
            correlate(slot)
        if held is None:
            owner_copy.wait()
            held = []
            for b in range(bands):
                hits = [(owner_ref[b, c] == band).astype(jnp.int32) for c in range(keep)]
                held.append(functools.reduce(lambda x, y: x + y, hits))
            total = functools.reduce(lambda x, y: x + y, held)
            for slot in range(RCAP):
                copy = pltpu.make_async_copy(zeros, out_ref.at[slot], zero_sems.at[slot])
                pl.when(slot >= total)(copy.start)
                pending.append((slot >= total, copy))
        for slot in batch:
            source = band ^ order[slot // slot_cap]
            rank = slot % slot_cap
            row = jnp.int32(rank)
            present = jnp.int32(0)
            for b in range(bands):
                row += jnp.where(b < source, held[b], 0)
                present += jnp.where(b == source, held[b], 0)
            copy = pltpu.make_async_copy(
                result.at[slot], out_ref.at[jnp.minimum(row, RCAP - 1)], sems.at[slot]
            )
            pl.when(rank < present)(copy.start)
            pending.append((rank < present, copy))
    for started, copy in pending:
        pl.when(started)(copy.wait)


def per_device(volts, taps, survive, owner):
    chan_count = lax.axis_size("chan")
    stn_count = lax.axis_size("stn")
    inputs, samples = volts.shape[2:]
    taps_count, fine_len = taps.shape
    keep = survive.shape[1]
    blocks = samples // fine_len
    times = blocks - taps_count + 1
    slot_cap = max(2, (RCAP + chan_count - 1) // chan_count)
    pack = max(1, LANES // inputs)
    lines = times // pack
    vmem = pl.BlockSpec(memory_space=pltpu.VMEM)
    anywhere = pl.BlockSpec(memory_space=pl.ANY)

    block = (slot_cap, 2 * lines, pack * inputs)
    pieces = pl.pallas_call(
        functools.partial(front_kernel, chan_count, slot_cap),
        out_shape=[jax.ShapeDtypeStruct(block, jnp.bfloat16)] * chan_count,
        in_specs=[anywhere] * 4,
        out_specs=[anywhere] * chan_count,
        scratch_shapes=[
            pltpu.VMEM((2, inputs, samples), jnp.bfloat16),
            pltpu.SMEM(survive.shape, jnp.int32),
            pltpu.SMEM(owner.shape, jnp.int32),
            pltpu.VMEM(taps.shape, jnp.float32),
            pltpu.VMEM((taps_count * 2 * keep, 2 * fine_len), jnp.bfloat16),
            pltpu.VMEM((taps_count * 2 * keep, -(-blocks // pack) * pack * inputs), jnp.float32),
            pltpu.VMEM((lines * 2 * keep, LANES), jnp.float32),
            pltpu.VMEM((chan_count,) + block, jnp.bfloat16),
            pltpu.SemaphoreType.DMA((len(group_sizes(blocks)),)),
            pltpu.SemaphoreType.DMA((3,)),
            pltpu.SemaphoreType.DMA((chan_count,)),
        ],
        compiler_params=pltpu.CompilerParams(vmem_limit_bytes=FRONT_VMEM),
    )(survive, owner, taps, volts)

    chips = list(range(stn_count // 2))
    order = [0] + list(range(2, chan_count)) + [1]
    out_shape = (RCAP, 2, inputs, stn_count * inputs)

    sequences = []
    for n in chips:
        other = n if n == 0 or (n == chips[-1] and n % 2) else n + 1 if n % 2 else n - 1
        sequences.append((n, other))

    def exchanged(block, distances):
        pairs = [(i, i ^ (2 * distances[i % 2])) for i in range(stn_count)]
        return lax.ppermute(block, "stn", pairs)

    def gathered(block):
        return [block] + [exchanged(block, pair) for pair in sequences[1:]]

    held = jnp.concatenate([pieces[0]] + [swapped(pieces[k], "chan", k) for k in order[1:]], 0)
    slots = held.shape[0]
    near = gathered(held)
    far = [swapped(x, "stn", 1) for x in near]
    visibilities = pl.pallas_call(
        functools.partial(back_kernel, sequences, order, slot_cap, times),
        out_shape=jax.ShapeDtypeStruct(out_shape, jnp.bfloat16),
        in_specs=[anywhere] + [vmem] * (2 * len(chips)),
        out_specs=anywhere,
        scratch_shapes=[
            pltpu.VMEM((slots,) + out_shape[1:], jnp.bfloat16),
            pltpu.VMEM(out_shape[1:], jnp.bfloat16),
            pltpu.SMEM(owner.shape, jnp.int32),
            pltpu.SemaphoreType.DMA(()),
            pltpu.SemaphoreType.DMA((slots,)),
            pltpu.SemaphoreType.DMA((RCAP,)),
        ],
        compiler_params=pltpu.CompilerParams(vmem_limit_bytes=BACK_VMEM),
    )(owner, *near, *far)
    return visibilities[None]


def solution(mesh):
    return jax.shard_map(
        per_device,
        mesh=mesh,
        in_specs=(P("chan", None, "stn", None), P(), P(), P()),
        out_specs=P("chan", None, None, "stn", None),
        check_vma=False,
    )
```

time: 32.7 us -> 29.6 us (0.905)
  Pallas kernels: 11.5 us -> 7.12 us
  waiting for transfers between devices: 10.9 us -> 11.8 us
  starting transfers between devices: 9.24 us -> 9.68 us
    ppermute x0 -> x3, waiting for transfers between devices: none -> 6.81 us  [exchanged(): return lax.ppermute(block, 'stn', pairs)]
    ppermute x10 -> x7, waiting for transfers between devices: 10.9 us -> 5 us  [swapped(): return lax.ppermute(x, axis, [(i, i ^ mask) for i in range(peers)])]
    pallas_call x3 -> x1, Pallas kernels: 7.24 us -> 2.91 us  [per_device(): pl.pallas_call(functools.partial(back_kernel, sequences, order, slot_cap,...]
    ppermute x0 -> x3, starting transfers between devices: none -> 3.55 us  [exchanged(): return lax.ppermute(block, 'stn', pairs)]
    ppermute x10 -> x7, starting transfers between devices: 9.24 us -> 6.13 us  [swapped(): return lax.ppermute(x, axis, [(i, i ^ mask) for i in range(peers)])]
  transfers between devices with their start and end apart: 10 -> 10, of which waited for: 5 -> 7; matrix products, arithmetic and copies ran while one was open for 3% -> 3% of each run, Pallas kernels for 16% -> 0%
where the time goes in v3:
time: 29.6 us; the launch traced here: 29.5 us
  waiting for transfers between devices  11.8 us (40%)
  starting transfers between devices  9.68 us (33%)
  Pallas kernels  7.12 us (24%)
  local copies, waits for them, and re-layouts  0.84 us (3%)
    ppermute x3, waiting for transfers between devices, exchanged(): return lax.ppermute(block, 'stn', pairs)  6.81 us
    ppermute x7, starting transfers between devices, swapped(): return lax.ppermute(x, axis, [(i, i ^ mask) for i in range(peers)])  6.13 us
    ppermute x7, waiting for transfers between devices, swapped(): return lax.ppermute(x, axis, [(i, i ^ mask) for i in range(peers)])  5 us
    pallas_call x1, Pallas kernels, per_device(): pl.pallas_call(functools.partial(front_kernel, chan_count, slot_cap), out...  4.21 us
    ppermute x3, starting transfers between devices, exchanged(): return lax.ppermute(block, 'stn', pairs)  3.55 us
    pallas_call x1, Pallas kernels, per_device(): pl.pallas_call(functools.partial(back_kernel, sequences, order, slot_cap,...  2.91 us
    unnamed x5, local copies, waits for them, and re-layouts  0.83 us
  transfers between devices with their start and end apart: 10, of which 7 were waited for; matrix products, arithmetic and copies ran while one was open for 3% of the time, Pallas kernels for 0%

profile of v3, /device:TPU:0, one launch (start us, length us, event | category | flops | bytes accessed | tf_op | source)
XLA Modules:
  0.0 29.5 jit_solution(11731932672926905749)
XLA Ops:
  0.0 0.0 copy-start
  0.0 4.2 %shard_map.46 = (bf16[6,32,128]{2,1,0:T(8,128)(2,1)}, bf16[6,32,128]{2,1,0:T(8,128)(2,1)}, bf16[6,32,128]{2,1,0:T(8,128)(2,1)}, bf16[6,32,128]{2,1,0:T(8,128)(2,1)}) custom-call(s32[4,8]{1,0:T(4,128)} %survive_any.1, s32[4,8]{1,0:T(4,128)} %owner_any.3, f32[16,384]{1,0:T(8,128)} %taps_any.1, bf16[1,2,64,18048]{3,2,1,0:T(8,128)(2,1)} %volts_ref.1), custom_call_target="tpu_custom_call" | custom-call | tf_op jit(solution)/shard_map/pallas_call | solution.py:258
  4.2 4.1 %collective-permute-start = (bf16[6,32,128]{2,1,0:T(8,128)(2,1)}, bf16[6,32,128]{2,1,0:T(8,128)(2,1)S(1)}, u32[]{:S(2)}, u32[]{:S(2)}) collective-permute-start(bf16[6,32,128]{2,1,0:T(8,128)(2,1)} %get-tuple-element.10), channel_id=1, source_target_pairs={{0,2},{1,3},{2,0},{3,1},{4,6},{5,7},{6,4},{7,5},{8,10},{9,11},{10,... | collective-permute-start | bytes 147464 | tf_op jit(solution)/shard_map/ppermute | solution.py:21
  8.3 1.3 %collective-permute-start.1 = (bf16[6,32,128]{2,1,0:T(8,128)(2,1)}, bf16[6,32,128]{2,1,0:T(8,128)(2,1)S(1)}, u32[]{:S(2)}, u32[]{:S(2)}) collective-permute-start(bf16[6,32,128]{2,1,0:T(8,128)(2,1)} %get-tuple-element.11), channel_id=1, source_target_pairs={{0,3},{1,2},{2,1},{3,0},{4,7},{5,6},{6,5},{7,4},{8,11},{9,10},{10,... | collective-permute-start | bytes 147464 | tf_op jit(solution)/shard_map/ppermute | solution.py:21
  9.7 0.2 collective-permute-start.2
  9.9 0.8 %constant_dynamic-update-slice_fusion.3 = bf16[24,32,128]{2,1,0:T(8,128)(2,1)S(1)} fusion(bf16[6,32,128]{2,1,0:T(8,128)(2,1)} %get-tuple-element.9), kind=kLoop, calls=%fused_computation.3 | loop fusion | bytes 98304
  10.7 0.4 %collective-permute-done = bf16[6,32,128]{2,1,0:T(8,128)(2,1)S(1)} collective-permute-done((bf16[6,32,128]{2,1,0:T(8,128)(2,1)}, bf16[6,32,128]{2,1,0:T(8,128)(2,1)S(1)}, u32[]{:S(2)}, u32[]{:S(2)}) %collective-permute-start) | collective-permute-done | bytes 49184 | tf_op jit(solution)/shard_map/ppermute | solution.py:21
  11.2 3.4 %collective-permute-done.1 = bf16[6,32,128]{2,1,0:T(8,128)(2,1)S(1)} collective-permute-done((bf16[6,32,128]{2,1,0:T(8,128)(2,1)}, bf16[6,32,128]{2,1,0:T(8,128)(2,1)S(1)}, u32[]{:S(2)}, u32[]{:S(2)}) %collective-permute-start.1) | collective-permute-done | bytes 49184 | tf_op jit(solution)/shard_map/ppermute | solution.py:21
  14.5 0.0 collective-permute-done.2
  14.5 2.5 %collective-permute-start.5 = (bf16[24,32,128]{2,1,0:T(8,128)(2,1)S(1)}, bf16[24,32,128]{2,1,0:T(8,128)(2,1)S(1)}, u32[]{:S(2)}, u32[]{:S(2)}) collective-permute-start(bf16[24,32,128]{2,1,0:T(8,128)(2,1)S(1)} %constant_dynamic-update-slice_fusion.rest_0_), channel_id=1, source_target_pairs={{0,24},{4,28},{8,16},{12,20},{16,8},{20,12},{24,0},{28,4},{1,25},{... | collective-permute-start | bytes 589832 | tf_op jit(solution)/shard_map/ppermute | solution.py:290
  17.0 0.5 %collective-permute-start.4 = (bf16[24,32,128]{2,1,0:T(8,128)(2,1)S(1)}, bf16[24,32,128]{2,1,0:T(8,128)(2,1)S(1)}, u32[]{:S(2)}, u32[]{:S(2)}) collective-permute-start(bf16[24,32,128]{2,1,0:T(8,128)(2,1)S(1)} %constant_dynamic-update-slice_fusion.rest_0_), channel_id=1, source_target_pairs={{0,16},{4,12},{8,24},{12,4},{16,0},{20,28},{24,8},{28,20},{1,17},{... | collective-permute-start | bytes 589832 | tf_op jit(solution)/shard_map/ppermute | solution.py:290
  17.6 0.5 %collective-permute-start.3 = (bf16[24,32,128]{2,1,0:T(8,128)(2,1)S(1)}, bf16[24,32,128]{2,1,0:T(8,128)(2,1)S(1)}, u32[]{:S(2)}, u32[]{:S(2)}) collective-permute-start(bf16[24,32,128]{2,1,0:T(8,128)(2,1)S(1)} %constant_dynamic-update-slice_fusion.rest_0_), channel_id=1, source_target_pairs={{0,8},{4,20},{8,0},{12,28},{16,24},{20,4},{24,16},{28,12},{1,9},{5... | collective-permute-start | bytes 589832 | tf_op jit(solution)/shard_map/ppermute | solution.py:290
  18.1 0.0 collective-permute-start.6
  18.1 4.7 %collective-permute-done.5.rest_3_ = bf16[24,32,128]{2,1,0:T(8,128)(2,1)S(1)} collective-permute-done((bf16[24,32,128]{2,1,0:T(8,128)(2,1)S(1)}, bf16[24,32,128]{2,1,0:T(8,128)(2,1)S(1)}, u32[]{:S(2)}, u32[]{:S(2)}) %collective-permute-start.5) | collective-permute-done | bytes 196640 | tf_op jit(solution)/shard_map/ppermute | solution.py:290
  22.8 0.0 collective-permute-start.9
  22.8 2.0 %collective-permute-done.4.rest_2_ = bf16[24,32,128]{2,1,0:T(8,128)(2,1)S(1)} collective-permute-done((bf16[24,32,128]{2,1,0:T(8,128)(2,1)S(1)}, bf16[24,32,128]{2,1,0:T(8,128)(2,1)S(1)}, u32[]{:S(2)}, u32[]{:S(2)}) %collective-permute-start.4) | collective-permute-done | bytes 196640 | tf_op jit(solution)/shard_map/ppermute | solution.py:290
  24.8 0.0 collective-permute-start.8
  24.9 0.1 collective-permute-done.3.rest_1_
  24.9 0.4 %collective-permute-start.7 = (bf16[24,32,128]{2,1,0:T(8,128)(2,1)S(1)}, bf16[24,32,128]{2,1,0:T(8,128)(2,1)S(1)}, u32[]{:S(2)}, u32[]{:S(2)}) collective-permute-start(bf16[24,32,128]{2,1,0:T(8,128)(2,1)S(1)} %collective-permute-done.3.rest_1_), channel_id=1, source_target_pairs={{0,4},{4,0},{8,12},{12,8},{16,20},{20,16},{24,28},{28,24},{1,5},{5... | collective-permute-start | bytes 589832 | tf_op jit(solution)/shard_map/ppermute | solution.py:21
  25.4 0.0 collective-permute-done.6.rest_4_
  25.4 0.0 collective-permute-done.9.rest_7_
  25.4 0.9 %collective-permute-done.8.rest_6_ = bf16[24,32,128]{2,1,0:T(8,128)(2,1)S(1)} collective-permute-done((bf16[24,32,128]{2,1,0:T(8,128)(2,1)S(1)}, bf16[24,32,128]{2,1,0:T(8,128)(2,1)S(1)}, u32[]{:S(2)}, u32[]{:S(2)}) %collective-permute-start.8) | collective-permute-done | bytes 196640 | tf_op jit(solution)/shard_map/ppermute | solution.py:21
  26.3 0.3 collective-permute-done.7.rest_5_
  26.6 0.0 copy-done
  26.6 2.9 %shard_map.47 = bf16[24,2,64,512]{3,2,1,0:T(8,128)(2,1)} custom-call(s32[4,8]{1,0:T(4,128)S(1)} %copy-done, bf16[24,32,128]{2,1,0:T(8,128)(2,1)S(1)} %constant_dynamic-update-slice_fusion.rest_0_, bf16[24,32,128]{2,1,0:T(8,128)(2,1)S(1)} %collective-permute-done.3.rest_1_, bf16[24,32,128]{2,1,0:T(8,128)(2,1)S(1)} %collective-permute-done.4.rest_2_, ...), custom_call_target="tpu_custom_call" | custom-call | tf_op jit(solution)/shard_map/pallas_call | solution.py:299
  (3 shorter events, 0.0 us)
Async XLA Ops:
  0.0 26.6 %copy-start = (s32[4,8]{1,0:T(4,128)S(1)}, s32[4,8]{1,0:T(4,128)}, u32[]{:S(2)}) copy-start(s32[4,8]{1,0:T(4,128)} %owner_any.3) | copy-start | bytes 388
  4.2 6.9 %collective-permute-start = (bf16[6,32,128]{2,1,0:T(8,128)(2,1)}, bf16[6,32,128]{2,1,0:T(8,128)(2,1)S(1)}, u32[]{:S(2)}, u32[]{:S(2)}) collective-permute-start(bf16[6,32,128]{2,1,0:T(8,128)(2,1)} %get-tuple-element.10), channel_id=1, source_target_pairs={{0,2},{1,3},{2,0},{3,1},{4,6},{5,7},{6,4},{7,5},{8,10},{9,11},{10,... | collective-permute-start | bytes 147464 | tf_op jit(solution)/shard_map/ppermute | solution.py:21
  8.3 6.2 %collective-permute-start.1 = (bf16[6,32,128]{2,1,0:T(8,128)(2,1)}, bf16[6,32,128]{2,1,0:T(8,128)(2,1)S(1)}, u32[]{:S(2)}, u32[]{:S(2)}) collective-permute-start(bf16[6,32,128]{2,1,0:T(8,128)(2,1)} %get-tuple-element.11), channel_id=1, source_target_pairs={{0,3},{1,2},{2,1},{3,0},{4,7},{5,6},{6,5},{7,4},{8,11},{9,10},{10,... | collective-permute-start | bytes 147464 | tf_op jit(solution)/shard_map/ppermute | solution.py:21
  9.7 4.8 %collective-permute-start.2 = (bf16[6,32,128]{2,1,0:T(8,128)(2,1)}, bf16[6,32,128]{2,1,0:T(8,128)(2,1)S(1)}, u32[]{:S(2)}, u32[]{:S(2)}) collective-permute-start(bf16[6,32,128]{2,1,0:T(8,128)(2,1)} %get-tuple-element.12), channel_id=1, source_target_pairs={{0,1},{1,0},{2,3},{3,2},{4,5},{5,4},{6,7},{7,6},{8,9},{9,8},{10,11... | collective-permute-start | bytes 147464 | tf_op jit(solution)/shard_map/ppermute | solution.py:21
  14.5 8.3 %collective-permute-start.5 = (bf16[24,32,128]{2,1,0:T(8,128)(2,1)S(1)}, bf16[24,32,128]{2,1,0:T(8,128)(2,1)S(1)}, u32[]{:S(2)}, u32[]{:S(2)}) collective-permute-start(bf16[24,32,128]{2,1,0:T(8,128)(2,1)S(1)} %constant_dynamic-update-slice_fusion.rest_0_), channel_id=1, source_target_pairs={{0,24},{4,28},{8,16},{12,20},{16,8},{20,12},{24,0},{28,4},{1,25},{... | collective-permute-start | bytes 589832 | tf_op jit(solution)/shard_map/ppermute | solution.py:290
  17.0 7.8 %collective-permute-start.4 = (bf16[24,32,128]{2,1,0:T(8,128)(2,1)S(1)}, bf16[24,32,128]{2,1,0:T(8,128)(2,1)S(1)}, u32[]{:S(2)}, u32[]{:S(2)}) collective-permute-start(bf16[24,32,128]{2,1,0:T(8,128)(2,1)S(1)} %constant_dynamic-update-slice_fusion.rest_0_), channel_id=1, source_target_pairs={{0,16},{4,12},{8,24},{12,4},{16,0},{20,28},{24,8},{28,20},{1,17},{... | collective-permute-start | bytes 589832 | tf_op jit(solution)/shard_map/ppermute | solution.py:290
  17.6 7.4 %collective-permute-start.3 = (bf16[24,32,128]{2,1,0:T(8,128)(2,1)S(1)}, bf16[24,32,128]{2,1,0:T(8,128)(2,1)S(1)}, u32[]{:S(2)}, u32[]{:S(2)}) collective-permute-start(bf16[24,32,128]{2,1,0:T(8,128)(2,1)S(1)} %constant_dynamic-update-slice_fusion.rest_0_), channel_id=1, source_target_pairs={{0,8},{4,20},{8,0},{12,28},{16,24},{20,4},{24,16},{28,12},{1,9},{5... | collective-permute-start | bytes 589832 | tf_op jit(solution)/shard_map/ppermute | solution.py:290
  18.1 7.3 %collective-permute-start.6 = (bf16[24,32,128]{2,1,0:T(8,128)(2,1)S(1)}, bf16[24,32,128]{2,1,0:T(8,128)(2,1)S(1)}, u32[]{:S(2)}, u32[]{:S(2)}) collective-permute-start(bf16[24,32,128]{2,1,0:T(8,128)(2,1)S(1)} %constant_dynamic-update-slice_fusion.rest_0_), channel_id=1, source_target_pairs={{0,4},{4,0},{8,12},{12,8},{16,20},{20,16},{24,28},{28,24},{1,5},{5... | collective-permute-start | bytes 589832 | tf_op jit(solution)/shard_map/ppermute | solution.py:21
  22.8 2.5 %collective-permute-start.9 = (bf16[24,32,128]{2,1,0:T(8,128)(2,1)S(1)}, bf16[24,32,128]{2,1,0:T(8,128)(2,1)S(1)}, u32[]{:S(2)}, u32[]{:S(2)}) collective-permute-start(bf16[24,32,128]{2,1,0:T(8,128)(2,1)S(1)} %collective-permute-done.5.rest_3_), channel_id=1, source_target_pairs={{0,4},{4,0},{8,12},{12,8},{16,20},{20,16},{24,28},{28,24},{1,5},{5... | collective-permute-start | bytes 589832 | tf_op jit(solution)/shard_map/ppermute | solution.py:21
  24.8 1.4 %collective-permute-start.8 = (bf16[24,32,128]{2,1,0:T(8,128)(2,1)S(1)}, bf16[24,32,128]{2,1,0:T(8,128)(2,1)S(1)}, u32[]{:S(2)}, u32[]{:S(2)}) collective-permute-start(bf16[24,32,128]{2,1,0:T(8,128)(2,1)S(1)} %collective-permute-done.4.rest_2_), channel_id=1, source_target_pairs={{0,4},{4,0},{8,12},{12,8},{16,20},{20,16},{24,28},{28,24},{1,5},{5... | collective-permute-start | bytes 589832 | tf_op jit(solution)/shard_map/ppermute | solution.py:21
  24.9 1.7 %collective-permute-start.7 = (bf16[24,32,128]{2,1,0:T(8,128)(2,1)S(1)}, bf16[24,32,128]{2,1,0:T(8,128)(2,1)S(1)}, u32[]{:S(2)}, u32[]{:S(2)}) collective-permute-start(bf16[24,32,128]{2,1,0:T(8,128)(2,1)S(1)} %collective-permute-done.3.rest_1_), channel_id=1, source_target_pairs={{0,4},{4,0},{8,12},{12,8},{16,20},{20,16},{24,28},{28,24},{1,5},{5... | collective-permute-start | bytes 589832 | tf_op jit(solution)/shard_map/ppermute | solution.py:21

commit v4 on v3

--- a/solution.py
+++ b/solution.py
@@ -9,10 +9,9 @@
 from jax.sharding import PartitionSpec as P
 
 RCAP = 24
-BATCH = 6
 LANES = 128
 GROUPS = (24, 23)
-FRONT_VMEM = 62 << 20
+FRONT_VMEM = 24 << 20
 BACK_VMEM = 16 << 20
 
 
@@ -30,10 +29,9 @@
     return groups
 
 
-def front_kernel(chan_count, slot_cap, survive_any, owner_any, taps_any, volts_ref, *rest):
-    outs = rest[:chan_count]
-    volts, survive_ref, owner_ref, taps_ref = rest[chan_count:-7]
-    table, products, spectra, stage, in_sems, small_sems, out_sems = rest[-7:]
+def front_kernel(chan_count, survive_any, owner_any, taps_any, volts_ref, *rest):
+    pieces, volts, survive_ref, owner_ref, taps_ref, table, products, spectra = rest[:-2]
+    in_sems, small_sems = rest[-2:]
     taps_count, fine_len = taps_ref.shape
     inputs, samples = volts_ref.shape[2:]
     keep = survive_ref.shape[1]
@@ -80,7 +78,7 @@
             both * jnp.concatenate([tap, tap], 1)
         ).astype(jnp.bfloat16)
 
-    stage[...] = jnp.zeros_like(stage)
+    pieces[...] = jnp.zeros_like(pieces)
     first_half = lax.broadcasted_iota(jnp.int32, (2 * keep, LANES), 1) < LANES // 2
 
     def finish(v):
@@ -133,22 +131,14 @@
         piece = owner ^ band
         for part in range(2):
             line = spectra[pl.ds(part * keep + c, lines, stride=2 * keep), :]
-            stage[piece, rank, part * lines : (part + 1) * lines, :] = line.astype(jnp.bfloat16)
-
-    copies = []
-    for k in range(chan_count):
-        copy = pltpu.make_async_copy(stage.at[k], outs[k], out_sems.at[k])
-        copy.start()
-        copies.append(copy)
-    for copy in copies:
-        copy.wait()
-
-
-def back_kernel(sequences, order, slot_cap, times, owner_any, *rest):
+            pieces[piece, rank, part * lines : (part + 1) * lines, :] = line.astype(jnp.bfloat16)
+
+
+def back_kernel(sequences, order, slot_cap, times, owner_ref, *rest):
     chips = len(sequences)
     near = rest[:chips]
     far = [rest[chips + sequences.index((m, n))] for n, m in sequences]
-    out_ref, result, zeros, owner_ref, owner_sem, sems, zero_sems = rest[2 * chips :]
+    out_ref, result, lefts, places, sems = rest[2 * chips :]
     bands, keep = owner_ref.shape
     slots = near[0].shape[0]
     inputs = out_ref.shape[2]
@@ -158,9 +148,13 @@
     core = stn % 2
     pack = max(1, LANES // inputs)
     lines = times // pack
-    owner_copy = pltpu.make_async_copy(owner_any, owner_ref, owner_sem)
-    owner_copy.start()
-    zeros[...] = jnp.zeros_like(zeros)
+
+    bits = jnp.where(
+        owner_ref[...] == band,
+        jnp.left_shift(1, lax.broadcasted_iota(jnp.int32, (bands, keep), 1)).astype(jnp.float32),
+        0.0,
+    )
+    held = [jnp.sum(bits[b : b + 1]).astype(jnp.int32) for b in range(bands)]
 
     lane = lax.broadcasted_iota(jnp.int32, (2 * lines, LANES), 1)
     low = lane < LANES // 2
@@ -169,21 +163,38 @@
     def turn(x):
         return jnp.concatenate([x[:, LANES // 2 :], x[:, : LANES // 2]], 1)
 
-    def correlate(slot):
-        mine = near[0][slot]
+    for place in range(slots):
+        mine = near[0][place]
         turned = jnp.concatenate([mine[lines:], -mine[:lines]], 0)
         if pack == 1:
-            left = jnp.concatenate([mine, turned], 1)
+            lefts[place] = jnp.concatenate([mine, turned], 1)
         else:
             ahead = jnp.where(low, mine, turn(turned))
             behind = jnp.where(low, turn(mine), turned)
-            left = jnp.concatenate(
+            lefts[place] = jnp.concatenate(
                 [jnp.where(core == 0, ahead, behind), jnp.where(core == 0, behind, ahead)], 0
             )
+
+    for slot in range(RCAP):
+        places[slot] = 0
+    total = jnp.int32(0)
+    for b in range(bands):
+        place = jnp.int32(0)
+        for n, k in enumerate(order):
+            place = jnp.where(b ^ band == k, n * slot_cap, place)
+        for c in range(keep):
+            mine = (held[b] >> c) & 1
+            places[jnp.where(mine == 1, total, RCAP)] = place
+            total += mine
+            place += mine
+
+    copies = []
+    for slot in range(RCAP):
+        place = places[slot]
         right = []
         for near_ref, far_ref in zip(near, far):
-            x = near_ref[slot]
-            y = far_ref[slot]
+            x = near_ref[place]
+            y = far_ref[place]
             if pack == 1:
                 right.append(
                     jnp.concatenate([jnp.where(core == 0, x, y), jnp.where(core == 0, y, x)], 1)
@@ -193,51 +204,23 @@
                     jnp.concatenate([jnp.where(first, x, y), turn(jnp.where(first, y, x))], 0)
                 )
         products = lax.dot_general(
-            left,
+            lefts[place],
             jnp.concatenate(right, 1),
             (((0,), (0,)), ((), ())),
             preferred_element_type=jnp.float32,
         )
-        products = (products * (1.0 / times)).astype(jnp.bfloat16)
+        products = jnp.where(slot < total, products * (1.0 / times), 0.0).astype(jnp.bfloat16)
         for n, distances in enumerate(sequences):
             other = chip ^ jnp.where(core == 0, distances[0], distances[1])
             here = pl.ds(pl.multiple_of(other * 2 * inputs, LANES), 2 * inputs)
             lanes = slice(n * 2 * inputs, (n + 1) * 2 * inputs)
             result[slot, 0, :, here] = products[:inputs, lanes]
             result[slot, 1, :, here] = products[inputs:, lanes]
-
-    pending = []
-    held = None
-    for start in range(0, slots, BATCH):
-        batch = range(start, min(slots, start + BATCH))
-        for slot in batch:
-            correlate(slot)
-        if held is None:
-            owner_copy.wait()
-            held = []
-            for b in range(bands):
-                hits = [(owner_ref[b, c] == band).astype(jnp.int32) for c in range(keep)]
-                held.append(functools.reduce(lambda x, y: x + y, hits))
-            total = functools.reduce(lambda x, y: x + y, held)
-            for slot in range(RCAP):
-                copy = pltpu.make_async_copy(zeros, out_ref.at[slot], zero_sems.at[slot])
-                pl.when(slot >= total)(copy.start)
-                pending.append((slot >= total, copy))
-        for slot in batch:
-            source = band ^ order[slot // slot_cap]
-            rank = slot % slot_cap
-            row = jnp.int32(rank)
-            present = jnp.int32(0)
-            for b in range(bands):
-                row += jnp.where(b < source, held[b], 0)
-                present += jnp.where(b == source, held[b], 0)
-            copy = pltpu.make_async_copy(
-                result.at[slot], out_ref.at[jnp.minimum(row, RCAP - 1)], sems.at[slot]
-            )
-            pl.when(rank < present)(copy.start)
-            pending.append((rank < present, copy))
-    for started, copy in pending:
-        pl.when(started)(copy.wait)
+        copy = pltpu.make_async_copy(result.at[slot], out_ref.at[slot], sems.at[slot])
+        copy.start()
+        copies.append(copy)
+    for copy in copies:
+        copy.wait()
 
 
 def per_device(volts, taps, survive, owner):
@@ -256,10 +239,10 @@
 
     block = (slot_cap, 2 * lines, pack * inputs)
     pieces = pl.pallas_call(
-        functools.partial(front_kernel, chan_count, slot_cap),
-        out_shape=[jax.ShapeDtypeStruct(block, jnp.bfloat16)] * chan_count,
-        in_specs=[anywhere] * 4,
-        out_specs=[anywhere] * chan_count,
+        functools.partial(front_kernel, chan_count),
+        out_shape=pltpu.VMEM((chan_count,) + block, jnp.bfloat16),
+        in_specs=[pl.BlockSpec(memory_space=pltpu.HBM)] * 4,
+        out_specs=vmem,
         scratch_shapes=[
             pltpu.VMEM((2, inputs, samples), jnp.bfloat16),
             pltpu.SMEM(survive.shape, jnp.int32),
@@ -268,16 +251,14 @@
             pltpu.VMEM((taps_count * 2 * keep, 2 * fine_len), jnp.bfloat16),
             pltpu.VMEM((taps_count * 2 * keep, -(-blocks // pack) * pack * inputs), jnp.float32),
             pltpu.VMEM((lines * 2 * keep, LANES), jnp.float32),
-            pltpu.VMEM((chan_count,) + block, jnp.bfloat16),
             pltpu.SemaphoreType.DMA((len(group_sizes(blocks)),)),
             pltpu.SemaphoreType.DMA((3,)),
-            pltpu.SemaphoreType.DMA((chan_count,)),
         ],
         compiler_params=pltpu.CompilerParams(vmem_limit_bytes=FRONT_VMEM),
-    )(survive, owner, taps, volts)
+    )(*[pltpu.with_memory_space_constraint(x, pltpu.HBM) for x in (survive, owner, taps, volts)])
 
     chips = list(range(stn_count // 2))
-    order = [0] + list(range(2, chan_count)) + [1]
+    order = [0, 1] + list(range(chan_count - 1, 1, -1))
     out_shape = (RCAP, 2, inputs, stn_count * inputs)
 
     sequences = []
@@ -299,14 +280,12 @@
     visibilities = pl.pallas_call(
         functools.partial(back_kernel, sequences, order, slot_cap, times),
         out_shape=jax.ShapeDtypeStruct(out_shape, jnp.bfloat16),
-        in_specs=[anywhere] + [vmem] * (2 * len(chips)),
+        in_specs=[vmem] * (1 + 2 * len(chips)),
         out_specs=anywhere,
         scratch_shapes=[
-            pltpu.VMEM((slots,) + out_shape[1:], jnp.bfloat16),
-            pltpu.VMEM(out_shape[1:], jnp.bfloat16),
-            pltpu.SMEM(owner.shape, jnp.int32),
-            pltpu.SemaphoreType.DMA(()),
-            pltpu.SemaphoreType.DMA((slots,)),
+            pltpu.VMEM(out_shape, jnp.bfloat16),
+            pltpu.VMEM((slots, 2 * lines * pack, 2 * inputs), jnp.bfloat16),
+            pltpu.SMEM((RCAP + 1,), jnp.int32),
             pltpu.SemaphoreType.DMA((RCAP,)),
         ],
         compiler_params=pltpu.CompilerParams(vmem_limit_bytes=BACK_VMEM),

time: 29.6 us -> 28.3 us (0.956)
  Pallas kernels: 7.12 us -> 6.03 us
  local copies, waits for them, and re-layouts: 0.84 us -> 0.02 us
  waiting for transfers between devices: 11.8 us -> 12.4 us
    unnamed x5 -> x2, local copies, waits for them, and re-layouts: 0.83 us -> 0.01 us
    pallas_call x1, Pallas kernels: 4.21 us -> 3.51 us  [per_device(): pl.pallas_call(functools.partial(front_kernel, chan_count), out_shape=plt...]
    ppermute x7, waiting for transfers between devices: 5 us -> 5.6 us  [swapped(): return lax.ppermute(x, axis, [(i, i ^ mask) for i in range(peers)])]
    pallas_call x1, Pallas kernels: 2.91 us -> 2.52 us  [per_device(): pl.pallas_call(functools.partial(back_kernel, sequences, order, slot_cap,...]
  transfers between devices with their start and end apart: 10 -> 10, of which waited for: 7 -> 7; matrix products, arithmetic and copies ran while one was open for 3% -> 0% of each run, Pallas kernels for 0% -> 0%
where the time goes in v4:
time: 28.3 us; the launch traced here: 28.2 us
  waiting for transfers between devices  12.4 us (44%)
  starting transfers between devices  9.68 us (34%)
  Pallas kernels  6.03 us (21%)
    ppermute x3, waiting for transfers between devices, exchanged(): return lax.ppermute(block, 'stn', pairs)  6.81 us
    ppermute x7, starting transfers between devices, swapped(): return lax.ppermute(x, axis, [(i, i ^ mask) for i in range(peers)])  6.13 us
    ppermute x7, waiting for transfers between devices, swapped(): return lax.ppermute(x, axis, [(i, i ^ mask) for i in range(peers)])  5.6 us
    ppermute x3, starting transfers between devices, exchanged(): return lax.ppermute(block, 'stn', pairs)  3.55 us
    pallas_call x1, Pallas kernels, per_device(): pl.pallas_call(functools.partial(front_kernel, chan_count), out_shape=plt...  3.51 us
    pallas_call x1, Pallas kernels, per_device(): pl.pallas_call(functools.partial(back_kernel, sequences, order, slot_cap,...  2.52 us
  transfers between devices with their start and end apart: 10, of which 7 were waited for; matrix products, arithmetic and copies ran while one was open for 0% of the time, Pallas kernels for 0%

profile of v4, /device:TPU:0, one launch (start us, length us, event | category | flops | bytes accessed | tf_op | source)
XLA Modules:
  0.0 28.2 jit_solution(5183002941511879909)
XLA Ops:
  0.0 0.0 copy-start
  0.0 3.5 %shard_map.46 = bf16[4,6,32,128]{3,2,1,0:T(8,128)(2,1)S(1)} custom-call(s32[4,8]{1,0:T(4,128)} %survive_any.1, s32[4,8]{1,0:T(4,128)} %owner_ref.1, f32[16,384]{1,0:T(8,128)} %taps_any.1, bf16[1,2,64,18048]{3,2,1,0:T(8,128)(2,1)} %volts_ref.1), custom_call_target="tpu_custom_call" | custom-call | tf_op jit(solution)/shard_map/pallas_call | solution.py:241
  3.5 4.1 %collective-permute-start.2 = (bf16[6,32,128]{2,1,0:T(8,128)(2,1)S(1)}, bf16[6,32,128]{2,1,0:T(8,128)(2,1)S(1)}, u32[]{:S(2)}, u32[]{:S(2)}) collective-permute-start(bf16[6,32,128]{2,1,0:T(8,128)(2,1)S(1)} %get-tuple-element.6), channel_id=1, source_target_pairs={{0,2},{1,3},{2,0},{3,1},{4,6},{5,7},{6,4},{7,5},{8,10},{9,11},{10,... | collective-permute-start | bytes 147464 | tf_op jit(solution)/shard_map/ppermute | solution.py:20
  7.7 1.3 %collective-permute-start.1 = (bf16[6,32,128]{2,1,0:T(8,128)(2,1)S(1)}, bf16[6,32,128]{2,1,0:T(8,128)(2,1)S(1)}, u32[]{:S(2)}, u32[]{:S(2)}) collective-permute-start(bf16[6,32,128]{2,1,0:T(8,128)(2,1)S(1)} %get-tuple-element.7), channel_id=1, source_target_pairs={{0,3},{1,2},{2,1},{3,0},{4,7},{5,6},{6,5},{7,4},{8,11},{9,10},{10,... | collective-permute-start | bytes 147464 | tf_op jit(solution)/shard_map/ppermute | solution.py:20
  9.0 0.2 collective-permute-start
  9.2 1.0 %collective-permute-done.2 = bf16[6,32,128]{2,1,0:T(8,128)(2,1)S(1)} collective-permute-done((bf16[6,32,128]{2,1,0:T(8,128)(2,1)S(1)}, bf16[6,32,128]{2,1,0:T(8,128)(2,1)S(1)}, u32[]{:S(2)}, u32[]{:S(2)}) %collective-permute-start.2) | collective-permute-done | bytes 49184 | tf_op jit(solution)/shard_map/ppermute | solution.py:20
  10.3 3.4 %collective-permute-done.1 = bf16[6,32,128]{2,1,0:T(8,128)(2,1)S(1)} collective-permute-done((bf16[6,32,128]{2,1,0:T(8,128)(2,1)S(1)}, bf16[6,32,128]{2,1,0:T(8,128)(2,1)S(1)}, u32[]{:S(2)}, u32[]{:S(2)}) %collective-permute-start.1) | collective-permute-done | bytes 49184 | tf_op jit(solution)/shard_map/ppermute | solution.py:20
  13.6 0.0 collective-permute-done
  13.7 2.5 %collective-permute-start.5 = (bf16[24,32,128]{2,1,0:T(8,128)(2,1)S(1)}, bf16[24,32,128]{2,1,0:T(8,128)(2,1)S(1)}, u32[]{:S(2)}, u32[]{:S(2)}) collective-permute-start(bf16[24,32,128]{2,1,0:T(8,128)(2,1)S(1)} %pad_maximum_fusion.rest_0_), channel_id=1, source_target_pairs={{0,24},{4,28},{8,16},{12,20},{16,8},{20,12},{24,0},{28,4},{1,25},{... | collective-permute-start | bytes 589832 | tf_op jit(solution)/shard_map/ppermute | solution.py:271
  16.2 0.5 %collective-permute-start.4 = (bf16[24,32,128]{2,1,0:T(8,128)(2,1)S(1)}, bf16[24,32,128]{2,1,0:T(8,128)(2,1)S(1)}, u32[]{:S(2)}, u32[]{:S(2)}) collective-permute-start(bf16[24,32,128]{2,1,0:T(8,128)(2,1)S(1)} %pad_maximum_fusion.rest_0_), channel_id=1, source_target_pairs={{0,16},{4,12},{8,24},{12,4},{16,0},{20,28},{24,8},{28,20},{1,17},{... | collective-permute-start | bytes 589832 | tf_op jit(solution)/shard_map/ppermute | solution.py:271
  16.7 0.5 %collective-permute-start.3 = (bf16[24,32,128]{2,1,0:T(8,128)(2,1)S(1)}, bf16[24,32,128]{2,1,0:T(8,128)(2,1)S(1)}, u32[]{:S(2)}, u32[]{:S(2)}) collective-permute-start(bf16[24,32,128]{2,1,0:T(8,128)(2,1)S(1)} %pad_maximum_fusion.rest_0_), channel_id=1, source_target_pairs={{0,8},{4,20},{8,0},{12,28},{16,24},{20,4},{24,16},{28,12},{1,9},{5... | collective-permute-start | bytes 589832 | tf_op jit(solution)/shard_map/ppermute | solution.py:271
  17.2 0.0 collective-permute-start.6
  17.2 4.7 %collective-permute-done.5.rest_3_ = bf16[24,32,128]{2,1,0:T(8,128)(2,1)S(1)} collective-permute-done((bf16[24,32,128]{2,1,0:T(8,128)(2,1)S(1)}, bf16[24,32,128]{2,1,0:T(8,128)(2,1)S(1)}, u32[]{:S(2)}, u32[]{:S(2)}) %collective-permute-start.5) | collective-permute-done | bytes 196640 | tf_op jit(solution)/shard_map/ppermute | solution.py:271
  22.0 0.0 collective-permute-start.9
  22.0 2.0 %collective-permute-done.4.rest_2_ = bf16[24,32,128]{2,1,0:T(8,128)(2,1)S(1)} collective-permute-done((bf16[24,32,128]{2,1,0:T(8,128)(2,1)S(1)}, bf16[24,32,128]{2,1,0:T(8,128)(2,1)S(1)}, u32[]{:S(2)}, u32[]{:S(2)}) %collective-permute-start.4) | collective-permute-done | bytes 196640 | tf_op jit(solution)/shard_map/ppermute | solution.py:271
  24.0 0.0 collective-permute-start.8
  24.0 0.1 collective-permute-done.3.rest_1_
  24.0 0.4 %collective-permute-start.7 = (bf16[24,32,128]{2,1,0:T(8,128)(2,1)S(1)}, bf16[24,32,128]{2,1,0:T(8,128)(2,1)S(1)}, u32[]{:S(2)}, u32[]{:S(2)}) collective-permute-start(bf16[24,32,128]{2,1,0:T(8,128)(2,1)S(1)} %collective-permute-done.3.rest_1_), channel_id=1, source_target_pairs={{0,4},{4,0},{8,12},{12,8},{16,20},{20,16},{24,28},{28,24},{1,5},{5... | collective-permute-start | bytes 589832 | tf_op jit(solution)/shard_map/ppermute | solution.py:20
  24.5 0.0 collective-permute-done.6.rest_4_
  24.5 0.0 collective-permute-done.9.rest_7_
  24.5 0.9 %collective-permute-done.8.rest_6_ = bf16[24,32,128]{2,1,0:T(8,128)(2,1)S(1)} collective-permute-done((bf16[24,32,128]{2,1,0:T(8,128)(2,1)S(1)}, bf16[24,32,128]{2,1,0:T(8,128)(2,1)S(1)}, u32[]{:S(2)}, u32[]{:S(2)}) %collective-permute-start.8) | collective-permute-done | bytes 196640 | tf_op jit(solution)/shard_map/ppermute | solution.py:20
  25.4 0.3 collective-permute-done.7.rest_5_
  25.7 0.0 copy-done
  25.7 2.5 %shard_map.47 = bf16[24,2,64,512]{3,2,1,0:T(8,128)(2,1)} custom-call(s32[4,8]{1,0:T(4,128)S(1)} %copy-done, bf16[24,32,128]{2,1,0:T(8,128)(2,1)S(1)} %pad_maximum_fusion.rest_0_, bf16[24,32,128]{2,1,0:T(8,128)(2,1)S(1)} %collective-permute-done.3.rest_1_, bf16[24,32,128]{2,1,0:T(8,128)(2,1)S(1)} %collective-permute-done.4.rest_2_, ...), custom_call_target="tpu_custom_call" | custom-call | tf_op jit(solution)/shard_map/pallas_call | solution.py:280
  (2 shorter events, 0.0 us)
Async XLA Ops:
  0.0 25.7 %copy-start = (s32[4,8]{1,0:T(4,128)S(1)}, s32[4,8]{1,0:T(4,128)}, u32[]{:S(2)}) copy-start(s32[4,8]{1,0:T(4,128)} %owner_ref.1) | copy-start | bytes 388
  3.5 6.7 %collective-permute-start.2 = (bf16[6,32,128]{2,1,0:T(8,128)(2,1)S(1)}, bf16[6,32,128]{2,1,0:T(8,128)(2,1)S(1)}, u32[]{:S(2)}, u32[]{:S(2)}) collective-permute-start(bf16[6,32,128]{2,1,0:T(8,128)(2,1)S(1)} %get-tuple-element.6), channel_id=1, source_target_pairs={{0,2},{1,3},{2,0},{3,1},{4,6},{5,7},{6,4},{7,5},{8,10},{9,11},{10,... | collective-permute-start | bytes 147464 | tf_op jit(solution)/shard_map/ppermute | solution.py:20
  7.7 6.0 %collective-permute-start.1 = (bf16[6,32,128]{2,1,0:T(8,128)(2,1)S(1)}, bf16[6,32,128]{2,1,0:T(8,128)(2,1)S(1)}, u32[]{:S(2)}, u32[]{:S(2)}) collective-permute-start(bf16[6,32,128]{2,1,0:T(8,128)(2,1)S(1)} %get-tuple-element.7), channel_id=1, source_target_pairs={{0,3},{1,2},{2,1},{3,0},{4,7},{5,6},{6,5},{7,4},{8,11},{9,10},{10,... | collective-permute-start | bytes 147464 | tf_op jit(solution)/shard_map/ppermute | solution.py:20
  9.0 4.6 %collective-permute-start = (bf16[6,32,128]{2,1,0:T(8,128)(2,1)S(1)}, bf16[6,32,128]{2,1,0:T(8,128)(2,1)S(1)}, u32[]{:S(2)}, u32[]{:S(2)}) collective-permute-start(bf16[6,32,128]{2,1,0:T(8,128)(2,1)S(1)} %get-tuple-element.8), channel_id=1, source_target_pairs={{0,1},{1,0},{2,3},{3,2},{4,5},{5,4},{6,7},{7,6},{8,9},{9,8},{10,11... | collective-permute-start | bytes 147464 | tf_op jit(solution)/shard_map/ppermute | solution.py:20
  13.7 8.3 %collective-permute-start.5 = (bf16[24,32,128]{2,1,0:T(8,128)(2,1)S(1)}, bf16[24,32,128]{2,1,0:T(8,128)(2,1)S(1)}, u32[]{:S(2)}, u32[]{:S(2)}) collective-permute-start(bf16[24,32,128]{2,1,0:T(8,128)(2,1)S(1)} %pad_maximum_fusion.rest_0_), channel_id=1, source_target_pairs={{0,24},{4,28},{8,16},{12,20},{16,8},{20,12},{24,0},{28,4},{1,25},{... | collective-permute-start | bytes 589832 | tf_op jit(solution)/shard_map/ppermute | solution.py:271
  16.2 7.8 %collective-permute-start.4 = (bf16[24,32,128]{2,1,0:T(8,128)(2,1)S(1)}, bf16[24,32,128]{2,1,0:T(8,128)(2,1)S(1)}, u32[]{:S(2)}, u32[]{:S(2)}) collective-permute-start(bf16[24,32,128]{2,1,0:T(8,128)(2,1)S(1)} %pad_maximum_fusion.rest_0_), channel_id=1, source_target_pairs={{0,16},{4,12},{8,24},{12,4},{16,0},{20,28},{24,8},{28,20},{1,17},{... | collective-permute-start | bytes 589832 | tf_op jit(solution)/shard_map/ppermute | solution.py:271
  16.7 7.4 %collective-permute-start.3 = (bf16[24,32,128]{2,1,0:T(8,128)(2,1)S(1)}, bf16[24,32,128]{2,1,0:T(8,128)(2,1)S(1)}, u32[]{:S(2)}, u32[]{:S(2)}) collective-permute-start(bf16[24,32,128]{2,1,0:T(8,128)(2,1)S(1)} %pad_maximum_fusion.rest_0_), channel_id=1, source_target_pairs={{0,8},{4,20},{8,0},{12,28},{16,24},{20,4},{24,16},{28,12},{1,9},{5... | collective-permute-start | bytes 589832 | tf_op jit(solution)/shard_map/ppermute | solution.py:271
  17.2 7.3 %collective-permute-start.6 = (bf16[24,32,128]{2,1,0:T(8,128)(2,1)S(1)}, bf16[24,32,128]{2,1,0:T(8,128)(2,1)S(1)}, u32[]{:S(2)}, u32[]{:S(2)}) collective-permute-start(bf16[24,32,128]{2,1,0:T(8,128)(2,1)S(1)} %pad_maximum_fusion.rest_0_), channel_id=1, source_target_pairs={{0,4},{4,0},{8,12},{12,8},{16,20},{20,16},{24,28},{28,24},{1,5},{5... | collective-permute-start | bytes 589832 | tf_op jit(solution)/shard_map/ppermute | solution.py:20
  22.0 2.5 %collective-permute-start.9 = (bf16[24,32,128]{2,1,0:T(8,128)(2,1)S(1)}, bf16[24,32,128]{2,1,0:T(8,128)(2,1)S(1)}, u32[]{:S(2)}, u32[]{:S(2)}) collective-permute-start(bf16[24,32,128]{2,1,0:T(8,128)(2,1)S(1)} %collective-permute-done.5.rest_3_), channel_id=1, source_target_pairs={{0,4},{4,0},{8,12},{12,8},{16,20},{20,16},{24,28},{28,24},{1,5},{5... | collective-permute-start | bytes 589832 | tf_op jit(solution)/shard_map/ppermute | solution.py:20
  24.0 1.4 %collective-permute-start.8 = (bf16[24,32,128]{2,1,0:T(8,128)(2,1)S(1)}, bf16[24,32,128]{2,1,0:T(8,128)(2,1)S(1)}, u32[]{:S(2)}, u32[]{:S(2)}) collective-permute-start(bf16[24,32,128]{2,1,0:T(8,128)(2,1)S(1)} %collective-permute-done.4.rest_2_), channel_id=1, source_target_pairs={{0,4},{4,0},{8,12},{12,8},{16,20},{20,16},{24,28},{28,24},{1,5},{5... | collective-permute-start | bytes 589832 | tf_op jit(solution)/shard_map/ppermute | solution.py:20
  24.0 1.7 %collective-permute-start.7 = (bf16[24,32,128]{2,1,0:T(8,128)(2,1)S(1)}, bf16[24,32,128]{2,1,0:T(8,128)(2,1)S(1)}, u32[]{:S(2)}, u32[]{:S(2)}) collective-permute-start(bf16[24,32,128]{2,1,0:T(8,128)(2,1)S(1)} %collective-permute-done.3.rest_1_), channel_id=1, source_target_pairs={{0,4},{4,0},{8,12},{12,8},{16,20},{20,16},{24,28},{28,24},{1,5},{5... | collective-permute-start | bytes 589832 | tf_op jit(solution)/shard_map/ppermute | solution.py:20

commit v5 on v4

--- a/solution.py
+++ b/solution.py
@@ -10,7 +10,8 @@
 
 RCAP = 24
 LANES = 128
-GROUPS = (24, 23)
+GROUPS = (16, 16, 15)
+GROUP = 8
 FRONT_VMEM = 24 << 20
 BACK_VMEM = 16 << 20
 
@@ -101,19 +102,21 @@
     ready = 0
     for first, count, copy in groups:
         copy.wait()
-        parts = []
-        for s in range(first, first + count):
-            lanes = slice(s * fine_len, (s + 1) * fine_len)
-            parts.append(jnp.concatenate([volts[0, :, lanes], volts[1, :, lanes]], 1))
-        if (count * inputs) % LANES:
-            parts.append(parts[-1])
-        end = first + len(parts)
-        products[:, first * inputs : end * inputs] = lax.dot_general(
-            table[...],
-            jnp.concatenate(parts, 0),
-            (((1,), (1,)), ((), ())),
-            preferred_element_type=jnp.float32,
-        )
+        end = first
+        while end < first + count:
+            parts = []
+            for s in range(end, min(end + GROUP, first + count)):
+                lanes = slice(s * fine_len, (s + 1) * fine_len)
+                parts.append(jnp.concatenate([volts[0, :, lanes], volts[1, :, lanes]], 1))
+            if (len(parts) * inputs) % LANES:
+                parts.append(parts[-1])
+            products[:, end * inputs : (end + len(parts)) * inputs] = lax.dot_general(
+                table[...],
+                jnp.concatenate(parts, 0),
+                (((1,), (1,)), ((), ())),
+                preferred_element_type=jnp.float32,
+            )
+            end += len(parts)
         while done < ready:
             finish(done)
             done += 1
@@ -134,39 +137,20 @@
             pieces[piece, rank, part * lines : (part + 1) * lines, :] = line.astype(jnp.bfloat16)
 
 
-def back_kernel(sequences, order, slot_cap, times, owner_ref, *rest):
-    chips = len(sequences)
-    near = rest[:chips]
-    far = [rest[chips + sequences.index((m, n))] for n, m in sequences]
-    out_ref, result, lefts, places, sems = rest[2 * chips :]
+def turn(x):
+    return jnp.concatenate([x[:, LANES // 2 :], x[:, : LANES // 2]], 1)
+
+
+def left_kernel(inputs, order, slot_cap, owner_ref, held_ref, lefts, places):
     bands, keep = owner_ref.shape
-    slots = near[0].shape[0]
-    inputs = out_ref.shape[2]
     band = lax.axis_index("chan")
-    stn = lax.axis_index("stn")
-    chip = stn // 2
-    core = stn % 2
-    pack = max(1, LANES // inputs)
-    lines = times // pack
-
-    bits = jnp.where(
-        owner_ref[...] == band,
-        jnp.left_shift(1, lax.broadcasted_iota(jnp.int32, (bands, keep), 1)).astype(jnp.float32),
-        0.0,
-    )
-    held = [jnp.sum(bits[b : b + 1]).astype(jnp.int32) for b in range(bands)]
-
-    lane = lax.broadcasted_iota(jnp.int32, (2 * lines, LANES), 1)
-    low = lane < LANES // 2
-    first = (lane // (LANES // 2)) == core
-
-    def turn(x):
-        return jnp.concatenate([x[:, LANES // 2 :], x[:, : LANES // 2]], 1)
-
+    core = lax.axis_index("stn") % 2
+    slots, lines = held_ref.shape[0], held_ref.shape[1] // 2
+    low = lax.broadcasted_iota(jnp.int32, (2 * lines, LANES), 1) < LANES // 2
     for place in range(slots):
-        mine = near[0][place]
+        mine = held_ref[place]
         turned = jnp.concatenate([mine[lines:], -mine[:lines]], 0)
-        if pack == 1:
+        if inputs >= LANES:
             lefts[place] = jnp.concatenate([mine, turned], 1)
         else:
             ahead = jnp.where(low, mine, turn(turned))
@@ -174,6 +158,13 @@
             lefts[place] = jnp.concatenate(
                 [jnp.where(core == 0, ahead, behind), jnp.where(core == 0, behind, ahead)], 0
             )
+
+    bits = jnp.where(
+        owner_ref[...] == band,
+        jnp.left_shift(1, lax.broadcasted_iota(jnp.int32, (bands, keep), 1)).astype(jnp.float32),
+        0.0,
+    )
+    held = [jnp.sum(bits[b : b + 1]).astype(jnp.int32) for b in range(bands)]
 
     for slot in range(RCAP):
         places[slot] = 0
@@ -187,7 +178,25 @@
             places[jnp.where(mine == 1, total, RCAP)] = place
             total += mine
             place += mine
-
+    places[RCAP + 1] = total
+
+
+def back_kernel(sequences, times, places, *rest):
+    chips = len(sequences)
+    near = rest[:chips]
+    far = [rest[chips + sequences.index((m, n))] for n, m in sequences]
+    lefts, out_ref, result, sems = rest[2 * chips :]
+    inputs = out_ref.shape[2]
+    stn = lax.axis_index("stn")
+    chip = stn // 2
+    core = stn % 2
+    pack = max(1, LANES // inputs)
+    lines = times // pack
+
+    lane = lax.broadcasted_iota(jnp.int32, (2 * lines, LANES), 1)
+    first = (lane // (LANES // 2)) == core
+
+    total = places[RCAP + 1]
     copies = []
     for slot in range(RCAP):
         place = places[slot]
@@ -235,6 +244,7 @@
     pack = max(1, LANES // inputs)
     lines = times // pack
     vmem = pl.BlockSpec(memory_space=pltpu.VMEM)
+    smem = pl.BlockSpec(memory_space=pltpu.SMEM)
     anywhere = pl.BlockSpec(memory_space=pl.ANY)
 
     block = (slot_cap, 2 * lines, pack * inputs)
@@ -277,19 +287,27 @@
     slots = held.shape[0]
     near = gathered(held)
     far = [swapped(x, "stn", 1) for x in near]
+    lefts, places = pl.pallas_call(
+        functools.partial(left_kernel, inputs, order, slot_cap),
+        out_shape=[
+            pltpu.VMEM((slots, 2 * lines * pack, 2 * inputs), jnp.bfloat16),
+            pltpu.SMEM((RCAP + 2,), jnp.int32),
+        ],
+        in_specs=[vmem] * 2,
+        out_specs=[vmem, smem],
+        compiler_params=pltpu.CompilerParams(vmem_limit_bytes=BACK_VMEM),
+    )(owner, held)
     visibilities = pl.pallas_call(
-        functools.partial(back_kernel, sequences, order, slot_cap, times),
+        functools.partial(back_kernel, sequences, times),
         out_shape=jax.ShapeDtypeStruct(out_shape, jnp.bfloat16),
-        in_specs=[vmem] * (1 + 2 * len(chips)),
+        in_specs=[smem] + [vmem] * (1 + 2 * len(chips)),
         out_specs=anywhere,
         scratch_shapes=[
             pltpu.VMEM(out_shape, jnp.bfloat16),
-            pltpu.VMEM((slots, 2 * lines * pack, 2 * inputs), jnp.bfloat16),
-            pltpu.SMEM((RCAP + 1,), jnp.int32),
             pltpu.SemaphoreType.DMA((RCAP,)),
         ],
         compiler_params=pltpu.CompilerParams(vmem_limit_bytes=BACK_VMEM),
-    )(owner, *near, *far)
+    )(places, *near, *far, lefts)
     return visibilities[None]
 
 

time: 28.3 us -> 28 us (0.989)
    pallas_call x1 -> x2, Pallas kernels: 2.52 us -> 2.47 us  [the longest x1 2.26 us: per_device(): pl.pallas_call(functools.partial(back_kernel, sequences, times), out_shap...]
  transfers between devices with their start and end apart: 10 -> 10, of which waited for: 7 -> 7; matrix products, arithmetic and copies ran while one was open for 0% -> 0% of each run, Pallas kernels for 0% -> 1%
where the time goes in v5:
time: 28 us; the launch traced here: 27.9 us
  waiting for transfers between devices  12.2 us (44%)
  starting transfers between devices  9.69 us (35%)
  Pallas kernels  5.92 us (21%)
    ppermute x3, waiting for transfers between devices, exchanged(): return lax.ppermute(block, 'stn', pairs)  6.82 us
    ppermute x7, starting transfers between devices, swapped(): return lax.ppermute(x, axis, [(i, i ^ mask) for i in range(peers)])  6.13 us
    ppermute x7, waiting for transfers between devices, swapped(): return lax.ppermute(x, axis, [(i, i ^ mask) for i in range(peers)])  5.35 us
    ppermute x3, starting transfers between devices, exchanged(): return lax.ppermute(block, 'stn', pairs)  3.55 us
    pallas_call x1, Pallas kernels, per_device(): pl.pallas_call(functools.partial(front_kernel, chan_count), out_shape=plt...  3.45 us
    pallas_call x1, Pallas kernels, per_device(): pl.pallas_call(functools.partial(back_kernel, sequences, times), out_shap...  2.26 us
  transfers between devices with their start and end apart: 10, of which 7 were waited for; matrix products, arithmetic and copies ran while one was open for 0% of the time, Pallas kernels for 1%

profile of v5, /device:TPU:0, one launch (start us, length us, event | category | flops | bytes accessed | tf_op | source)
XLA Modules:
  0.0 27.9 jit_solution(4938331446893261874)
XLA Ops:
  0.0 0.0 copy-start
  0.0 3.5 %shard_map.46 = bf16[4,6,32,128]{3,2,1,0:T(8,128)(2,1)S(1)} custom-call(s32[4,8]{1,0:T(4,128)} %survive_any.1, s32[4,8]{1,0:T(4,128)} %owner_ref.1, f32[16,384]{1,0:T(8,128)} %taps_any.1, bf16[1,2,64,18048]{3,2,1,0:T(8,128)(2,1)} %volts_ref.1), custom_call_target="tpu_custom_call" | custom-call | tf_op jit(solution)/shard_map/pallas_call | solution.py:251
  3.5 4.1 %collective-permute-start.2 = (bf16[6,32,128]{2,1,0:T(8,128)(2,1)S(1)}, bf16[6,32,128]{2,1,0:T(8,128)(2,1)S(1)}, u32[]{:S(2)}, u32[]{:S(2)}) collective-permute-start(bf16[6,32,128]{2,1,0:T(8,128)(2,1)S(1)} %get-tuple-element.10), channel_id=1, source_target_pairs={{0,2},{1,3},{2,0},{3,1},{4,6},{5,7},{6,4},{7,5},{8,10},{9,11},{10,... | collective-permute-start | bytes 147464 | tf_op jit(solution)/shard_map/ppermute | solution.py:21
  7.6 1.3 %collective-permute-start.1 = (bf16[6,32,128]{2,1,0:T(8,128)(2,1)S(1)}, bf16[6,32,128]{2,1,0:T(8,128)(2,1)S(1)}, u32[]{:S(2)}, u32[]{:S(2)}) collective-permute-start(bf16[6,32,128]{2,1,0:T(8,128)(2,1)S(1)} %get-tuple-element.11), channel_id=1, source_target_pairs={{0,3},{1,2},{2,1},{3,0},{4,7},{5,6},{6,5},{7,4},{8,11},{9,10},{10,... | collective-permute-start | bytes 147464 | tf_op jit(solution)/shard_map/ppermute | solution.py:21
  8.9 0.2 collective-permute-start
  9.2 1.0 %collective-permute-done.2 = bf16[6,32,128]{2,1,0:T(8,128)(2,1)S(1)} collective-permute-done((bf16[6,32,128]{2,1,0:T(8,128)(2,1)S(1)}, bf16[6,32,128]{2,1,0:T(8,128)(2,1)S(1)}, u32[]{:S(2)}, u32[]{:S(2)}) %collective-permute-start.2) | collective-permute-done | bytes 49184 | tf_op jit(solution)/shard_map/ppermute | solution.py:21
  10.2 3.4 %collective-permute-done.1 = bf16[6,32,128]{2,1,0:T(8,128)(2,1)S(1)} collective-permute-done((bf16[6,32,128]{2,1,0:T(8,128)(2,1)S(1)}, bf16[6,32,128]{2,1,0:T(8,128)(2,1)S(1)}, u32[]{:S(2)}, u32[]{:S(2)}) %collective-permute-start.1) | collective-permute-done | bytes 49184 | tf_op jit(solution)/shard_map/ppermute | solution.py:21
  13.6 0.0 collective-permute-done
  13.6 2.5 %collective-permute-start.5 = (bf16[24,32,128]{2,1,0:T(8,128)(2,1)S(1)}, bf16[24,32,128]{2,1,0:T(8,128)(2,1)S(1)}, u32[]{:S(2)}, u32[]{:S(2)}) collective-permute-start(bf16[24,32,128]{2,1,0:T(8,128)(2,1)S(1)} %pad_maximum_fusion.held_ref.rest_0_), channel_id=1, source_target_pairs={{0,24},{4,28},{8,16},{12,20},{16,8},{20,12},{24,0},{28,4},{1,25},{... | collective-permute-start | bytes 589832 | tf_op jit(solution)/shard_map/ppermute | solution.py:281
  16.1 0.5 %collective-permute-start.4 = (bf16[24,32,128]{2,1,0:T(8,128)(2,1)S(1)}, bf16[24,32,128]{2,1,0:T(8,128)(2,1)S(1)}, u32[]{:S(2)}, u32[]{:S(2)}) collective-permute-start(bf16[24,32,128]{2,1,0:T(8,128)(2,1)S(1)} %pad_maximum_fusion.held_ref.rest_0_), channel_id=1, source_target_pairs={{0,16},{4,12},{8,24},{12,4},{16,0},{20,28},{24,8},{28,20},{1,17},{... | collective-permute-start | bytes 589832 | tf_op jit(solution)/shard_map/ppermute | solution.py:281
  16.6 0.5 %collective-permute-start.3 = (bf16[24,32,128]{2,1,0:T(8,128)(2,1)S(1)}, bf16[24,32,128]{2,1,0:T(8,128)(2,1)S(1)}, u32[]{:S(2)}, u32[]{:S(2)}) collective-permute-start(bf16[24,32,128]{2,1,0:T(8,128)(2,1)S(1)} %pad_maximum_fusion.held_ref.rest_0_), channel_id=1, source_target_pairs={{0,8},{4,20},{8,0},{12,28},{16,24},{20,4},{24,16},{28,12},{1,9},{5... | collective-permute-start | bytes 589832 | tf_op jit(solution)/shard_map/ppermute | solution.py:281
  17.1 0.0 collective-permute-start.6
  17.1 4.8 %collective-permute-done.5.rest_3_ = bf16[24,32,128]{2,1,0:T(8,128)(2,1)S(1)} collective-permute-done((bf16[24,32,128]{2,1,0:T(8,128)(2,1)S(1)}, bf16[24,32,128]{2,1,0:T(8,128)(2,1)S(1)}, u32[]{:S(2)}, u32[]{:S(2)}) %collective-permute-start.5) | collective-permute-done | bytes 196640 | tf_op jit(solution)/shard_map/ppermute | solution.py:281
  21.9 0.0 collective-permute-start.9
  21.9 2.0 %collective-permute-done.4.rest_2_ = bf16[24,32,128]{2,1,0:T(8,128)(2,1)S(1)} collective-permute-done((bf16[24,32,128]{2,1,0:T(8,128)(2,1)S(1)}, bf16[24,32,128]{2,1,0:T(8,128)(2,1)S(1)}, u32[]{:S(2)}, u32[]{:S(2)}) %collective-permute-start.4) | collective-permute-done | bytes 196640 | tf_op jit(solution)/shard_map/ppermute | solution.py:281
  23.9 0.0 collective-permute-start.8
  23.9 0.1 collective-permute-done.3.rest_1_
  24.0 0.4 %collective-permute-start.7 = (bf16[24,32,128]{2,1,0:T(8,128)(2,1)S(1)}, bf16[24,32,128]{2,1,0:T(8,128)(2,1)S(1)}, u32[]{:S(2)}, u32[]{:S(2)}) collective-permute-start(bf16[24,32,128]{2,1,0:T(8,128)(2,1)S(1)} %collective-permute-done.3.rest_1_), channel_id=1, source_target_pairs={{0,4},{4,0},{8,12},{12,8},{16,20},{20,16},{24,28},{28,24},{1,5},{5... | collective-permute-start | bytes 589832 | tf_op jit(solution)/shard_map/ppermute | solution.py:21
  24.4 0.0 copy-done
  24.4 0.2 shard_map.47
  24.6 0.0 collective-permute-done.6.rest_4_
  24.6 0.0 collective-permute-done.9.rest_7_
  24.7 0.7 %collective-permute-done.8.rest_6_ = bf16[24,32,128]{2,1,0:T(8,128)(2,1)S(1)} collective-permute-done((bf16[24,32,128]{2,1,0:T(8,128)(2,1)S(1)}, bf16[24,32,128]{2,1,0:T(8,128)(2,1)S(1)}, u32[]{:S(2)}, u32[]{:S(2)}) %collective-permute-start.8) | collective-permute-done | bytes 196640 | tf_op jit(solution)/shard_map/ppermute | solution.py:21
  25.3 0.3 %collective-permute-done.7.rest_5_ = bf16[24,32,128]{2,1,0:T(8,128)(2,1)S(1)} collective-permute-done((bf16[24,32,128]{2,1,0:T(8,128)(2,1)S(1)}, bf16[24,32,128]{2,1,0:T(8,128)(2,1)S(1)}, u32[]{:S(2)}, u32[]{:S(2)}) %collective-permute-start.7) | collective-permute-done | bytes 196640 | tf_op jit(solution)/shard_map/ppermute | solution.py:21
  25.6 2.3 %shard_map.48 = bf16[24,2,64,512]{3,2,1,0:T(8,128)(2,1)} custom-call(s32[26]{0:T(128)S(4)} %get-tuple-element.7.places, bf16[24,32,128]{2,1,0:T(8,128)(2,1)S(1)} %pad_maximum_fusion.held_ref.rest_0_, bf16[24,32,128]{2,1,0:T(8,128)(2,1)S(1)} %collective-permute-done.3.rest_1_, bf16[24,32,128]{2,1,0:T(8,128)(2,1)S(1)} %collective-permute-done.4.rest_2_, ...), custom_call_target="tpu_custom_call" | custom-call | tf_op jit(solution)/shard_map/pallas_call | solution.py:300
  (2 shorter events, 0.0 us)
Async XLA Ops:
  0.0 24.4 %copy-start = (s32[4,8]{1,0:T(4,128)S(1)}, s32[4,8]{1,0:T(4,128)}, u32[]{:S(2)}) copy-start(s32[4,8]{1,0:T(4,128)} %owner_ref.1) | copy-start | bytes 388
  3.5 6.7 %collective-permute-start.2 = (bf16[6,32,128]{2,1,0:T(8,128)(2,1)S(1)}, bf16[6,32,128]{2,1,0:T(8,128)(2,1)S(1)}, u32[]{:S(2)}, u32[]{:S(2)}) collective-permute-start(bf16[6,32,128]{2,1,0:T(8,128)(2,1)S(1)} %get-tuple-element.10), channel_id=1, source_target_pairs={{0,2},{1,3},{2,0},{3,1},{4,6},{5,7},{6,4},{7,5},{8,10},{9,11},{10,... | collective-permute-start | bytes 147464 | tf_op jit(solution)/shard_map/ppermute | solution.py:21
  7.6 6.0 %collective-permute-start.1 = (bf16[6,32,128]{2,1,0:T(8,128)(2,1)S(1)}, bf16[6,32,128]{2,1,0:T(8,128)(2,1)S(1)}, u32[]{:S(2)}, u32[]{:S(2)}) collective-permute-start(bf16[6,32,128]{2,1,0:T(8,128)(2,1)S(1)} %get-tuple-element.11), channel_id=1, source_target_pairs={{0,3},{1,2},{2,1},{3,0},{4,7},{5,6},{6,5},{7,4},{8,11},{9,10},{10,... | collective-permute-start | bytes 147464 | tf_op jit(solution)/shard_map/ppermute | solution.py:21
  8.9 4.6 %collective-permute-start = (bf16[6,32,128]{2,1,0:T(8,128)(2,1)S(1)}, bf16[6,32,128]{2,1,0:T(8,128)(2,1)S(1)}, u32[]{:S(2)}, u32[]{:S(2)}) collective-permute-start(bf16[6,32,128]{2,1,0:T(8,128)(2,1)S(1)} %get-tuple-element.12), channel_id=1, source_target_pairs={{0,1},{1,0},{2,3},{3,2},{4,5},{5,4},{6,7},{7,6},{8,9},{9,8},{10,11... | collective-permute-start | bytes 147464 | tf_op jit(solution)/shard_map/ppermute | solution.py:21
  13.6 8.3 %collective-permute-start.5 = (bf16[24,32,128]{2,1,0:T(8,128)(2,1)S(1)}, bf16[24,32,128]{2,1,0:T(8,128)(2,1)S(1)}, u32[]{:S(2)}, u32[]{:S(2)}) collective-permute-start(bf16[24,32,128]{2,1,0:T(8,128)(2,1)S(1)} %pad_maximum_fusion.held_ref.rest_0_), channel_id=1, source_target_pairs={{0,24},{4,28},{8,16},{12,20},{16,8},{20,12},{24,0},{28,4},{1,25},{... | collective-permute-start | bytes 589832 | tf_op jit(solution)/shard_map/ppermute | solution.py:281
  16.1 7.8 %collective-permute-start.4 = (bf16[24,32,128]{2,1,0:T(8,128)(2,1)S(1)}, bf16[24,32,128]{2,1,0:T(8,128)(2,1)S(1)}, u32[]{:S(2)}, u32[]{:S(2)}) collective-permute-start(bf16[24,32,128]{2,1,0:T(8,128)(2,1)S(1)} %pad_maximum_fusion.held_ref.rest_0_), channel_id=1, source_target_pairs={{0,16},{4,12},{8,24},{12,4},{16,0},{20,28},{24,8},{28,20},{1,17},{... | collective-permute-start | bytes 589832 | tf_op jit(solution)/shard_map/ppermute | solution.py:281
  16.6 7.4 %collective-permute-start.3 = (bf16[24,32,128]{2,1,0:T(8,128)(2,1)S(1)}, bf16[24,32,128]{2,1,0:T(8,128)(2,1)S(1)}, u32[]{:S(2)}, u32[]{:S(2)}) collective-permute-start(bf16[24,32,128]{2,1,0:T(8,128)(2,1)S(1)} %pad_maximum_fusion.held_ref.rest_0_), channel_id=1, source_target_pairs={{0,8},{4,20},{8,0},{12,28},{16,24},{20,4},{24,16},{28,12},{1,9},{5... | collective-permute-start | bytes 589832 | tf_op jit(solution)/shard_map/ppermute | solution.py:281
  17.1 7.5 %collective-permute-start.6 = (bf16[24,32,128]{2,1,0:T(8,128)(2,1)S(1)}, bf16[24,32,128]{2,1,0:T(8,128)(2,1)S(1)}, u32[]{:S(2)}, u32[]{:S(2)}) collective-permute-start(bf16[24,32,128]{2,1,0:T(8,128)(2,1)S(1)} %pad_maximum_fusion.held_ref.rest_0_), channel_id=1, source_target_pairs={{0,4},{4,0},{8,12},{12,8},{16,20},{20,16},{24,28},{28,24},{1,5},{5... | collective-permute-start | bytes 589832 | tf_op jit(solution)/shard_map/ppermute | solution.py:21
  21.9 2.8 %collective-permute-start.9 = (bf16[24,32,128]{2,1,0:T(8,128)(2,1)S(1)}, bf16[24,32,128]{2,1,0:T(8,128)(2,1)S(1)}, u32[]{:S(2)}, u32[]{:S(2)}) collective-permute-start(bf16[24,32,128]{2,1,0:T(8,128)(2,1)S(1)} %collective-permute-done.5.rest_3_), channel_id=1, source_target_pairs={{0,4},{4,0},{8,12},{12,8},{16,20},{20,16},{24,28},{28,24},{1,5},{5... | collective-permute-start | bytes 589832 | tf_op jit(solution)/shard_map/ppermute | solution.py:21
  23.9 1.4 %collective-permute-start.8 = (bf16[24,32,128]{2,1,0:T(8,128)(2,1)S(1)}, bf16[24,32,128]{2,1,0:T(8,128)(2,1)S(1)}, u32[]{:S(2)}, u32[]{:S(2)}) collective-permute-start(bf16[24,32,128]{2,1,0:T(8,128)(2,1)S(1)} %collective-permute-done.4.rest_2_), channel_id=1, source_target_pairs={{0,4},{4,0},{8,12},{12,8},{16,20},{20,16},{24,28},{28,24},{1,5},{5... | collective-permute-start | bytes 589832 | tf_op jit(solution)/shard_map/ppermute | solution.py:21
  24.0 1.6 %collective-permute-start.7 = (bf16[24,32,128]{2,1,0:T(8,128)(2,1)S(1)}, bf16[24,32,128]{2,1,0:T(8,128)(2,1)S(1)}, u32[]{:S(2)}, u32[]{:S(2)}) collective-permute-start(bf16[24,32,128]{2,1,0:T(8,128)(2,1)S(1)} %collective-permute-done.3.rest_1_), channel_id=1, source_target_pairs={{0,4},{4,0},{8,12},{12,8},{16,20},{20,16},{24,28},{28,24},{1,5},{5... | collective-permute-start | bytes 589832 | tf_op jit(solution)/shard_map/ppermute | solution.py:21

commit v6 on v5

--- a/solution.py
+++ b/solution.py
@@ -141,7 +141,44 @@
     return jnp.concatenate([x[:, LANES // 2 :], x[:, : LANES // 2]], 1)
 
 
-def left_kernel(inputs, order, slot_cap, owner_ref, held_ref, lefts, places):
+def fill(result, slot, place, total, times, members, near, far, lefts):
+    stn = lax.axis_index("stn")
+    chip = stn // 2
+    core = stn % 2
+    inputs = result.shape[2]
+    lane = lax.broadcasted_iota(jnp.int32, near[0].shape[1:], 1)
+    first = (lane // (LANES // 2)) == core
+    right = []
+    for near_ref, far_ref in zip(near, far):
+        x = near_ref[place]
+        y = far_ref[place]
+        if inputs >= LANES:
+            right.append(
+                jnp.concatenate([jnp.where(core == 0, x, y), jnp.where(core == 0, y, x)], 1)
+            )
+        else:
+            right.append(jnp.concatenate([jnp.where(first, x, y), turn(jnp.where(first, y, x))], 0))
+    products = lax.dot_general(
+        lefts[place],
+        jnp.concatenate(right, 1),
+        (((1,), (0,)), ((), ())),
+        preferred_element_type=jnp.float32,
+    )
+    products = jnp.where(slot < total, products * (1.0 / times), 0.0).astype(jnp.bfloat16)
+    for n, distances in enumerate(members):
+        other = chip ^ jnp.where(core == 0, distances[0], distances[1])
+        here = pl.ds(pl.multiple_of(other * 2 * inputs, LANES), 2 * inputs)
+        lanes = slice(n * 2 * inputs, (n + 1) * 2 * inputs)
+        result[slot, 0, :, here] = products[:inputs, lanes]
+        result[slot, 1, :, here] = products[inputs:, lanes]
+
+
+def first_kernel(members, order, slot_cap, times, owner_ref, *rest):
+    near = rest[: len(members)]
+    far = rest[len(members) : 2 * len(members)]
+    lefts, places, result = rest[2 * len(members) :]
+    held_ref = near[0]
+    inputs = result.shape[2]
     bands, keep = owner_ref.shape
     band = lax.axis_index("chan")
     core = lax.axis_index("stn") % 2
@@ -151,13 +188,14 @@
         mine = held_ref[place]
         turned = jnp.concatenate([mine[lines:], -mine[:lines]], 0)
         if inputs >= LANES:
-            lefts[place] = jnp.concatenate([mine, turned], 1)
+            left = jnp.concatenate([mine, turned], 1)
         else:
             ahead = jnp.where(low, mine, turn(turned))
             behind = jnp.where(low, turn(mine), turned)
-            lefts[place] = jnp.concatenate(
+            left = jnp.concatenate(
                 [jnp.where(core == 0, ahead, behind), jnp.where(core == 0, behind, ahead)], 0
             )
+        lefts[place] = left.T
 
     bits = jnp.where(
         owner_ref[...] == band,
@@ -179,52 +217,19 @@
             total += mine
             place += mine
     places[RCAP + 1] = total
-
-
-def back_kernel(sequences, times, places, *rest):
-    chips = len(sequences)
-    near = rest[:chips]
-    far = [rest[chips + sequences.index((m, n))] for n, m in sequences]
-    lefts, out_ref, result, sems = rest[2 * chips :]
-    inputs = out_ref.shape[2]
-    stn = lax.axis_index("stn")
-    chip = stn // 2
-    core = stn % 2
-    pack = max(1, LANES // inputs)
-    lines = times // pack
-
-    lane = lax.broadcasted_iota(jnp.int32, (2 * lines, LANES), 1)
-    first = (lane // (LANES // 2)) == core
-
+    for slot in range(RCAP):
+        fill(result, slot, places[slot], total, times, members, near, far, lefts)
+
+
+def back_kernel(members, times, places, *rest):
+    near = rest[: len(members)]
+    far = [rest[len(members) + members.index((m, n))] for n, m in members]
+    lefts = rest[2 * len(members)]
+    out_ref, result, sems = rest[-3:]
     total = places[RCAP + 1]
     copies = []
     for slot in range(RCAP):
-        place = places[slot]
-        right = []
-        for near_ref, far_ref in zip(near, far):
-            x = near_ref[place]
-            y = far_ref[place]
-            if pack == 1:
-                right.append(
-                    jnp.concatenate([jnp.where(core == 0, x, y), jnp.where(core == 0, y, x)], 1)
-                )
-            else:
-                right.append(
-                    jnp.concatenate([jnp.where(first, x, y), turn(jnp.where(first, y, x))], 0)
-                )
-        products = lax.dot_general(
-            lefts[place],
-            jnp.concatenate(right, 1),
-            (((0,), (0,)), ((), ())),
-            preferred_element_type=jnp.float32,
-        )
-        products = jnp.where(slot < total, products * (1.0 / times), 0.0).astype(jnp.bfloat16)
-        for n, distances in enumerate(sequences):
-            other = chip ^ jnp.where(core == 0, distances[0], distances[1])
-            here = pl.ds(pl.multiple_of(other * 2 * inputs, LANES), 2 * inputs)
-            lanes = slice(n * 2 * inputs, (n + 1) * 2 * inputs)
-            result[slot, 0, :, here] = products[:inputs, lanes]
-            result[slot, 1, :, here] = products[inputs:, lanes]
+        fill(result, slot, places[slot], total, times, members, near, far, lefts)
         copy = pltpu.make_async_copy(result.at[slot], out_ref.at[slot], sems.at[slot])
         copy.start()
         copies.append(copy)
@@ -287,27 +292,27 @@
     slots = held.shape[0]
     near = gathered(held)
     far = [swapped(x, "stn", 1) for x in near]
-    lefts, places = pl.pallas_call(
-        functools.partial(left_kernel, inputs, order, slot_cap),
+    ahead, behind = [0, chips[-1]], chips[1:-1]
+    lefts, places, result = pl.pallas_call(
+        functools.partial(first_kernel, [sequences[n] for n in ahead], order, slot_cap, times),
         out_shape=[
-            pltpu.VMEM((slots, 2 * lines * pack, 2 * inputs), jnp.bfloat16),
+            pltpu.VMEM((slots, 2 * inputs, 2 * lines * pack), jnp.bfloat16),
             pltpu.SMEM((RCAP + 2,), jnp.int32),
+            pltpu.VMEM(out_shape, jnp.bfloat16),
         ],
-        in_specs=[vmem] * 2,
-        out_specs=[vmem, smem],
+        in_specs=[vmem] * (1 + 2 * len(ahead)),
+        out_specs=[vmem, smem, vmem],
         compiler_params=pltpu.CompilerParams(vmem_limit_bytes=BACK_VMEM),
-    )(owner, held)
-    visibilities = pl.pallas_call(
-        functools.partial(back_kernel, sequences, times),
-        out_shape=jax.ShapeDtypeStruct(out_shape, jnp.bfloat16),
-        in_specs=[smem] + [vmem] * (1 + 2 * len(chips)),
-        out_specs=anywhere,
-        scratch_shapes=[
-            pltpu.VMEM(out_shape, jnp.bfloat16),
-            pltpu.SemaphoreType.DMA((RCAP,)),
-        ],
+    )(owner, *[near[n] for n in ahead], *[far[n] for n in ahead])
+    visibilities, _ = pl.pallas_call(
+        functools.partial(back_kernel, [sequences[n] for n in behind], times),
+        out_shape=[jax.ShapeDtypeStruct(out_shape, jnp.bfloat16), pltpu.VMEM(out_shape, jnp.bfloat16)],
+        in_specs=[smem] + [vmem] * (2 + 2 * len(behind)),
+        out_specs=[anywhere, vmem],
+        input_output_aliases={2 + 2 * len(behind): 1},
+        scratch_shapes=[pltpu.SemaphoreType.DMA((RCAP,))],
         compiler_params=pltpu.CompilerParams(vmem_limit_bytes=BACK_VMEM),
-    )(places, *near, *far, lefts)
+    )(places, *[near[n] for n in behind], *[far[n] for n in behind], lefts, result)
     return visibilities[None]
 
 

time: 28 us -> 27.9 us (level)
  waiting for transfers between devices: 12.2 us -> 11.3 us
  Pallas kernels: 5.92 us -> 6.69 us
    ppermute x7, waiting for transfers between devices: 5.35 us -> 4.44 us  [swapped(): return lax.ppermute(x, axis, [(i, i ^ mask) for i in range(peers)])]
    pallas_call x2, Pallas kernels: 2.47 us -> 3.24 us  [the longest x1 2.11 us: per_device(): pl.pallas_call(functools.partial(back_kernel, [sequences[n] for n in behi...]
  transfers between devices with their start and end apart: 10 -> 10, of which waited for: 7 -> 6; matrix products, arithmetic and copies ran while one was open for 0% -> 0% of each run, Pallas kernels for 1% -> 4%
where the time goes in v6:
time: 27.9 us; the launch traced here: 27.7 us
  waiting for transfers between devices  11.3 us (41%)
  starting transfers between devices  9.69 us (35%)
  Pallas kernels  6.69 us (24%)
    ppermute x3, waiting for transfers between devices, exchanged(): return lax.ppermute(block, 'stn', pairs)  6.82 us
    ppermute x7, starting transfers between devices, swapped(): return lax.ppermute(x, axis, [(i, i ^ mask) for i in range(peers)])  6.13 us
    ppermute x7, waiting for transfers between devices, swapped(): return lax.ppermute(x, axis, [(i, i ^ mask) for i in range(peers)])  4.44 us
    ppermute x3, starting transfers between devices, exchanged(): return lax.ppermute(block, 'stn', pairs)  3.55 us
    pallas_call x1, Pallas kernels, per_device(): pl.pallas_call(functools.partial(front_kernel, chan_count), out_shape=plt...  3.45 us
    pallas_call x1, Pallas kernels, per_device(): pl.pallas_call(functools.partial(back_kernel, [sequences[n] for n in behi...  2.11 us
    pallas_call x1, Pallas kernels, per_device(): pl.pallas_call(functools.partial(first_kernel, [sequences[n] for n in ahe...  1.13 us
  transfers between devices with their start and end apart: 10, of which 6 were waited for; matrix products, arithmetic and copies ran while one was open for 0% of the time, Pallas kernels for 4%

profile of v6, /device:TPU:0, one launch (start us, length us, event | category | flops | bytes accessed | tf_op | source)
XLA Modules:
  0.0 27.7 jit_solution(5627150295350275109)
XLA Ops:
  0.0 0.0 copy-start
  0.0 3.5 %shard_map.46 = bf16[4,6,32,128]{3,2,1,0:T(8,128)(2,1)S(1)} custom-call(s32[4,8]{1,0:T(4,128)} %survive_any.1, s32[4,8]{1,0:T(4,128)} %owner_ref.1, f32[16,384]{1,0:T(8,128)} %taps_any.1, bf16[1,2,64,18048]{3,2,1,0:T(8,128)(2,1)} %volts_ref.1), custom_call_target="tpu_custom_call" | custom-call | tf_op jit(solution)/shard_map/pallas_call | solution.py:256
  3.5 4.1 %collective-permute-start.2 = (bf16[6,32,128]{2,1,0:T(8,128)(2,1)S(1)}, bf16[6,32,128]{2,1,0:T(8,128)(2,1)S(1)}, u32[]{:S(2)}, u32[]{:S(2)}) collective-permute-start(bf16[6,32,128]{2,1,0:T(8,128)(2,1)S(1)} %get-tuple-element.14), channel_id=1, source_target_pairs={{0,2},{1,3},{2,0},{3,1},{4,6},{5,7},{6,4},{7,5},{8,10},{9,11},{10,... | collective-permute-start | bytes 147464 | tf_op jit(solution)/shard_map/ppermute | solution.py:21
  7.6 1.3 %collective-permute-start.1 = (bf16[6,32,128]{2,1,0:T(8,128)(2,1)S(1)}, bf16[6,32,128]{2,1,0:T(8,128)(2,1)S(1)}, u32[]{:S(2)}, u32[]{:S(2)}) collective-permute-start(bf16[6,32,128]{2,1,0:T(8,128)(2,1)S(1)} %get-tuple-element.15), channel_id=1, source_target_pairs={{0,3},{1,2},{2,1},{3,0},{4,7},{5,6},{6,5},{7,4},{8,11},{9,10},{10,... | collective-permute-start | bytes 147464 | tf_op jit(solution)/shard_map/ppermute | solution.py:21
  8.9 0.2 collective-permute-start
  9.2 1.0 %collective-permute-done.2 = bf16[6,32,128]{2,1,0:T(8,128)(2,1)S(1)} collective-permute-done((bf16[6,32,128]{2,1,0:T(8,128)(2,1)S(1)}, bf16[6,32,128]{2,1,0:T(8,128)(2,1)S(1)}, u32[]{:S(2)}, u32[]{:S(2)}) %collective-permute-start.2) | collective-permute-done | bytes 49184 | tf_op jit(solution)/shard_map/ppermute | solution.py:21
  10.2 3.4 %collective-permute-done.1 = bf16[6,32,128]{2,1,0:T(8,128)(2,1)S(1)} collective-permute-done((bf16[6,32,128]{2,1,0:T(8,128)(2,1)S(1)}, bf16[6,32,128]{2,1,0:T(8,128)(2,1)S(1)}, u32[]{:S(2)}, u32[]{:S(2)}) %collective-permute-start.1) | collective-permute-done | bytes 49184 | tf_op jit(solution)/shard_map/ppermute | solution.py:21
  13.6 0.0 collective-permute-done
  13.6 2.5 %collective-permute-start.3 = (bf16[24,32,128]{2,1,0:T(8,128)(2,1)S(1)}, bf16[24,32,128]{2,1,0:T(8,128)(2,1)S(1)}, u32[]{:S(2)}, u32[]{:S(2)}) collective-permute-start(bf16[24,32,128]{2,1,0:T(8,128)(2,1)S(1)} %pad_maximum_fusion.rest_0_), channel_id=1, source_target_pairs={{0,24},{4,28},{8,16},{12,20},{16,8},{20,12},{24,0},{28,4},{1,25},{... | collective-permute-start | bytes 589832 | tf_op jit(solution)/shard_map/ppermute | solution.py:286
  16.1 0.5 %collective-permute-start.7 = (bf16[24,32,128]{2,1,0:T(8,128)(2,1)S(1)}, bf16[24,32,128]{2,1,0:T(8,128)(2,1)S(1)}, u32[]{:S(2)}, u32[]{:S(2)}) collective-permute-start(bf16[24,32,128]{2,1,0:T(8,128)(2,1)S(1)} %pad_maximum_fusion.rest_0_), channel_id=1, source_target_pairs={{0,16},{4,12},{8,24},{12,4},{16,0},{20,28},{24,8},{28,20},{1,17},{... | collective-permute-start | bytes 589832 | tf_op jit(solution)/shard_map/ppermute | solution.py:286
  16.6 0.5 %collective-permute-start.6 = (bf16[24,32,128]{2,1,0:T(8,128)(2,1)S(1)}, bf16[24,32,128]{2,1,0:T(8,128)(2,1)S(1)}, u32[]{:S(2)}, u32[]{:S(2)}) collective-permute-start(bf16[24,32,128]{2,1,0:T(8,128)(2,1)S(1)} %pad_maximum_fusion.rest_0_), channel_id=1, source_target_pairs={{0,8},{4,20},{8,0},{12,28},{16,24},{20,4},{24,16},{28,12},{1,9},{5... | collective-permute-start | bytes 589832 | tf_op jit(solution)/shard_map/ppermute | solution.py:286
  17.1 0.0 collective-permute-start.4
  17.1 4.8 %collective-permute-done.3.rest_1_ = bf16[24,32,128]{2,1,0:T(8,128)(2,1)S(1)} collective-permute-done((bf16[24,32,128]{2,1,0:T(8,128)(2,1)S(1)}, bf16[24,32,128]{2,1,0:T(8,128)(2,1)S(1)}, u32[]{:S(2)}, u32[]{:S(2)}) %collective-permute-start.3) | collective-permute-done | bytes 196640 | tf_op jit(solution)/shard_map/ppermute | solution.py:286
  21.9 0.0 collective-permute-start.5
  21.9 2.0 %collective-permute-done.7.rest_1_ = bf16[24,32,128]{2,1,0:T(8,128)(2,1)S(1)} collective-permute-done((bf16[24,32,128]{2,1,0:T(8,128)(2,1)S(1)}, bf16[24,32,128]{2,1,0:T(8,128)(2,1)S(1)}, u32[]{:S(2)}, u32[]{:S(2)}) %collective-permute-start.7) | collective-permute-done | bytes 196640 | tf_op jit(solution)/shard_map/ppermute | solution.py:286
  23.9 0.0 collective-permute-start.9
  23.9 0.1 collective-permute-done.6.rest_0_
  24.0 0.4 %collective-permute-start.8 = (bf16[24,32,128]{2,1,0:T(8,128)(2,1)S(1)}, bf16[24,32,128]{2,1,0:T(8,128)(2,1)S(1)}, u32[]{:S(2)}, u32[]{:S(2)}) collective-permute-start(bf16[24,32,128]{2,1,0:T(8,128)(2,1)S(1)} %collective-permute-done.6.rest_0_), channel_id=1, source_target_pairs={{0,4},{4,0},{8,12},{12,8},{16,20},{20,16},{24,28},{28,24},{1,5},{5... | collective-permute-start | bytes 589832 | tf_op jit(solution)/shard_map/ppermute | solution.py:21
  24.4 0.0 collective-permute-done.4.rest_2_
  24.4 0.0 collective-permute-done.5.rest_3_
  24.4 0.0 copy-done
  24.4 1.1 %shard_map.47 = (bf16[24,128,64]{2,1,0:T(8,128)(2,1)S(1)}, s32[26]{0:T(128)S(4)}, bf16[24,2,64,512]{3,2,1,0:T(8,128)(2,1)S(1)}) custom-call(s32[4,8]{1,0:T(4,128)S(1)} %copy-done, bf16[24,32,128]{2,1,0:T(8,128)(2,1)S(1)} %pad_maximum_fusion.rest_0_, bf16[24,32,128]{2,1,0:T(8,128)(2,1)S(1)} %collective-permute-done.3.rest_1_, ...), custom_call_target="tpu_custom_call" | custom-call | tf_op jit(solution)/shard_map/pallas_call | solution.py:296
  25.6 0.0 collective-permute-done.9.rest_3_
  25.6 0.1 collective-permute-done.8.rest_2_
  25.6 2.1 %shard_map.48 = (bf16[24,2,64,512]{3,2,1,0:T(8,128)(2,1)}, bf16[24,2,64,512]{3,2,1,0:T(8,128)(2,1)S(1)}) custom-call(s32[26]{0:T(128)S(4)} %get-tuple-element.9.places, bf16[24,32,128]{2,1,0:T(8,128)(2,1)S(1)} %collective-permute-done.6.rest_0_, bf16[24,32,128]{2,1,0:T(8,128)(2,1)S(1)} %collective-permute-done.7.rest_1_, ...), custom_call_target="tpu_custom_call", output_to_operand_aliasing={{1}: (6, {})} | custom-call | tf_op jit(solution)/shard_map/pallas_call | solution.py:307
  (2 shorter events, 0.0 us)
Async XLA Ops:
  0.0 24.4 %copy-start = (s32[4,8]{1,0:T(4,128)S(1)}, s32[4,8]{1,0:T(4,128)}, u32[]{:S(2)}) copy-start(s32[4,8]{1,0:T(4,128)} %owner_ref.1) | copy-start | bytes 388
  3.5 6.7 %collective-permute-start.2 = (bf16[6,32,128]{2,1,0:T(8,128)(2,1)S(1)}, bf16[6,32,128]{2,1,0:T(8,128)(2,1)S(1)}, u32[]{:S(2)}, u32[]{:S(2)}) collective-permute-start(bf16[6,32,128]{2,1,0:T(8,128)(2,1)S(1)} %get-tuple-element.14), channel_id=1, source_target_pairs={{0,2},{1,3},{2,0},{3,1},{4,6},{5,7},{6,4},{7,5},{8,10},{9,11},{10,... | collective-permute-start | bytes 147464 | tf_op jit(solution)/shard_map/ppermute | solution.py:21
  7.6 6.0 %collective-permute-start.1 = (bf16[6,32,128]{2,1,0:T(8,128)(2,1)S(1)}, bf16[6,32,128]{2,1,0:T(8,128)(2,1)S(1)}, u32[]{:S(2)}, u32[]{:S(2)}) collective-permute-start(bf16[6,32,128]{2,1,0:T(8,128)(2,1)S(1)} %get-tuple-element.15), channel_id=1, source_target_pairs={{0,3},{1,2},{2,1},{3,0},{4,7},{5,6},{6,5},{7,4},{8,11},{9,10},{10,... | collective-permute-start | bytes 147464 | tf_op jit(solution)/shard_map/ppermute | solution.py:21
  8.9 4.6 %collective-permute-start = (bf16[6,32,128]{2,1,0:T(8,128)(2,1)S(1)}, bf16[6,32,128]{2,1,0:T(8,128)(2,1)S(1)}, u32[]{:S(2)}, u32[]{:S(2)}) collective-permute-start(bf16[6,32,128]{2,1,0:T(8,128)(2,1)S(1)} %get-tuple-element.16), channel_id=1, source_target_pairs={{0,1},{1,0},{2,3},{3,2},{4,5},{5,4},{6,7},{7,6},{8,9},{9,8},{10,11... | collective-permute-start | bytes 147464 | tf_op jit(solution)/shard_map/ppermute | solution.py:21
  13.6 8.3 %collective-permute-start.3 = (bf16[24,32,128]{2,1,0:T(8,128)(2,1)S(1)}, bf16[24,32,128]{2,1,0:T(8,128)(2,1)S(1)}, u32[]{:S(2)}, u32[]{:S(2)}) collective-permute-start(bf16[24,32,128]{2,1,0:T(8,128)(2,1)S(1)} %pad_maximum_fusion.rest_0_), channel_id=1, source_target_pairs={{0,24},{4,28},{8,16},{12,20},{16,8},{20,12},{24,0},{28,4},{1,25},{... | collective-permute-start | bytes 589832 | tf_op jit(solution)/shard_map/ppermute | solution.py:286
  16.1 7.8 %collective-permute-start.7 = (bf16[24,32,128]{2,1,0:T(8,128)(2,1)S(1)}, bf16[24,32,128]{2,1,0:T(8,128)(2,1)S(1)}, u32[]{:S(2)}, u32[]{:S(2)}) collective-permute-start(bf16[24,32,128]{2,1,0:T(8,128)(2,1)S(1)} %pad_maximum_fusion.rest_0_), channel_id=1, source_target_pairs={{0,16},{4,12},{8,24},{12,4},{16,0},{20,28},{24,8},{28,20},{1,17},{... | collective-permute-start | bytes 589832 | tf_op jit(solution)/shard_map/ppermute | solution.py:286
  16.6 7.4 %collective-permute-start.6 = (bf16[24,32,128]{2,1,0:T(8,128)(2,1)S(1)}, bf16[24,32,128]{2,1,0:T(8,128)(2,1)S(1)}, u32[]{:S(2)}, u32[]{:S(2)}) collective-permute-start(bf16[24,32,128]{2,1,0:T(8,128)(2,1)S(1)} %pad_maximum_fusion.rest_0_), channel_id=1, source_target_pairs={{0,8},{4,20},{8,0},{12,28},{16,24},{20,4},{24,16},{28,12},{1,9},{5... | collective-permute-start | bytes 589832 | tf_op jit(solution)/shard_map/ppermute | solution.py:286
  17.1 7.3 %collective-permute-start.4 = (bf16[24,32,128]{2,1,0:T(8,128)(2,1)S(1)}, bf16[24,32,128]{2,1,0:T(8,128)(2,1)S(1)}, u32[]{:S(2)}, u32[]{:S(2)}) collective-permute-start(bf16[24,32,128]{2,1,0:T(8,128)(2,1)S(1)} %pad_maximum_fusion.rest_0_), channel_id=1, source_target_pairs={{0,4},{4,0},{8,12},{12,8},{16,20},{20,16},{24,28},{28,24},{1,5},{5... | collective-permute-start | bytes 589832 | tf_op jit(solution)/shard_map/ppermute | solution.py:21
  21.9 2.5 %collective-permute-start.5 = (bf16[24,32,128]{2,1,0:T(8,128)(2,1)S(1)}, bf16[24,32,128]{2,1,0:T(8,128)(2,1)S(1)}, u32[]{:S(2)}, u32[]{:S(2)}) collective-permute-start(bf16[24,32,128]{2,1,0:T(8,128)(2,1)S(1)} %collective-permute-done.3.rest_1_), channel_id=1, source_target_pairs={{0,4},{4,0},{8,12},{12,8},{16,20},{20,16},{24,28},{28,24},{1,5},{5... | collective-permute-start | bytes 589832 | tf_op jit(solution)/shard_map/ppermute | solution.py:21
  23.9 1.7 %collective-permute-start.9 = (bf16[24,32,128]{2,1,0:T(8,128)(2,1)S(1)}, bf16[24,32,128]{2,1,0:T(8,128)(2,1)S(1)}, u32[]{:S(2)}, u32[]{:S(2)}) collective-permute-start(bf16[24,32,128]{2,1,0:T(8,128)(2,1)S(1)} %collective-permute-done.7.rest_1_), channel_id=1, source_target_pairs={{0,4},{4,0},{8,12},{12,8},{16,20},{20,16},{24,28},{28,24},{1,5},{5... | collective-permute-start | bytes 589832 | tf_op jit(solution)/shard_map/ppermute | solution.py:21
  24.0 1.6 %collective-permute-start.8 = (bf16[24,32,128]{2,1,0:T(8,128)(2,1)S(1)}, bf16[24,32,128]{2,1,0:T(8,128)(2,1)S(1)}, u32[]{:S(2)}, u32[]{:S(2)}) collective-permute-start(bf16[24,32,128]{2,1,0:T(8,128)(2,1)S(1)} %collective-permute-done.6.rest_0_), channel_id=1, source_target_pairs={{0,4},{4,0},{8,12},{12,8},{16,20},{20,16},{24,28},{28,24},{1,5},{5... | collective-permute-start | bytes 589832 | tf_op jit(solution)/shard_map/ppermute | solution.py:21

commit v7 on v6

--- a/solution.py
+++ b/solution.py
@@ -132,9 +132,8 @@
         for earlier in range(c):
             rank += (owner_ref[band, earlier] == owner).astype(jnp.int32)
         piece = owner ^ band
-        for part in range(2):
-            line = spectra[pl.ds(part * keep + c, lines, stride=2 * keep), :]
-            pieces[piece, rank, part * lines : (part + 1) * lines, :] = line.astype(jnp.bfloat16)
+        both = [spectra[pl.ds(part * keep + c, lines, stride=2 * keep), :] for part in range(2)]
+        pieces[piece, rank] = jnp.concatenate(both, 0).astype(jnp.bfloat16)
 
 
 def turn(x):

time: 27.9 us -> 27.9 us (level)
  no operation moved by 1% of the time
where the time goes in v7:
time: 27.9 us; the launch traced here: 27.7 us
  waiting for transfers between devices  11.3 us (41%)
  starting transfers between devices  9.69 us (35%)
  Pallas kernels  6.69 us (24%)
    ppermute x3, waiting for transfers between devices, exchanged(): return lax.ppermute(block, 'stn', pairs)  6.82 us
    ppermute x7, starting transfers between devices, swapped(): return lax.ppermute(x, axis, [(i, i ^ mask) for i in range(peers)])  6.13 us
    ppermute x7, waiting for transfers between devices, swapped(): return lax.ppermute(x, axis, [(i, i ^ mask) for i in range(peers)])  4.44 us
    ppermute x3, starting transfers between devices, exchanged(): return lax.ppermute(block, 'stn', pairs)  3.55 us
    pallas_call x1, Pallas kernels, per_device(): pl.pallas_call(functools.partial(front_kernel, chan_count), out_shape=plt...  3.45 us
    pallas_call x1, Pallas kernels, per_device(): pl.pallas_call(functools.partial(back_kernel, [sequences[n] for n in behi...  2.11 us
    pallas_call x1, Pallas kernels, per_device(): pl.pallas_call(functools.partial(first_kernel, [sequences[n] for n in ahe...  1.13 us
  transfers between devices with their start and end apart: 10, of which 6 were waited for; matrix products, arithmetic and copies ran while one was open for 0% of the time, Pallas kernels for 4%

profile of v7, /device:TPU:0, one launch (start us, length us, event | category | flops | bytes accessed | tf_op | source)
XLA Modules:
  0.0 27.7 jit_solution(5627150295350275109)
XLA Ops:
  0.0 0.0 copy-start
  0.0 3.5 %shard_map.46 = bf16[4,6,32,128]{3,2,1,0:T(8,128)(2,1)S(1)} custom-call(s32[4,8]{1,0:T(4,128)} %survive_any.1, s32[4,8]{1,0:T(4,128)} %owner_ref.1, f32[16,384]{1,0:T(8,128)} %taps_any.1, bf16[1,2,64,18048]{3,2,1,0:T(8,128)(2,1)} %volts_ref.1), custom_call_target="tpu_custom_call" | custom-call | tf_op jit(solution)/shard_map/pallas_call | solution.py:255
  3.5 4.1 %collective-permute-start.2 = (bf16[6,32,128]{2,1,0:T(8,128)(2,1)S(1)}, bf16[6,32,128]{2,1,0:T(8,128)(2,1)S(1)}, u32[]{:S(2)}, u32[]{:S(2)}) collective-permute-start(bf16[6,32,128]{2,1,0:T(8,128)(2,1)S(1)} %get-tuple-element.14), channel_id=1, source_target_pairs={{0,2},{1,3},{2,0},{3,1},{4,6},{5,7},{6,4},{7,5},{8,10},{9,11},{10,... | collective-permute-start | bytes 147464 | tf_op jit(solution)/shard_map/ppermute | solution.py:21
  7.6 1.3 %collective-permute-start.1 = (bf16[6,32,128]{2,1,0:T(8,128)(2,1)S(1)}, bf16[6,32,128]{2,1,0:T(8,128)(2,1)S(1)}, u32[]{:S(2)}, u32[]{:S(2)}) collective-permute-start(bf16[6,32,128]{2,1,0:T(8,128)(2,1)S(1)} %get-tuple-element.15), channel_id=1, source_target_pairs={{0,3},{1,2},{2,1},{3,0},{4,7},{5,6},{6,5},{7,4},{8,11},{9,10},{10,... | collective-permute-start | bytes 147464 | tf_op jit(solution)/shard_map/ppermute | solution.py:21
  8.9 0.2 collective-permute-start
  9.2 1.0 %collective-permute-done.2 = bf16[6,32,128]{2,1,0:T(8,128)(2,1)S(1)} collective-permute-done((bf16[6,32,128]{2,1,0:T(8,128)(2,1)S(1)}, bf16[6,32,128]{2,1,0:T(8,128)(2,1)S(1)}, u32[]{:S(2)}, u32[]{:S(2)}) %collective-permute-start.2) | collective-permute-done | bytes 49184 | tf_op jit(solution)/shard_map/ppermute | solution.py:21
  10.2 3.4 %collective-permute-done.1 = bf16[6,32,128]{2,1,0:T(8,128)(2,1)S(1)} collective-permute-done((bf16[6,32,128]{2,1,0:T(8,128)(2,1)S(1)}, bf16[6,32,128]{2,1,0:T(8,128)(2,1)S(1)}, u32[]{:S(2)}, u32[]{:S(2)}) %collective-permute-start.1) | collective-permute-done | bytes 49184 | tf_op jit(solution)/shard_map/ppermute | solution.py:21
  13.6 0.0 collective-permute-done
  13.6 2.5 %collective-permute-start.3 = (bf16[24,32,128]{2,1,0:T(8,128)(2,1)S(1)}, bf16[24,32,128]{2,1,0:T(8,128)(2,1)S(1)}, u32[]{:S(2)}, u32[]{:S(2)}) collective-permute-start(bf16[24,32,128]{2,1,0:T(8,128)(2,1)S(1)} %pad_maximum_fusion.rest_0_), channel_id=1, source_target_pairs={{0,24},{4,28},{8,16},{12,20},{16,8},{20,12},{24,0},{28,4},{1,25},{... | collective-permute-start | bytes 589832 | tf_op jit(solution)/shard_map/ppermute | solution.py:285
  16.1 0.5 %collective-permute-start.7 = (bf16[24,32,128]{2,1,0:T(8,128)(2,1)S(1)}, bf16[24,32,128]{2,1,0:T(8,128)(2,1)S(1)}, u32[]{:S(2)}, u32[]{:S(2)}) collective-permute-start(bf16[24,32,128]{2,1,0:T(8,128)(2,1)S(1)} %pad_maximum_fusion.rest_0_), channel_id=1, source_target_pairs={{0,16},{4,12},{8,24},{12,4},{16,0},{20,28},{24,8},{28,20},{1,17},{... | collective-permute-start | bytes 589832 | tf_op jit(solution)/shard_map/ppermute | solution.py:285
  16.6 0.5 %collective-permute-start.6 = (bf16[24,32,128]{2,1,0:T(8,128)(2,1)S(1)}, bf16[24,32,128]{2,1,0:T(8,128)(2,1)S(1)}, u32[]{:S(2)}, u32[]{:S(2)}) collective-permute-start(bf16[24,32,128]{2,1,0:T(8,128)(2,1)S(1)} %pad_maximum_fusion.rest_0_), channel_id=1, source_target_pairs={{0,8},{4,20},{8,0},{12,28},{16,24},{20,4},{24,16},{28,12},{1,9},{5... | collective-permute-start | bytes 589832 | tf_op jit(solution)/shard_map/ppermute | solution.py:285
  17.1 0.0 collective-permute-start.4
  17.1 4.8 %collective-permute-done.3.rest_1_ = bf16[24,32,128]{2,1,0:T(8,128)(2,1)S(1)} collective-permute-done((bf16[24,32,128]{2,1,0:T(8,128)(2,1)S(1)}, bf16[24,32,128]{2,1,0:T(8,128)(2,1)S(1)}, u32[]{:S(2)}, u32[]{:S(2)}) %collective-permute-start.3) | collective-permute-done | bytes 196640 | tf_op jit(solution)/shard_map/ppermute | solution.py:285
  21.9 0.0 collective-permute-start.5
  21.9 2.0 %collective-permute-done.7.rest_1_ = bf16[24,32,128]{2,1,0:T(8,128)(2,1)S(1)} collective-permute-done((bf16[24,32,128]{2,1,0:T(8,128)(2,1)S(1)}, bf16[24,32,128]{2,1,0:T(8,128)(2,1)S(1)}, u32[]{:S(2)}, u32[]{:S(2)}) %collective-permute-start.7) | collective-permute-done | bytes 196640 | tf_op jit(solution)/shard_map/ppermute | solution.py:285
  23.9 0.0 collective-permute-start.9
  23.9 0.1 collective-permute-done.6.rest_0_
  24.0 0.4 %collective-permute-start.8 = (bf16[24,32,128]{2,1,0:T(8,128)(2,1)S(1)}, bf16[24,32,128]{2,1,0:T(8,128)(2,1)S(1)}, u32[]{:S(2)}, u32[]{:S(2)}) collective-permute-start(bf16[24,32,128]{2,1,0:T(8,128)(2,1)S(1)} %collective-permute-done.6.rest_0_), channel_id=1, source_target_pairs={{0,4},{4,0},{8,12},{12,8},{16,20},{20,16},{24,28},{28,24},{1,5},{5... | collective-permute-start | bytes 589832 | tf_op jit(solution)/shard_map/ppermute | solution.py:21
  24.4 0.0 collective-permute-done.4.rest_2_
  24.4 0.0 collective-permute-done.5.rest_3_
  24.4 0.0 copy-done
  24.4 1.1 %shard_map.47 = (bf16[24,128,64]{2,1,0:T(8,128)(2,1)S(1)}, s32[26]{0:T(128)S(4)}, bf16[24,2,64,512]{3,2,1,0:T(8,128)(2,1)S(1)}) custom-call(s32[4,8]{1,0:T(4,128)S(1)} %copy-done, bf16[24,32,128]{2,1,0:T(8,128)(2,1)S(1)} %pad_maximum_fusion.rest_0_, bf16[24,32,128]{2,1,0:T(8,128)(2,1)S(1)} %collective-permute-done.3.rest_1_, ...), custom_call_target="tpu_custom_call" | custom-call | tf_op jit(solution)/shard_map/pallas_call | solution.py:295
  25.6 0.0 collective-permute-done.9.rest_3_
  25.6 0.1 collective-permute-done.8.rest_2_
  25.6 2.1 %shard_map.48 = (bf16[24,2,64,512]{3,2,1,0:T(8,128)(2,1)}, bf16[24,2,64,512]{3,2,1,0:T(8,128)(2,1)S(1)}) custom-call(s32[26]{0:T(128)S(4)} %get-tuple-element.9.places, bf16[24,32,128]{2,1,0:T(8,128)(2,1)S(1)} %collective-permute-done.6.rest_0_, bf16[24,32,128]{2,1,0:T(8,128)(2,1)S(1)} %collective-permute-done.7.rest_1_, ...), custom_call_target="tpu_custom_call", output_to_operand_aliasing={{1}: (6, {})} | custom-call | tf_op jit(solution)/shard_map/pallas_call | solution.py:306
  (2 shorter events, 0.0 us)
Async XLA Ops:
  0.0 24.4 %copy-start = (s32[4,8]{1,0:T(4,128)S(1)}, s32[4,8]{1,0:T(4,128)}, u32[]{:S(2)}) copy-start(s32[4,8]{1,0:T(4,128)} %owner_ref.1) | copy-start | bytes 388
  3.5 6.7 %collective-permute-start.2 = (bf16[6,32,128]{2,1,0:T(8,128)(2,1)S(1)}, bf16[6,32,128]{2,1,0:T(8,128)(2,1)S(1)}, u32[]{:S(2)}, u32[]{:S(2)}) collective-permute-start(bf16[6,32,128]{2,1,0:T(8,128)(2,1)S(1)} %get-tuple-element.14), channel_id=1, source_target_pairs={{0,2},{1,3},{2,0},{3,1},{4,6},{5,7},{6,4},{7,5},{8,10},{9,11},{10,... | collective-permute-start | bytes 147464 | tf_op jit(solution)/shard_map/ppermute | solution.py:21
  7.6 6.0 %collective-permute-start.1 = (bf16[6,32,128]{2,1,0:T(8,128)(2,1)S(1)}, bf16[6,32,128]{2,1,0:T(8,128)(2,1)S(1)}, u32[]{:S(2)}, u32[]{:S(2)}) collective-permute-start(bf16[6,32,128]{2,1,0:T(8,128)(2,1)S(1)} %get-tuple-element.15), channel_id=1, source_target_pairs={{0,3},{1,2},{2,1},{3,0},{4,7},{5,6},{6,5},{7,4},{8,11},{9,10},{10,... | collective-permute-start | bytes 147464 | tf_op jit(solution)/shard_map/ppermute | solution.py:21
  8.9 4.6 %collective-permute-start = (bf16[6,32,128]{2,1,0:T(8,128)(2,1)S(1)}, bf16[6,32,128]{2,1,0:T(8,128)(2,1)S(1)}, u32[]{:S(2)}, u32[]{:S(2)}) collective-permute-start(bf16[6,32,128]{2,1,0:T(8,128)(2,1)S(1)} %get-tuple-element.16), channel_id=1, source_target_pairs={{0,1},{1,0},{2,3},{3,2},{4,5},{5,4},{6,7},{7,6},{8,9},{9,8},{10,11... | collective-permute-start | bytes 147464 | tf_op jit(solution)/shard_map/ppermute | solution.py:21
  13.6 8.3 %collective-permute-start.3 = (bf16[24,32,128]{2,1,0:T(8,128)(2,1)S(1)}, bf16[24,32,128]{2,1,0:T(8,128)(2,1)S(1)}, u32[]{:S(2)}, u32[]{:S(2)}) collective-permute-start(bf16[24,32,128]{2,1,0:T(8,128)(2,1)S(1)} %pad_maximum_fusion.rest_0_), channel_id=1, source_target_pairs={{0,24},{4,28},{8,16},{12,20},{16,8},{20,12},{24,0},{28,4},{1,25},{... | collective-permute-start | bytes 589832 | tf_op jit(solution)/shard_map/ppermute | solution.py:285
  16.1 7.8 %collective-permute-start.7 = (bf16[24,32,128]{2,1,0:T(8,128)(2,1)S(1)}, bf16[24,32,128]{2,1,0:T(8,128)(2,1)S(1)}, u32[]{:S(2)}, u32[]{:S(2)}) collective-permute-start(bf16[24,32,128]{2,1,0:T(8,128)(2,1)S(1)} %pad_maximum_fusion.rest_0_), channel_id=1, source_target_pairs={{0,16},{4,12},{8,24},{12,4},{16,0},{20,28},{24,8},{28,20},{1,17},{... | collective-permute-start | bytes 589832 | tf_op jit(solution)/shard_map/ppermute | solution.py:285
  16.6 7.4 %collective-permute-start.6 = (bf16[24,32,128]{2,1,0:T(8,128)(2,1)S(1)}, bf16[24,32,128]{2,1,0:T(8,128)(2,1)S(1)}, u32[]{:S(2)}, u32[]{:S(2)}) collective-permute-start(bf16[24,32,128]{2,1,0:T(8,128)(2,1)S(1)} %pad_maximum_fusion.rest_0_), channel_id=1, source_target_pairs={{0,8},{4,20},{8,0},{12,28},{16,24},{20,4},{24,16},{28,12},{1,9},{5... | collective-permute-start | bytes 589832 | tf_op jit(solution)/shard_map/ppermute | solution.py:285
  17.1 7.3 %collective-permute-start.4 = (bf16[24,32,128]{2,1,0:T(8,128)(2,1)S(1)}, bf16[24,32,128]{2,1,0:T(8,128)(2,1)S(1)}, u32[]{:S(2)}, u32[]{:S(2)}) collective-permute-start(bf16[24,32,128]{2,1,0:T(8,128)(2,1)S(1)} %pad_maximum_fusion.rest_0_), channel_id=1, source_target_pairs={{0,4},{4,0},{8,12},{12,8},{16,20},{20,16},{24,28},{28,24},{1,5},{5... | collective-permute-start | bytes 589832 | tf_op jit(solution)/shard_map/ppermute | solution.py:21
  21.9 2.5 %collective-permute-start.5 = (bf16[24,32,128]{2,1,0:T(8,128)(2,1)S(1)}, bf16[24,32,128]{2,1,0:T(8,128)(2,1)S(1)}, u32[]{:S(2)}, u32[]{:S(2)}) collective-permute-start(bf16[24,32,128]{2,1,0:T(8,128)(2,1)S(1)} %collective-permute-done.3.rest_1_), channel_id=1, source_target_pairs={{0,4},{4,0},{8,12},{12,8},{16,20},{20,16},{24,28},{28,24},{1,5},{5... | collective-permute-start | bytes 589832 | tf_op jit(solution)/shard_map/ppermute | solution.py:21
  23.9 1.7 %collective-permute-start.9 = (bf16[24,32,128]{2,1,0:T(8,128)(2,1)S(1)}, bf16[24,32,128]{2,1,0:T(8,128)(2,1)S(1)}, u32[]{:S(2)}, u32[]{:S(2)}) collective-permute-start(bf16[24,32,128]{2,1,0:T(8,128)(2,1)S(1)} %collective-permute-done.7.rest_1_), channel_id=1, source_target_pairs={{0,4},{4,0},{8,12},{12,8},{16,20},{20,16},{24,28},{28,24},{1,5},{5... | collective-permute-start | bytes 589832 | tf_op jit(solution)/shard_map/ppermute | solution.py:21
  24.0 1.6 %collective-permute-start.8 = (bf16[24,32,128]{2,1,0:T(8,128)(2,1)S(1)}, bf16[24,32,128]{2,1,0:T(8,128)(2,1)S(1)}, u32[]{:S(2)}, u32[]{:S(2)}) collective-permute-start(bf16[24,32,128]{2,1,0:T(8,128)(2,1)S(1)} %collective-permute-done.6.rest_0_), channel_id=1, source_target_pairs={{0,4},{4,0},{8,12},{12,8},{16,20},{20,16},{24,28},{28,24},{1,5},{5... | collective-permute-start | bytes 589832 | tf_op jit(solution)/shard_map/ppermute | solution.py:21
